TPU v7x, 32 devices: a whole 2x2x4 slice. The times are simulated.
32 devices in a mesh: dp: 4 (over x, core), chan: 2 (over y), ctx: 4 (over z).
Axes of the slice: x: 2, y: 2, z: 4, core: 2. Of those that a mesh axis runs over, the one named last changes fastest.
Arguments:
- query_proj: bfloat16 [4, 512, 4096], P('dp', 'ctx', 'chan'), may hold values from -6 to 6
- key_proj: bfloat16 [4, 512, 4096], P('dp', 'ctx', 'chan'), may hold values from -6 to 6
- value_proj: bfloat16 [4, 512, 4096], P('dp', 'ctx', 'chan'), may hold values from -6 to 6
- out_grad: bfloat16 [4, 512, 4096], P('dp', 'ctx', 'chan'), may hold values from -6 to 6
- filter_taps: float32 [4096, 512], P(('chan', 'ctx')), may hold values from -0.25 to 0.25
Outputs:
- grad_q: bfloat16 [4, 512, 4096], P('dp', 'ctx', 'chan')
- grad_k: bfloat16 [4, 512, 4096], P('dp', 'ctx', 'chan')
- grad_v: bfloat16 [4, 512, 4096], P('dp', 'ctx', 'chan')
- grad_filt: float32 [4096, 512], P(('chan', 'ctx'))
All inputs are finite; a program needn't handle non-finite values.
Results may differ from a plain program's by a relative error of at most 0.014.
Values may be sent and summed in bfloat16 or wider, within the bound.
No kernel may reach another device: no remote copies, remote signals or barrier semaphores. Data moves between devices by JAX's collectives and lax.ppermute only.
A program may use at most 64 MiB of HBM per device.

v0:
```python
import functools
import math

import jax
import jax.numpy as jnp
import ml_dtypes
import numpy as np
from jax import lax
from jax.experimental import pallas as pl
from jax.experimental.pallas import tpu as pltpu
from jax.sharding import PartitionSpec as P

bf16 = jnp.bfloat16
f32 = jnp.float32
VMEM_LIMIT = 20 * 1024 * 1024
CONV_VMEM = 20 * 1024 * 1024
GATE_VMEM = 63 * 1024 * 1024
ROW_CHUNKS = 4


def dft_table(size):
    freq = np.arange(size // 2)[:, None]
    pos = np.arange(-size // 2, size // 2)[None, :]
    angle = 2.0 * np.pi * (((2 * freq + 1) * pos) % (2 * size)) / (2 * size)
    return np.concatenate([np.cos(angle), -np.sin(angle)], 0)


def as_const(table):
    return jnp.asarray(np.ascontiguousarray(table).astype(ml_dtypes.bfloat16))


def mm(left, right, dims=((1,), (0,))):
    return lax.dot_general(left, right, (dims, ((), ())), preferred_element_type=f32)


def cmul(left, right):
    half = left.shape[0] // 2
    lr, li, rr, ri = left[:half], left[half:], right[:half], right[half:]
    return lr * rr - li * ri, lr * ri + li * rr


def cmulc(left, right):
    half = left.shape[0] // 2
    lr, li, rr, ri = left[:half], left[half:], right[:half], right[half:]
    return lr * rr + li * ri, lr * ri - li * rr


def join(pair):
    return jnp.concatenate([pair[0], pair[1]], 0)


def lanes(start, width):
    return pl.ds(pl.multiple_of(start, 128), width)


def call(kernel, outs, n_in, smem_first=True, cost=(0, 0), limit=VMEM_LIMIT, in_hbm=0, out_hbm=False, scratch=()):
    vmem, hbm = pl.BlockSpec(memory_space=pltpu.VMEM), pl.BlockSpec(memory_space=pltpu.HBM)
    in_specs = [hbm] * in_hbm + [vmem] * (n_in - in_hbm)
    if smem_first:
        in_specs = [pl.BlockSpec(memory_space=pltpu.SMEM)] + in_specs
    return pl.pallas_call(
        kernel,
        out_shape=[jax.ShapeDtypeStruct(s, d) for s, d in outs],
        in_specs=in_specs,
        out_specs=[hbm if out_hbm else vmem] * len(outs),
        scratch_shapes=scratch,
        compiler_params=pltpu.CompilerParams(vmem_limit_bytes=limit),
        cost_estimate=pl.CostEstimate(flops=cost[0], bytes_accessed=cost[1], transcendentals=0),
    )


def gate_kernel(quarter, idx, q, k, v, g, taps, keep_own, keep_far, own1, far1, to2, to3, piece):
    z, upper = idx[0], idx[2]
    piece[...] = taps[...].astype(bf16)
    for r, dest in ((3, far1), (2, keep_far), (1, own1), (0, keep_own)):
        cols = lanes((z ^ r) * quarter, quarter)
        gated = (q[0, :, cols].astype(f32) * k[0, :, cols].astype(f32)).astype(bf16)
        grad = (g[0, :, cols].astype(f32) * v[0, :, cols].astype(f32)).astype(bf16)
        dest[0] = gated
        dest[1] = grad
        if r >= 2:
            sel = jnp.where(upper == 0, gated.astype(f32), grad.astype(f32)).astype(bf16)
            (to2 if r == 2 else to3)[...] = sel


def own_filter_kernel(table, taps, near, cross, inv):
    half = taps.shape[1] // 2
    inv[...] = (table[:, half:].astype(f32).T * (1.0 / half)).astype(bf16)
    vals = taps[...].astype(bf16)
    cross[...] = mm(table[...], vals, ((1,), (1,))).astype(bf16)
    near[...] = mm(table[:, half:], vals[:, :half], ((1,), (1,))).astype(bf16)


def in_order(low, mine, partner, held):
    block = mine.shape[0]
    held[pl.ds(pl.multiple_of(low * block, block), block), :] = mine
    held[pl.ds(pl.multiple_of((1 - low) * block, block), block), :] = partner
    return held[...]


def halves(low, vals, held, mine, partner):
    held[...] = vals
    block = vals.shape[0] // 2
    mine[...] = held[pl.ds(pl.multiple_of(low * block, block), block), :]
    partner[...] = held[pl.ds(pl.multiple_of((1 - low) * block, block), block), :]


def filt_part(core, table, terms, keep, send):
    half = table.shape[1] // 2
    width = keep.shape[0]
    for dest, which in ((send, 1 - core), (keep, core)):
        cols = lanes(which * width, width)
        for first, pairs in terms:
            vals = sum(mm(q[:, cols], table[:, start : start + half], ((0,), (0,))) for q, start in pairs)
            dest[:, first : first + half] = (vals * (1.0 / half)).astype(dest.dtype)


def conv_far_kernel(idx, table, inv, mine, across, keep, recv, okeep, o1, gkeep, gsend, filt, q_far, held):
    low, dp = idx[1], idx[3]
    half = table.shape[1] // 2
    share = mine.shape[0] // 2
    fwd = table[:, half:]
    x = mm(fwd, in_order(low, keep[0], recv[0], held.at[0]))
    g = mm(fwd, in_order(low, keep[1], recv[1], held.at[1]))
    for j in range(4):
        piece = (mine if j < 2 else across)[(j % 2) * share : (j % 2 + 1) * share, :]
        filt[:, lanes((dp ^ j) * share, share)] = mm(fwd, piece, ((1,), (1,)))
    h = filt[...]
    q_far[...] = join(cmulc(x, g)).astype(bf16)
    for kind, pair in ((0, cmul(x, h)), (1, cmulc(h, g))):
        halves(low, mm(inv[...], join(pair).astype(bf16)).astype(bf16), held.at[2 + kind], okeep.at[kind], o1.at[kind])
    filt_part(dp & 1, table, [(0, [(q_far, half)])], gkeep, gsend)


def conv_own_kernel(idx, table, inv, near, cross, keep, recv, r2, r3, okeep, o1, o2, o3, gkeep, gsend, q_near, q_cross, held):
    low, upper, core = idx[1], idx[2], idx[3] & 1
    half = table.shape[1] // 2

    def inverse(pair):
        return mm(inv[...], join(pair).astype(bf16)).astype(bf16)

    def run(is_upper):
        fwd = table[:, half:]
        x = mm(fwd, in_order(low, keep[0], recv[0], held.at[0]))
        g = mm(fwd, in_order(low, keep[1], recv[1], held.at[1]))
        rec = mm(fwd, in_order(low, r2[...], r3[...], held.at[2]))
        hx = cross[...].astype(f32)
        halves(low, inverse(cmulc(hx, g) if is_upper else cmul(hx, x)), held.at[3], o2, o3)
        add = cmul(hx, rec) if is_upper else cmulc(hx, rec)
        h = near[...].astype(f32)
        conv = cmul(x, h)
        back = cmulc(h, g)
        if is_upper:
            conv = (conv[0] + add[0], conv[1] + add[1])
        else:
            back = (back[0] + add[0], back[1] + add[1])
        halves(low, inverse(conv), held.at[4], okeep.at[0], o1.at[0])
        halves(low, inverse(back), held.at[5], okeep.at[1], o1.at[1])
        q_near[...] = join(cmulc(x, g)).astype(bf16)
        q_cross[...] = join(cmulc(rec, g) if is_upper else cmulc(x, rec)).astype(bf16)

    pl.when(upper == 0)(functools.partial(run, False))
    pl.when(upper != 0)(functools.partial(run, True))
    filt_part(core, table, [(0, [(q_cross, 0), (q_near, half)]), (half, [(q_cross, half)])], gkeep, gsend)


def final_kernel(quarter, idx, q, k, g, own, far, own1, far1, r2, r3, mine, other, dq, dk, dv, grad_filt, held, filt_held, sems):
    z, upper, core = idx[0], idx[2], idx[3] & 1
    is_up = jnp.where(upper == 0, 0.0, 1.0)
    size = mine.shape[0]
    for which, piece in ((core, mine), (1 - core, other)):
        filt_held[pl.ds(pl.multiple_of(which * size, 8), size), :] = piece[...].astype(f32)
    copies = [pltpu.make_async_copy(filt_held, grad_filt, sems.at[3 * ROW_CHUNKS])]
    copies[0].start()
    rows = q.shape[1] // ROW_CHUNKS
    for c in range(ROW_CHUNKS):
        part = pl.ds(c * rows, rows)
        for r, src in enumerate((own, own1, far, far1)):
            cols = lanes((z ^ r) * quarter, quarter)
            conv = src[0, part].astype(f32)
            back = src[1, part].astype(f32)
            if r >= 2:
                add = (r2 if r == 2 else r3)[part].astype(f32)
                conv = conv + is_up * add
                back = back + (1.0 - is_up) * add
            held[0, part, cols] = (back * k[0, part, cols].astype(f32)).astype(bf16)
            held[1, part, cols] = (back * q[0, part, cols].astype(f32)).astype(bf16)
            held[2, part, cols] = (g[0, part, cols].astype(f32) * conv).astype(bf16)
        for j, dest in enumerate((dq, dk, dv)):
            copies.append(pltpu.make_async_copy(held.at[j, part], dest.at[0, part], sems.at[3 * c + j]))
            copies[-1].start()
    for copy in copies:
        copy.wait()


def half_plan(query_proj, key_proj, value_proj, out_grad, filter_taps):
    z = lax.axis_index("ctx").astype(jnp.int32)
    dp = lax.axis_index("dp").astype(jnp.int32)
    idx = jnp.stack([z, z & 1, z >> 1, dp])
    block, group = query_proj.shape[1:]
    quarter, length = filter_taps.shape
    half = length // 2
    rows = quarter // 2
    table = as_const(dft_table(length))
    macs = length * half * quarter

    def xz(vals, k):
        return lax.ppermute(vals, "ctx", [(i, i ^ k) for i in range(4)])

    def xd(vals, k):
        return lax.ppermute(vals, "dp", [(i, i ^ k) for i in range(4)])

    def apart(run, *args):
        shapes = jax.eval_shape(run, *args)
        return lax.cond(dp >= 0, run, lambda *_: jax.tree.map(lambda s: jnp.zeros(s.shape, s.dtype), shapes), *args)

    def over_cores(keep, send):
        return (keep + xd(send, 1).astype(f32)).astype(bf16)

    share = quarter // 4
    one, two, spec = ((block, quarter), bf16), ((2, block, quarter), bf16), ((length, quarter), bf16)
    act_in = ((1, block, group), lambda i, idx: (0, 0, 0))
    two_out = ((2, block, quarter), lambda i, idx: (0, 0, 0)) + two
    one_out = ((block, quarter), lambda i, idx: (0, 0)) + one
    gate_ins = [act_in] * 4 + [((share, half), lambda i, idx: (idx[3], 0))]
    gate_outs = [two_out] * 4 + [one_out] * 2 + [((share, half), lambda i, idx: (0, 0), (share, half), bf16)]
    keep_own, keep_far, own1, far1, to2, to3, piece = pl.pallas_call(
        functools.partial(gate_kernel, quarter),
        out_shape=[jax.ShapeDtypeStruct(s, d) for _, _, s, d in gate_outs],
        grid_spec=pltpu.PrefetchScalarGridSpec(
            num_scalar_prefetch=1,
            grid=(1,),
            in_specs=[pl.BlockSpec(blk, at) for blk, at in gate_ins],
            out_specs=[pl.BlockSpec(blk, at) for blk, at, _, _ in gate_outs],
        ),
        compiler_params=pltpu.CompilerParams(vmem_limit_bytes=GATE_VMEM),
        cost_estimate=pl.CostEstimate(flops=2 * block * group, bytes_accessed=16 * block * group, transcendentals=0),
    )(idx, query_proj, key_proj, value_proj, out_grad, filter_taps)
    near, cross, inv = call(
        own_filter_kernel, [spec] * 2 + [((half, length), bf16)], 2, smem_first=False, cost=(6 * macs, 16 * length * quarter)
    )(table, filter_taps)
    near, cross, inv, piece = lax.optimization_barrier((near, cross, inv, xz(piece, 2)))
    pair = jnp.concatenate([piece, xd(piece, 1)], 0)
    across = xd(pair, 2)
    far1, to2, to3, own1 = xz(far1, 1), xz(to2, 2), xz(to3, 3), xz(own1, 1)

    okeep_far, ofar1, *far_parts = call(
        conv_far_kernel,
        [two, two, ((rows, half), f32), ((rows, half), bf16)],
        6,
        cost=(32 * macs, 32 * length * quarter),
        limit=CONV_VMEM,
        scratch=[pltpu.VMEM((length, quarter), f32), pltpu.VMEM((length, quarter), bf16), pltpu.VMEM((4, half, quarter), bf16)],
    )(idx, table, inv, pair, across, keep_far, far1)
    ofar1 = xz(ofar1, 1)
    far = xz(apart(over_cores, *far_parts), 2)
    okeep, o1, o2, o3, *own_parts = call(
        conv_own_kernel,
        [two] * 2 + [one] * 2 + [((rows, length), f32), ((rows, length), bf16)],
        8,
        cost=(32 * macs, 32 * length * quarter),
        limit=CONV_VMEM,
        scratch=[pltpu.VMEM((length, quarter), bf16)] * 2 + [pltpu.VMEM((6, half, quarter), bf16)],
    )(idx, table, inv, near, cross, keep_own, own1, to2, to3)
    chip = apart(over_cores, *own_parts)

    def across_chips(chip, far, o1, o2, o3):
        chip = chip.astype(f32)
        chip = jnp.concatenate([chip[:, :half] + far.astype(f32), chip[:, half:]], 1)
        chip = lax.reduce_precision(chip, 8, 7).astype(bf16)
        theirs = xd(chip, 2)
        o1, o2, o3 = xz(o1, 1), xz(o2, 2), xz(o3, 3)

        def both_cores(chip, theirs):
            mine = (chip.astype(f32) + theirs.astype(f32)).astype(bf16)
            return mine, xd(mine, 1)

        return o1, o2, o3, *apart(both_cores, chip, theirs)

    o1, o2, o3, mine, other = apart(across_chips, chip, far, o1, o2, o3)
    act = (query_proj.shape, bf16)
    return call(
        functools.partial(final_kernel, quarter),
        [act] * 3 + [(filter_taps.shape, f32)],
        11,
        out_hbm=True,
        cost=(3 * block * group, 18 * block * group),
        scratch=[
            pltpu.VMEM((3, block, group), bf16),
            pltpu.VMEM(filter_taps.shape, f32),
            pltpu.SemaphoreType.DMA((3 * ROW_CHUNKS + 1,)),
        ],
    )(idx, query_proj, key_proj, out_grad, okeep, okeep_far, o1, ofar1, o2, o3, mine, other)


exact_mode = lax.Precision.HIGHEST
field_mode = lax.Precision.HIGH


def factor_sizes(length):
    col_count = min(128, length)
    return (2 * length // col_count, col_count)


def angle_table(first_size, second_size, period):
    product = (
        jnp.arange(first_size, dtype=jnp.int32)[:, None]
        * jnp.arange(second_size, dtype=jnp.int32)[None, :]
        % period
    )
    angles = product.astype(jnp.float32) * (2.0 * math.pi / period)
    return (jnp.cos(angles), jnp.sin(angles))


def make_tables(length):
    row_count, col_count = factor_sizes(length)
    outer_cos, outer_sin = angle_table(row_count, row_count // 2, row_count)
    twist_cos, twist_sin = angle_table(row_count, col_count, row_count * col_count)
    inner_cos, inner_sin = angle_table(col_count, col_count, col_count)
    real_outer = jnp.stack([outer_cos, -outer_sin])
    mixed_outer = jnp.stack([jnp.stack([outer_cos, outer_sin]), jnp.stack([-outer_sin, outer_cos])])
    fwd_twist = jnp.stack([twist_cos, -twist_sin])[:, None]
    inv_twist = jnp.stack([twist_cos, twist_sin])[:, None]
    fwd_inner = jnp.stack([jnp.stack([inner_cos, -inner_sin]), jnp.stack([inner_sin, inner_cos])])
    inv_inner = jnp.stack([jnp.stack([inner_cos, inner_sin]), jnp.stack([-inner_sin, inner_cos])])
    back_outer = jnp.stack([outer_cos, -outer_sin]) / float(row_count * col_count)
    return (real_outer, mixed_outer, fwd_twist, inv_twist, fwd_inner, inv_inner, back_outer)


def complex_mul(left, right):
    return jnp.stack(
        [left[0] * right[0] - left[1] * right[1], left[0] * right[1] + left[1] * right[0]]
    )


def conjugate(values):
    return jnp.stack([values[0], -values[1]])


def forward(values, tables, mode):
    real_outer, mixed_outer, fwd_twist, inv_twist, fwd_inner, inv_inner, back_outer = tables
    half_rows = real_outer.shape[2]
    col_count = fwd_inner.shape[2]
    grid = values.reshape(values.shape[0], half_rows, col_count)
    first = jnp.einsum("sca,hab->shcb", real_outer, grid, precision=mode)
    turned = complex_mul(first, fwd_twist)
    return jnp.einsum("shcb,stbd->thcd", turned, fwd_inner, precision=mode)


def inverse(spectrum, tables, mode):
    real_outer, mixed_outer, fwd_twist, inv_twist, fwd_inner, inv_inner, back_outer = tables
    back = jnp.einsum("shcd,stdb->thcb", spectrum, inv_inner, precision=mode)
    turned = complex_mul(back, inv_twist)
    out_grid = jnp.einsum("sca,shcb->hab", back_outer, turned, precision=mode)
    return out_grid.reshape(out_grid.shape[0], -1)


def whole_plan(query_proj, key_proj, value_proj, out_grad, filter_taps):
    query_vals = query_proj[0].astype(jnp.float32)
    key_vals = key_proj[0].astype(jnp.float32)
    grad_vals = out_grad[0].astype(jnp.float32)
    gated_vals = (query_vals * key_vals).astype(jnp.bfloat16).T
    grad_conv = (grad_vals * value_proj[0].astype(jnp.float32)).astype(jnp.bfloat16).T
    length = filter_taps.shape[1]
    tables = make_tables(length)
    filt_spec = forward(filter_taps, tables, exact_mode)
    gated_all = lax.all_to_all(gated_vals, "ctx", split_axis=0, concat_axis=1, tiled=True)
    gate_spec = forward(gated_all.astype(jnp.float32), tables, field_mode)
    conv_full = inverse(complex_mul(gate_spec, filt_spec), tables, field_mode).astype(jnp.bfloat16)
    conv_local = lax.all_to_all(conv_full, "ctx", split_axis=1, concat_axis=0, tiled=True)
    grad_all = lax.all_to_all(grad_conv, "ctx", split_axis=0, concat_axis=1, tiled=True)
    grad_spec = forward(grad_all.astype(jnp.float32), tables, field_mode)
    back_full = inverse(complex_mul(grad_spec, conjugate(filt_spec)), tables, field_mode).astype(
        jnp.bfloat16
    )
    back_local = lax.all_to_all(back_full, "ctx", split_axis=1, concat_axis=0, tiled=True)
    grad_v = (grad_vals * conv_local.T.astype(jnp.float32)).astype(jnp.bfloat16)[None]
    back_vals = back_local.T.astype(jnp.float32)
    grad_q = (back_vals * key_vals).astype(jnp.bfloat16)[None]
    grad_k = (back_vals * query_vals).astype(jnp.bfloat16)[None]
    cross_spec = complex_mul(conjugate(gate_spec), grad_spec)
    grad_filt = lax.psum(inverse(cross_spec, tables, exact_mode).astype(jnp.bfloat16), "dp").astype(
        jnp.float32
    )
    return (grad_q, grad_k, grad_v, grad_filt)

def solution(mesh):
    split = mesh.shape["ctx"] == 4 and mesh.shape["dp"] == 4
    body = half_plan if split else whole_plan
    acts = P("dp", "ctx", "chan")
    taps = P(("chan", "ctx"), None)
    return jax.shard_map(
        body,
        mesh=mesh,
        in_specs=(acts, acts, acts, acts, taps),
        out_specs=(acts, acts, acts, taps),
        check_vma=False,
    )
```

profile of v0, /device:TPU:0, one launch (start us, length us, event | category | flops | bytes accessed | tf_op | source)
XLA Modules:
  0.0 59.8 jit_solution(8385995632172001608)
XLA Ops:
  1.3 3.5 %shard_map.94 = (bf16[2,128,512]{2,1,0:T(8,128)(2,1)}, bf16[2,128,512]{2,1,0:T(8,128)(2,1)}, bf16[2,128,512]{2,1,0:T(8,128)(2,1)}, bf16[2,128,512]{2,1,0:T(8,128...) custom-call(s32[4]{0:T(128)} %pad_add_fusion.idx, bf16[1,128,2048]{2,1,0:T(8,128)(2,1)} %q.3, ...), custom_call_target="tpu_custom_call" | custom-call | flops 524288 | bytes 4194304 | tf_op jit(solution)/shard_map/pallas_call | solution.py:227
  4.8 4.0 %collective-permute-start.7 = (bf16[128,256]{1,0:T(8,128)(2,1)}, bf16[128,256]{1,0:T(8,128)(2,1)S(1)}, u32[]{:S(2)}, u32[]{:S(2)}) collective-permute-start(bf16[128,256]{1,0:T(8,128)(2,1)} %get-tuple-element.80), channel_id=1, source_target_pairs={{0,2},{1,3},{2,0},{3,1},{4,6},{5,7},{6,4},{7,5},{8,10},{9,11},{10,... | collective-permute-start | bytes 196616 | tf_op jit(solution)/shard_map/ppermute | solution.py:208
  8.8 1.6 %collective-permute-start.13 = (bf16[2,128,512]{2,1,0:T(8,128)(2,1)}, bf16[2,128,512]{2,1,0:T(8,128)(2,1)S(1)}, u32[]{:S(2)}, u32[]{:S(2)}) collective-permute-start(bf16[2,128,512]{2,1,0:T(8,128)(2,1)} %get-tuple-element.91), channel_id=1, source_target_pairs={{0,1},{1,0},{2,3},{3,2},{4,5},{5,4},{6,7},{7,6},{8,9},{9,8},{10,11... | collective-permute-start | bytes 786440 | tf_op jit(solution)/shard_map/ppermute | solution.py:208
  12.3 1.2 %collective-permute-done.11 = bf16[128,256]{1,0:T(8,128)(2,1)S(1)} collective-permute-done((bf16[128,256]{1,0:T(8,128)(2,1)S(1)}, bf16[128,256]{1,0:T(8,128)(2,1)S(1)}, u32[]{:S(2)}, u32[]{:S(2)}) %collective-permute-start.11) | collective-permute-done | bytes 65568 | tf_op jit(solution)/shard_map/ppermute | solution.py:211
  13.6 1.6 %collective-permute-start.12 = (bf16[256,256]{1,0:T(8,128)(2,1)S(1)}, bf16[256,256]{1,0:T(8,128)(2,1)S(1)}, u32[]{:S(2)}, u32[]{:S(2)}) collective-permute-start(bf16[256,256]{1,0:T(8,128)(2,1)S(1)} %constant_dynamic-update-slice_fusion.mine), channel_id=1, source_target_pairs={{0,16},{8,24},{16,0},{24,8},{1,17},{9,25},{17,1},{25,9},{2,18},{10... | collective-permute-start | bytes 393224 | tf_op jit(solution)/shard_map/ppermute | solution.py:211
  15.2 1.5 %collective-permute-start.8 = (bf16[2,128,512]{2,1,0:T(8,128)(2,1)}, bf16[2,128,512]{2,1,0:T(8,128)(2,1)S(1)}, u32[]{:S(2)}, u32[]{:S(2)}) collective-permute-start(bf16[2,128,512]{2,1,0:T(8,128)(2,1)} %get-tuple-element.85), channel_id=1, source_target_pairs={{0,1},{1,0},{2,3},{3,2},{4,5},{5,4},{6,7},{7,6},{8,9},{9,8},{10,11... | collective-permute-start | bytes 786440 | tf_op jit(solution)/shard_map/ppermute | solution.py:208
  16.6 2.3 %collective-permute-start.10 = (bf16[128,512]{1,0:T(8,128)(2,1)}, bf16[128,512]{1,0:T(8,128)(2,1)S(1)}, u32[]{:S(2)}, u32[]{:S(2)}) collective-permute-start(bf16[128,512]{1,0:T(8,128)(2,1)} %get-tuple-element.87), channel_id=1, source_target_pairs={{0,3},{1,2},{2,1},{3,0},{4,7},{5,6},{6,5},{7,4},{8,11},{9,10},{10,... | collective-permute-start | bytes 393224 | tf_op jit(solution)/shard_map/ppermute | solution.py:208
  19.6 3.0 %shard_map.96 = (bf16[2,128,512]{2,1,0:T(8,128)(2,1)S(1)}, bf16[2,128,512]{2,1,0:T(8,128)(2,1)S(1)}, f32[256,256]{1,0:T(8,128)}, bf16[256,256]{1,0:T(8,128)(2,1)}) custom-call(s32[4]{0:T(128)S(1)} %copy-done.5, bf16[512,512]{1,0:T(8,128)(2,1)S(1)} %copy-done.4, bf16[256,512]{1,0:T(8,128)(2,1)S(1)} %get-tuple-element.81.inv, ...), custom_call_target="tpu_custom_call" | custom-call | flops 2147483648 | bytes 8388608 | tf_op jit(solution)/shard_map/pallas_call | solution.py:247
  22.5 1.5 %collective-permute-start.15 = (bf16[2,128,512]{2,1,0:T(8,128)(2,1)S(1)}, bf16[2,128,512]{2,1,0:T(8,128)(2,1)S(1)}, u32[]{:S(2)}, u32[]{:S(2)}) collective-permute-start(bf16[2,128,512]{2,1,0:T(8,128)(2,1)S(1)} %get-tuple-element.101), channel_id=1, source_target_pairs={{0,1},{1,0},{2,3},{3,2},{4,5},{5,4},{6,7},{7,6},{8,9},{9,8},{10,11... | collective-permute-start | bytes 786440 | tf_op jit(solution)/shard_map/ppermute | solution.py:208
  24.0 3.2 %conditional.5 = (bf16[256,256]{1,0:T(8,128)(2,1)}) conditional(s32[]{:T(128)} %convert_element_type.38, () %tuple.40, (bf16[256,256]{1,0:T(8,128)(2,1)}, f32[256,256]{1,0:T(8,128)}) %tuple.41), branch_computations={%region_2.0_spmd, %region_3.0_spmd} | conditional | flops 196608 | bytes 1048624 | solution.py:215
  24.0 1.6 %collective-permute-done.1 = bf16[256,256]{1,0:T(8,128)(2,1)S(1)} collective-permute-done((bf16[256,256]{1,0:T(8,128)(2,1)}, bf16[256,256]{1,0:T(8,128)(2,1)S(1)}, u32[]{:S(2)}, u32[]{:S(2)}) %collective-permute-start.1) | collective-permute-done | bytes 131104 | tf_op jit(solution)/shard_map/cond/branch_1_fun/ppermute | solution.py:211
  25.6 1.6 %add_convert_fusion.1 = bf16[256,256]{1,0:T(8,128)(2,1)} fusion(f32[256,256]{1,0:T(8,128)} %get-tuple-element.32, bf16[256,256]{1,0:T(8,128)(2,1)S(1)} %collective-permute-done.1), kind=kLoop, calls=%fused_computation.1 | loop fusion | flops 196608 | bytes 524288 | tf_op jit(solution)/shard_map/cond/branch_1_fun/convert_element_type | solution.py:218
  27.2 2.4 %collective-permute-start.14 = (bf16[256,256]{1,0:T(8,128)(2,1)}, bf16[256,256]{1,0:T(8,128)(2,1)}, u32[]{:S(2)}, u32[]{:S(2)}) collective-permute-start(bf16[256,256]{1,0:T(8,128)(2,1)} %get-tuple-element.121), channel_id=1, source_target_pairs={{0,2},{1,3},{2,0},{3,1},{4,6},{5,7},{6,4},{7,5},{8,10},{9,11},{10,... | collective-permute-start | bytes 393224 | tf_op jit(solution)/shard_map/ppermute | solution.py:208
  32.3 3.9 %shard_map.95 = (bf16[2,128,512]{2,1,0:T(8,128)(2,1)S(1)}, bf16[2,128,512]{2,1,0:T(8,128)(2,1)}, bf16[128,512]{1,0:T(8,128)(2,1)}, bf16[128,512]{1,0:T(8,128)(2,...) custom-call(s32[4]{0:T(128)S(1)} %copy-done.5, bf16[512,512]{1,0:T(8,128)(2,1)S(1)} %copy-done.4, ...), custom_call_target="tpu_custom_call" | custom-call | flops 2147483648 | bytes 8388608 | tf_op jit(solution)/shard_map/pallas_call | solution.py:257
  36.2 2.9 %conditional.4 = (bf16[256,512]{1,0:T(8,128)(2,1)S(1)}) conditional(s32[]{:T(128)} %convert_element_type.38, () %tuple.38, (bf16[256,512]{1,0:T(8,128)(2,1)}, f32[256,512]{1,0:T(8,128)}) %tuple.39), branch_computations={%region_0.0_spmd, %region_1.0_spmd} | conditional | flops 393216 | bytes 2097200 | solution.py:215
  36.2 1.7 %collective-permute-done = bf16[256,512]{1,0:T(8,128)(2,1)S(1)} collective-permute-done((bf16[256,512]{1,0:T(8,128)(2,1)}, bf16[256,512]{1,0:T(8,128)(2,1)S(1)}, u32[]{:S(2)}, u32[]{:S(2)}) %collective-permute-start) | collective-permute-done | bytes 262176 | tf_op jit(solution)/shard_map/cond/branch_1_fun/ppermute | solution.py:211
  39.1 17.7 %conditional.6 = (bf16[2,128,512]{2,1,0:T(8,128)(2,1)}, bf16[128,512]{1,0:T(8,128)(2,1)}, bf16[128,512]{1,0:T(8,128)(2,1)}, bf16[256,512]{1,0:T(8,128)(2,1)}, bf16[256,512]{1,0:T(8,128)(2,1)}) conditional(s32[]{:T(128)} %convert_element_type.38, () %tuple.37, (bf16[2,128,512]{2,1,0:T(8,128)(2,1)S(1)}, bf16[128,512]{1,0:T(8,128)(2,1)S(1)}, ...), branch_computations={%region_4.0_spmd, %region_5.0_spmd} | conditional | flops 1179650 | bytes 7733534 | solution.py:215
  40.9 1.8 %collective-permute-start.3 = (bf16[2,128,512]{2,1,0:T(8,128)(2,1)S(1)}, bf16[2,128,512]{2,1,0:T(8,128)(2,1)}, u32[]{:S(2)}, u32[]{:S(2)}) collective-permute-start(bf16[2,128,512]{2,1,0:T(8,128)(2,1)S(1)} %get-tuple-element.36), channel_id=1, source_target_pairs={{0,1},{1,0},{2,3},{3,2},{4,5},{5,4},{6,7},{7,6},{8,9},{9,8},{10,11... | collective-permute-start | bytes 786440 | tf_op jit(solution)/shard_map/cond/branch_1_fun/ppermute | solution.py:208
  42.8 2.2 %collective-permute-start.4 = (bf16[128,512]{1,0:T(8,128)(2,1)S(1)}, bf16[128,512]{1,0:T(8,128)(2,1)}, u32[]{:S(2)}, u32[]{:S(2)}) collective-permute-start(bf16[128,512]{1,0:T(8,128)(2,1)S(1)} %get-tuple-element.37), channel_id=1, source_target_pairs={{0,2},{1,3},{2,0},{3,1},{4,6},{5,7},{6,4},{7,5},{8,10},{9,11},{10,... | collective-permute-start | bytes 393224 | tf_op jit(solution)/shard_map/cond/branch_1_fun/ppermute | solution.py:208
  45.3 3.4 %collective-permute-done.6 = bf16[256,512]{1,0:T(8,128)(2,1)S(1)} collective-permute-done((bf16[256,512]{1,0:T(8,128)(2,1)S(1)}, bf16[256,512]{1,0:T(8,128)(2,1)S(1)}, u32[]{:S(2)}, u32[]{:S(2)}) %collective-permute-start.6) | collective-permute-done | bytes 262176 | tf_op jit(solution)/shard_map/cond/branch_1_fun/ppermute | solution.py:211
  48.7 2.6 %conditional = (bf16[256,512]{1,0:T(8,128)(2,1)}, bf16[256,512]{1,0:T(8,128)(2,1)}) conditional(s32[]{:T(128)} %convert_element_type.33, () %tuple.25, (bf16[256,512]{1,0:T(8,128)(2,1)S(1)}, bf16[256,512]{1,0:T(8,128)(2,1)S(1)}) %tuple.26), branch_computations={%region_6.0_spmd, %region_7.0_spmd} | conditional | flops 524288 | bytes 1835064 | solution.py:215
  49.5 1.9 %collective-permute-done.2 = bf16[256,512]{1,0:T(8,128)(2,1)} collective-permute-done((bf16[256,512]{1,0:T(8,128)(2,1)}, bf16[256,512]{1,0:T(8,128)(2,1)}, u32[]{:S(2)}, u32[]{:S(2)}) %collective-permute-start.2) | collective-permute-done | bytes 262176 | tf_op jit(solution)/shard_map/cond/branch_1_fun/cond/branch_1_fun/ppermute | solution.py:211
  52.3 4.5 %collective-permute-done.5 = bf16[128,512]{1,0:T(8,128)(2,1)} collective-permute-done((bf16[128,512]{1,0:T(8,128)(2,1)}, bf16[128,512]{1,0:T(8,128)(2,1)}, u32[]{:S(2)}, u32[]{:S(2)}) %collective-permute-start.5) | collective-permute-done | bytes 131104 | tf_op jit(solution)/shard_map/cond/branch_1_fun/ppermute | solution.py:208
  56.8 2.9 %shard_map.97 = (bf16[1,128,2048]{2,1,0:T(8,128)(2,1)}, bf16[1,128,2048]{2,1,0:T(8,128)(2,1)}, bf16[1,128,2048]{2,1,0:T(8,128)(2,1)}, f32[512,512]{1,0:T(8,128)}) custom-call(s32[4]{0:T(128)S(1)} %copy-done.5, bf16[1,128,2048]{2,1,0:T(8,128)(2,1)S(1)} %copy-done.1, bf16[1,128,2048]{2,1,0:T(8,128)(2,1)S(1)} %copy-done.2, bf16[1,128,2048]{2,1,0:T(8,128)(2,1)S(1)} %copy-done.3, ...), custom_call_target="tpu_custom_call" | custom-call | flops 786432 | bytes 4718592 | tf_op jit(solution)/shard_map/pallas_call | solution.py:282
  (51 shorter events, 10.9 us)
Async XLA Ops:
  1.3 9.1 %copy-start.4 = (bf16[512,512]{1,0:T(8,128)(2,1)S(1)}, bf16[512,512]{1,0:T(8,128)(2,1)}, u32[]{:S(2)}) copy-start(bf16[512,512]{1,0:T(8,128)(2,1)} %constant.17.clone.table) | copy-start | bytes 1572868
  4.8 7.5 %collective-permute-start.7 = (bf16[128,256]{1,0:T(8,128)(2,1)}, bf16[128,256]{1,0:T(8,128)(2,1)S(1)}, u32[]{:S(2)}, u32[]{:S(2)}) collective-permute-start(bf16[128,256]{1,0:T(8,128)(2,1)} %get-tuple-element.80), channel_id=1, source_target_pairs={{0,2},{1,3},{2,0},{3,1},{4,6},{5,7},{6,4},{7,5},{8,10},{9,11},{10,... | collective-permute-start | bytes 196616 | tf_op jit(solution)/shard_map/ppermute | solution.py:208
  8.8 10.6 %collective-permute-start.13 = (bf16[2,128,512]{2,1,0:T(8,128)(2,1)}, bf16[2,128,512]{2,1,0:T(8,128)(2,1)S(1)}, u32[]{:S(2)}, u32[]{:S(2)}) collective-permute-start(bf16[2,128,512]{2,1,0:T(8,128)(2,1)} %get-tuple-element.91), channel_id=1, source_target_pairs={{0,1},{1,0},{2,3},{3,2},{4,5},{5,4},{6,7},{7,6},{8,9},{9,8},{10,11... | collective-permute-start | bytes 786440 | tf_op jit(solution)/shard_map/ppermute | solution.py:208
  12.2 7.2 %copy-start.9 = (bf16[2,128,512]{2,1,0:T(8,128)(2,1)S(1)}, bf16[2,128,512]{2,1,0:T(8,128)(2,1)}, u32[]{:S(2)}) copy-start(bf16[2,128,512]{2,1,0:T(8,128)(2,1)} %get-tuple-element.90.keep) | copy-start | bytes 786436
  12.2 1.3 %collective-permute-start.11 = (bf16[128,256]{1,0:T(8,128)(2,1)S(1)}, bf16[128,256]{1,0:T(8,128)(2,1)S(1)}, u32[]{:S(2)}, u32[]{:S(2)}) collective-permute-start(bf16[128,256]{1,0:T(8,128)(2,1)S(1)} %collective-permute-done.7), channel_id=1, source_target_pairs={{0,8},{8,0},{16,24},{24,16},{1,9},{9,1},{17,25},{25,17},{2,10},{10... | collective-permute-start | bytes 196616 | tf_op jit(solution)/shard_map/ppermute | solution.py:211
  13.6 5.9 %collective-permute-start.12 = (bf16[256,256]{1,0:T(8,128)(2,1)S(1)}, bf16[256,256]{1,0:T(8,128)(2,1)S(1)}, u32[]{:S(2)}, u32[]{:S(2)}) collective-permute-start(bf16[256,256]{1,0:T(8,128)(2,1)S(1)} %constant_dynamic-update-slice_fusion.mine), channel_id=1, source_target_pairs={{0,16},{8,24},{16,0},{24,8},{1,17},{9,25},{17,1},{25,9},{2,18},{10... | collective-permute-start | bytes 393224 | tf_op jit(solution)/shard_map/ppermute | solution.py:211
  15.2 15.5 %collective-permute-start.8 = (bf16[2,128,512]{2,1,0:T(8,128)(2,1)}, bf16[2,128,512]{2,1,0:T(8,128)(2,1)S(1)}, u32[]{:S(2)}, u32[]{:S(2)}) collective-permute-start(bf16[2,128,512]{2,1,0:T(8,128)(2,1)} %get-tuple-element.85), channel_id=1, source_target_pairs={{0,1},{1,0},{2,3},{3,2},{4,5},{5,4},{6,7},{7,6},{8,9},{9,8},{10,11... | collective-permute-start | bytes 786440 | tf_op jit(solution)/shard_map/ppermute | solution.py:208
  16.6 13.0 %collective-permute-start.10 = (bf16[128,512]{1,0:T(8,128)(2,1)}, bf16[128,512]{1,0:T(8,128)(2,1)S(1)}, u32[]{:S(2)}, u32[]{:S(2)}) collective-permute-start(bf16[128,512]{1,0:T(8,128)(2,1)} %get-tuple-element.87), channel_id=1, source_target_pairs={{0,3},{1,2},{2,1},{3,0},{4,7},{5,6},{6,5},{7,4},{8,11},{9,10},{10,... | collective-permute-start | bytes 393224 | tf_op jit(solution)/shard_map/ppermute | solution.py:208
  18.9 11.7 %collective-permute-start.9 = (bf16[128,512]{1,0:T(8,128)(2,1)}, bf16[128,512]{1,0:T(8,128)(2,1)S(1)}, u32[]{:S(2)}, u32[]{:S(2)}) collective-permute-start(bf16[128,512]{1,0:T(8,128)(2,1)} %get-tuple-element.86), channel_id=1, source_target_pairs={{0,2},{1,3},{2,0},{3,1},{4,6},{5,7},{6,4},{7,5},{8,10},{9,11},{10,... | collective-permute-start | bytes 393224 | tf_op jit(solution)/shard_map/ppermute | solution.py:208
  22.5 34.3 %collective-permute-start.15 = (bf16[2,128,512]{2,1,0:T(8,128)(2,1)S(1)}, bf16[2,128,512]{2,1,0:T(8,128)(2,1)S(1)}, u32[]{:S(2)}, u32[]{:S(2)}) collective-permute-start(bf16[2,128,512]{2,1,0:T(8,128)(2,1)S(1)} %get-tuple-element.101), channel_id=1, source_target_pairs={{0,1},{1,0},{2,3},{3,2},{4,5},{5,4},{6,7},{7,6},{8,9},{9,8},{10,11... | collective-permute-start | bytes 786440 | tf_op jit(solution)/shard_map/ppermute | solution.py:208
  24.0 7.4 %copy-start.6 = (bf16[2,128,512]{2,1,0:T(8,128)(2,1)S(1)}, bf16[2,128,512]{2,1,0:T(8,128)(2,1)}, u32[]{:S(2)}) copy-start(bf16[2,128,512]{2,1,0:T(8,128)(2,1)} %get-tuple-element.84.keep) | copy-start | bytes 786436
  24.0 1.6 %collective-permute-start.1 = (bf16[256,256]{1,0:T(8,128)(2,1)}, bf16[256,256]{1,0:T(8,128)(2,1)S(1)}, u32[]{:S(2)}, u32[]{:S(2)}) collective-permute-start(bf16[256,256]{1,0:T(8,128)(2,1)} %get-tuple-element.33), channel_id=1, source_target_pairs={{0,8},{8,0},{16,24},{24,16},{1,9},{9,1},{17,25},{25,17},{2,10},{10... | collective-permute-start | bytes 393224 | tf_op jit(solution)/shard_map/cond/branch_1_fun/ppermute | solution.py:211
  27.2 11.9 %collective-permute-start.14 = (bf16[256,256]{1,0:T(8,128)(2,1)}, bf16[256,256]{1,0:T(8,128)(2,1)}, u32[]{:S(2)}, u32[]{:S(2)}) collective-permute-start(bf16[256,256]{1,0:T(8,128)(2,1)} %get-tuple-element.121), channel_id=1, source_target_pairs={{0,2},{1,3},{2,0},{3,1},{4,6},{5,7},{6,4},{7,5},{8,10},{9,11},{10,... | collective-permute-start | bytes 393224 | tf_op jit(solution)/shard_map/ppermute | solution.py:208
  36.2 2.9 %copy-start.10 = (bf16[2,128,512]{2,1,0:T(8,128)(2,1)S(1)}, bf16[2,128,512]{2,1,0:T(8,128)(2,1)}, u32[]{:S(2)}) copy-start(bf16[2,128,512]{2,1,0:T(8,128)(2,1)} %get-tuple-element.93) | copy-start | bytes 786436
  36.2 2.9 %copy-start.11 = (bf16[128,512]{1,0:T(8,128)(2,1)S(1)}, bf16[128,512]{1,0:T(8,128)(2,1)}, u32[]{:S(2)}) copy-start(bf16[128,512]{1,0:T(8,128)(2,1)} %get-tuple-element.94) | copy-start | bytes 393220
  36.2 1.7 %collective-permute-start = (bf16[256,512]{1,0:T(8,128)(2,1)}, bf16[256,512]{1,0:T(8,128)(2,1)S(1)}, u32[]{:S(2)}, u32[]{:S(2)}) collective-permute-start(bf16[256,512]{1,0:T(8,128)(2,1)} %get-tuple-element.12), channel_id=1, source_target_pairs={{0,8},{8,0},{16,24},{24,16},{1,9},{9,1},{17,25},{25,17},{2,10},{10... | collective-permute-start | bytes 786440 | tf_op jit(solution)/shard_map/cond/branch_1_fun/ppermute | solution.py:211
  39.1 17.7 %copy-start.1 = (bf16[1,128,2048]{2,1,0:T(8,128)(2,1)S(1)}, bf16[1,128,2048]{2,1,0:T(8,128)(2,1)}, u32[]{:S(2)}) copy-start(bf16[1,128,2048]{2,1,0:T(8,128)(2,1)} %q.3) | copy-start | bytes 1572868
  39.1 17.7 %copy-start.2 = (bf16[1,128,2048]{2,1,0:T(8,128)(2,1)S(1)}, bf16[1,128,2048]{2,1,0:T(8,128)(2,1)}, u32[]{:S(2)}) copy-start(bf16[1,128,2048]{2,1,0:T(8,128)(2,1)} %k.3) | copy-start | bytes 1572868
  39.1 17.7 %copy-start.3 = (bf16[1,128,2048]{2,1,0:T(8,128)(2,1)S(1)}, bf16[1,128,2048]{2,1,0:T(8,128)(2,1)}, u32[]{:S(2)}) copy-start(bf16[1,128,2048]{2,1,0:T(8,128)(2,1)} %g.3) | copy-start | bytes 1572868
  40.3 8.4 %collective-permute-start.6 = (bf16[256,512]{1,0:T(8,128)(2,1)S(1)}, bf16[256,512]{1,0:T(8,128)(2,1)S(1)}, u32[]{:S(2)}, u32[]{:S(2)}) collective-permute-start(bf16[256,512]{1,0:T(8,128)(2,1)S(1)} %fusion), channel_id=1, source_target_pairs={{0,16},{8,24},{16,0},{24,8},{1,17},{9,25},{17,1},{25,9},{2,18},{10... | collective-permute-start | bytes 786440 | tf_op jit(solution)/shard_map/cond/branch_1_fun/ppermute | solution.py:211
  40.9 15.9 %collective-permute-start.3 = (bf16[2,128,512]{2,1,0:T(8,128)(2,1)S(1)}, bf16[2,128,512]{2,1,0:T(8,128)(2,1)}, u32[]{:S(2)}, u32[]{:S(2)}) collective-permute-start(bf16[2,128,512]{2,1,0:T(8,128)(2,1)S(1)} %get-tuple-element.36), channel_id=1, source_target_pairs={{0,1},{1,0},{2,3},{3,2},{4,5},{5,4},{6,7},{7,6},{8,9},{9,8},{10,11... | collective-permute-start | bytes 786440 | tf_op jit(solution)/shard_map/cond/branch_1_fun/ppermute | solution.py:208
  42.8 9.6 %collective-permute-start.4 = (bf16[128,512]{1,0:T(8,128)(2,1)S(1)}, bf16[128,512]{1,0:T(8,128)(2,1)}, u32[]{:S(2)}, u32[]{:S(2)}) collective-permute-start(bf16[128,512]{1,0:T(8,128)(2,1)S(1)} %get-tuple-element.37), channel_id=1, source_target_pairs={{0,2},{1,3},{2,0},{3,1},{4,6},{5,7},{6,4},{7,5},{8,10},{9,11},{10,... | collective-permute-start | bytes 393224 | tf_op jit(solution)/shard_map/cond/branch_1_fun/ppermute | solution.py:208
  44.9 11.9 %collective-permute-start.5 = (bf16[128,512]{1,0:T(8,128)(2,1)}, bf16[128,512]{1,0:T(8,128)(2,1)}, u32[]{:S(2)}, u32[]{:S(2)}) collective-permute-start(bf16[128,512]{1,0:T(8,128)(2,1)} %get-tuple-element.38), channel_id=1, source_target_pairs={{0,3},{1,2},{2,1},{3,0},{4,7},{5,6},{6,5},{7,4},{8,11},{9,10},{10,... | collective-permute-start | bytes 393224 | tf_op jit(solution)/shard_map/cond/branch_1_fun/ppermute | solution.py:208
  49.5 1.9 %collective-permute-start.2 = (bf16[256,512]{1,0:T(8,128)(2,1)}, bf16[256,512]{1,0:T(8,128)(2,1)}, u32[]{:S(2)}, u32[]{:S(2)}) collective-permute-start(bf16[256,512]{1,0:T(8,128)(2,1)} %add_convert_fusion.2), channel_id=1, source_target_pairs={{0,8},{8,0},{16,24},{24,16},{1,9},{9,1},{17,25},{25,17},{2,10},{10... | collective-permute-start | bytes 786440 | tf_op jit(solution)/shard_map/cond/branch_1_fun/cond/branch_1_fun/ppermute | solution.py:211
  (4 other events, 3.5 us)
where the time goes:
time: 60.1 us; the launch traced here: 59.8 us
  starting transfers between devices  20.4 us (34%)
  waiting for transfers between devices  16.3 us (27%)
  Pallas kernels  13.8 us (23%)
  other arithmetic  5.3 us (9%)
  local copies, waits for them, and re-layouts  3.12 us (5%)
  between operations  0.77 us (1%)
    ppermute x10, starting transfers between devices, xz(): return lax.ppermute(vals, 'ctx', [(i, i ^ k) for i in range(4)])  18.1 us
    ppermute x6, waiting for transfers between devices, xd(): return lax.ppermute(vals, 'dp', [(i, i ^ k) for i in range(4)])  9.82 us
    ppermute x10, waiting for transfers between devices, xz(): return lax.ppermute(vals, 'ctx', [(i, i ^ k) for i in range(4)])  6.45 us
    pallas_call x1, Pallas kernels, half_plan(): call(conv_own_kernel, [two] * 2 + [one] * 2 + [((rows, length), f32), ((r...  3.89 us
    pallas_call x1, Pallas kernels, half_plan(): pl.pallas_call(functools.partial(gate_kernel, quarter), out_shape=[jax.Sh...  3.46 us
    unnamed x25, local copies, waits for them, and re-layouts  3.09 us
    pallas_call x1, Pallas kernels, half_plan(): call(conv_far_kernel, [two, two, ((rows, half), f32), ((rows, half), bf16...  2.96 us
    pallas_call x1, Pallas kernels, half_plan(): call(functools.partial(final_kernel, quarter), [act] * 3 + [(filter_taps....  2.92 us
  transfers between devices with their start and end apart: 16, of which 8 were waited for; matrix products, arithmetic and copies ran while one was open for 8% of the time, Pallas kernels for 12%

commit v1 on v0

--- a/solution.py
+++ b/solution.py
@@ -54,7 +54,7 @@
 
 
 def call(kernel, outs, n_in, smem_first=True, cost=(0, 0), limit=VMEM_LIMIT, in_hbm=0, out_hbm=False, scratch=()):
-    vmem, hbm = pl.BlockSpec(memory_space=pltpu.VMEM), pl.BlockSpec(memory_space=pltpu.HBM)
+    vmem, hbm = pl.BlockSpec(memory_space=pltpu.VMEM), pl.BlockSpec(memory_space=pl.ANY)
     in_specs = [hbm] * in_hbm + [vmem] * (n_in - in_hbm)
     if smem_first:
         in_specs = [pl.BlockSpec(memory_space=pltpu.SMEM)] + in_specs
@@ -115,26 +115,41 @@
             dest[:, first : first + half] = (vals * (1.0 / half)).astype(dest.dtype)
 
 
-def conv_far_kernel(idx, table, inv, mine, across, keep, recv, okeep, o1, gkeep, gsend, filt, q_far, held):
-    low, dp = idx[1], idx[3]
+def conv_far_kernel(idx, table, inv, mine, other, keep, recv, okeep, o1, gkeep, gsend, filt, q_far, held):
+    low, core = idx[1], idx[3] & 1
     half = table.shape[1] // 2
-    share = mine.shape[0] // 2
+    share = mine.shape[0]
     fwd = table[:, half:]
     x = mm(fwd, in_order(low, keep[0], recv[0], held.at[0]))
     g = mm(fwd, in_order(low, keep[1], recv[1], held.at[1]))
-    for j in range(4):
-        piece = (mine if j < 2 else across)[(j % 2) * share : (j % 2 + 1) * share, :]
-        filt[:, lanes((dp ^ j) * share, share)] = mm(fwd, piece, ((1,), (1,)))
+    for which, piece in ((core, mine), (1 - core, other)):
+        filt[:, lanes(which * share, share)] = mm(fwd, piece[...], ((1,), (1,)))
     h = filt[...]
     q_far[...] = join(cmulc(x, g)).astype(bf16)
     for kind, pair in ((0, cmul(x, h)), (1, cmulc(h, g))):
         halves(low, mm(inv[...], join(pair).astype(bf16)).astype(bf16), held.at[2 + kind], okeep.at[kind], o1.at[kind])
-    filt_part(dp & 1, table, [(0, [(q_far, half)])], gkeep, gsend)
-
-
-def conv_own_kernel(idx, table, inv, near, cross, keep, recv, r2, r3, okeep, o1, o2, o3, gkeep, gsend, q_near, q_cross, held):
+    filt_part(core, table, [(0, [(q_far, half)])], gkeep, gsend)
+
+
+def cross_kernel(idx, table, inv, cross, keep, recv, o2, o3, held):
+    low, upper = idx[1], idx[2]
+    half = table.shape[1] // 2
+    spec = mm(table[:, half:], in_order(low, keep[upper], recv[upper], held.at[0]))
+    h = cross[...].astype(f32)
+    sign = jnp.where(upper == 0, 1.0, -1.0)
+    pair = cmul(jnp.concatenate([h[:half], h[half:] * sign], 0), spec)
+    halves(low, mm(inv[...], join(pair).astype(bf16)).astype(bf16), held.at[1], o2, o3)
+
+
+def conv_own_kernel(idx, r2, r3, table, inv, near, cross, keep, recv, okeep, o1, gkeep, gsend, q_near, q_cross, held, sems):
     low, upper, core = idx[1], idx[2], idx[3] & 1
     half = table.shape[1] // 2
+    block = r2.shape[0]
+    loads = []
+    for j, (src, place) in enumerate(((r2, low), (r3, 1 - low))):
+        at = pl.ds(pl.multiple_of(place * block, block), block)
+        loads.append(pltpu.make_async_copy(src, held.at[2, at], sems.at[j]))
+        loads[j].start()
 
     def inverse(pair):
         return mm(inv[...], join(pair).astype(bf16)).astype(bf16)
@@ -143,9 +158,10 @@
         fwd = table[:, half:]
         x = mm(fwd, in_order(low, keep[0], recv[0], held.at[0]))
         g = mm(fwd, in_order(low, keep[1], recv[1], held.at[1]))
-        rec = mm(fwd, in_order(low, r2[...], r3[...], held.at[2]))
+        for load in loads:
+            load.wait()
+        rec = mm(fwd, held[2])
         hx = cross[...].astype(f32)
-        halves(low, inverse(cmulc(hx, g) if is_upper else cmul(hx, x)), held.at[3], o2, o3)
         add = cmul(hx, rec) if is_upper else cmulc(hx, rec)
         h = near[...].astype(f32)
         conv = cmul(x, h)
@@ -154,8 +170,8 @@
             conv = (conv[0] + add[0], conv[1] + add[1])
         else:
             back = (back[0] + add[0], back[1] + add[1])
-        halves(low, inverse(conv), held.at[4], okeep.at[0], o1.at[0])
-        halves(low, inverse(back), held.at[5], okeep.at[1], o1.at[1])
+        halves(low, inverse(conv), held.at[3], okeep.at[0], o1.at[0])
+        halves(low, inverse(back), held.at[4], okeep.at[1], o1.at[1])
         q_near[...] = join(cmulc(x, g)).astype(bf16)
         q_cross[...] = join(cmulc(rec, g) if is_upper else cmulc(x, rec)).astype(bf16)
 
@@ -215,14 +231,14 @@
         return lax.cond(dp >= 0, run, lambda *_: jax.tree.map(lambda s: jnp.zeros(s.shape, s.dtype), shapes), *args)
 
     def over_cores(keep, send):
-        return (keep + xd(send, 1).astype(f32)).astype(bf16)
-
-    share = quarter // 4
+        return (keep.astype(f32) + xd(send, 1).astype(f32)).astype(bf16)
+
+    share = quarter // 2
     one, two, spec = ((block, quarter), bf16), ((2, block, quarter), bf16), ((length, quarter), bf16)
     act_in = ((1, block, group), lambda i, idx: (0, 0, 0))
     two_out = ((2, block, quarter), lambda i, idx: (0, 0, 0)) + two
     one_out = ((block, quarter), lambda i, idx: (0, 0)) + one
-    gate_ins = [act_in] * 4 + [((share, half), lambda i, idx: (idx[3], 0))]
+    gate_ins = [act_in] * 4 + [((share, half), lambda i, idx: (idx[3] & 1, 0))]
     gate_outs = [two_out] * 4 + [one_out] * 2 + [((share, half), lambda i, idx: (0, 0), (share, half), bf16)]
     keep_own, keep_far, own1, far1, to2, to3, piece = pl.pallas_call(
         functools.partial(gate_kernel, quarter),
@@ -236,48 +252,54 @@
         compiler_params=pltpu.CompilerParams(vmem_limit_bytes=GATE_VMEM),
         cost_estimate=pl.CostEstimate(flops=2 * block * group, bytes_accessed=16 * block * group, transcendentals=0),
     )(idx, query_proj, key_proj, value_proj, out_grad, filter_taps)
+    piece = xz(piece, 2)
     near, cross, inv = call(
         own_filter_kernel, [spec] * 2 + [((half, length), bf16)], 2, smem_first=False, cost=(6 * macs, 16 * length * quarter)
     )(table, filter_taps)
-    near, cross, inv, piece = lax.optimization_barrier((near, cross, inv, xz(piece, 2)))
-    pair = jnp.concatenate([piece, xd(piece, 1)], 0)
-    across = xd(pair, 2)
+    near, cross, inv, piece = lax.optimization_barrier((near, cross, inv, piece))
+    other_piece = xd(piece, 1)
     far1, to2, to3, own1 = xz(far1, 1), xz(to2, 2), xz(to3, 3), xz(own1, 1)
-
     okeep_far, ofar1, *far_parts = call(
         conv_far_kernel,
-        [two, two, ((rows, half), f32), ((rows, half), bf16)],
+        [two] * 2 + [((rows, half), bf16)] * 2,
         6,
-        cost=(32 * macs, 32 * length * quarter),
+        cost=(8 * macs, 32 * length * quarter),
         limit=CONV_VMEM,
         scratch=[pltpu.VMEM((length, quarter), f32), pltpu.VMEM((length, quarter), bf16), pltpu.VMEM((4, half, quarter), bf16)],
-    )(idx, table, inv, pair, across, keep_far, far1)
+    )(idx, table, inv, piece, other_piece, keep_far, far1)
     ofar1 = xz(ofar1, 1)
-    far = xz(apart(over_cores, *far_parts), 2)
-    okeep, o1, o2, o3, *own_parts = call(
+    far = apart(over_cores, *far_parts)
+    far, cross = lax.optimization_barrier((far, cross))
+    far = xz(far, 2)
+    o2, o3 = call(
+        cross_kernel, [one] * 2, 5, cost=(4 * macs, 8 * length * quarter), scratch=[pltpu.VMEM((2, half, quarter), bf16)]
+    )(idx, table, inv, cross, keep_own, own1)
+    o2, o3 = xz(o2, 2), xz(o3, 3)
+    okeep, o1, *own_parts = call(
         conv_own_kernel,
-        [two] * 2 + [one] * 2 + [((rows, length), f32), ((rows, length), bf16)],
+        [two] * 2 + [((rows, length), bf16)] * 2,
         8,
-        cost=(32 * macs, 32 * length * quarter),
+        in_hbm=2,
+        cost=(48 * macs, 32 * length * quarter),
         limit=CONV_VMEM,
-        scratch=[pltpu.VMEM((length, quarter), bf16)] * 2 + [pltpu.VMEM((6, half, quarter), bf16)],
-    )(idx, table, inv, near, cross, keep_own, own1, to2, to3)
+        scratch=[pltpu.VMEM((length, quarter), bf16)] * 2
+        + [pltpu.VMEM((5, half, quarter), bf16), pltpu.SemaphoreType.DMA((2,))],
+    )(idx, to2, to3, table, inv, near, cross, keep_own, own1)
     chip = apart(over_cores, *own_parts)
 
-    def across_chips(chip, far, o1, o2, o3):
-        chip = chip.astype(f32)
-        chip = jnp.concatenate([chip[:, :half] + far.astype(f32), chip[:, half:]], 1)
-        chip = lax.reduce_precision(chip, 8, 7).astype(bf16)
+    def across_chips(chip, far, o1):
+        low = lax.reduce_precision(chip[:, :half].astype(f32) + far.astype(f32), 8, 7).astype(bf16)
+        chip = jnp.concatenate([low, chip[:, half:]], 1)
         theirs = xd(chip, 2)
-        o1, o2, o3 = xz(o1, 1), xz(o2, 2), xz(o3, 3)
+        o1 = xz(o1, 1)
 
         def both_cores(chip, theirs):
             mine = (chip.astype(f32) + theirs.astype(f32)).astype(bf16)
             return mine, xd(mine, 1)
 
-        return o1, o2, o3, *apart(both_cores, chip, theirs)
-
-    o1, o2, o3, mine, other = apart(across_chips, chip, far, o1, o2, o3)
+        return o1, *apart(both_cores, chip, theirs)
+
+    o1, mine, other = apart(across_chips, chip, far, o1)
     act = (query_proj.shape, bf16)
     return call(
         functools.partial(final_kernel, quarter),

time: 60.1 us -> 56.4 us (0.938)
  starting transfers between devices: 20.4 us -> 16.7 us
  Pallas kernels: 13.8 us -> 15.9 us
  other arithmetic: 5.3 us -> 4.12 us
  local copies, waits for them, and re-layouts: 3.12 us -> 2.06 us
    ppermute x10, starting transfers between devices: 18.1 us -> 15 us  [xz(): return lax.ppermute(vals, 'ctx', [(i, i ^ k) for i in range(4)])]
    pallas_call x2 -> x3, Pallas kernels: 6.85 us -> 8.97 us  [the longest x1 4.23 us: half_plan(): call(conv_own_kernel, [two] * 2 + [((rows, length), bf16)] * 2, 8, in_hbm...]
    ppermute x6 -> x5, waiting for transfers between devices: 9.82 us -> 11 us  [xd(): return lax.ppermute(vals, 'dp', [(i, i ^ k) for i in range(4)])]
    unnamed x25 -> x20, local copies, waits for them, and re-layouts: 3.09 us -> 2.05 us
    add x1 -> x0, other arithmetic: 1.04 us -> none  [across_chips(): chip[:, :half] + far.astype(f32)]
    ppermute x10, waiting for transfers between devices: 6.45 us -> 5.5 us  [xz(): return lax.ppermute(vals, 'ctx', [(i, i ^ k) for i in range(4)])]
    ppermute x6 -> x5, starting transfers between devices: 2.29 us -> 1.69 us  [xd(): return lax.ppermute(vals, 'dp', [(i, i ^ k) for i in range(4)])]
    convert_element_type x4 -> x3, other arithmetic: 2.84 us -> 2.75 us  [the longest x2 1.69 us: over_cores(): return (keep.astype(f32) + xd(send, 1).astype(f32)).astype(bf16)]
  transfers between devices with their start and end apart: 16 -> 15, of which waited for: 8 -> 6; matrix products, arithmetic and copies ran while one was open for 8% -> 6% of each run, Pallas kernels for 12% -> 17%
where the time goes in v1:
time: 56.4 us; the launch traced here: 56.1 us
  starting transfers between devices  16.7 us (30%)
  waiting for transfers between devices  16.5 us (29%)
  Pallas kernels  15.9 us (28%)
  other arithmetic  4.12 us (7%)
  local copies, waits for them, and re-layouts  2.06 us (4%)
  between operations  0.75 us (1%)
    ppermute x10, starting transfers between devices, xz(): return lax.ppermute(vals, 'ctx', [(i, i ^ k) for i in range(4)])  15 us
    ppermute x5, waiting for transfers between devices, xd(): return lax.ppermute(vals, 'dp', [(i, i ^ k) for i in range(4)])  11 us
    ppermute x10, waiting for transfers between devices, xz(): return lax.ppermute(vals, 'ctx', [(i, i ^ k) for i in range(4)])  5.5 us
    pallas_call x1, Pallas kernels, half_plan(): call(conv_own_kernel, [two] * 2 + [((rows, length), bf16)] * 2, 8, in_hbm...  4.23 us
    pallas_call x1, Pallas kernels, half_plan(): pl.pallas_call(functools.partial(gate_kernel, quarter), out_shape=[jax.Sh...  3.53 us
    pallas_call x1, Pallas kernels, half_plan(): call(conv_far_kernel, [two] * 2 + [((rows, half), bf16)] * 2, 6, cost=(8...  2.82 us
    pallas_call x1, Pallas kernels, half_plan(): call(functools.partial(final_kernel, quarter), [act] * 3 + [(filter_taps....  2.81 us
    unnamed x20, local copies, waits for them, and re-layouts  2.05 us
  transfers between devices with their start and end apart: 15, of which 6 were waited for; matrix products, arithmetic and copies ran while one was open for 6% of the time, Pallas kernels for 17%

profile of v1, /device:TPU:0, one launch (start us, length us, event | category | flops | bytes accessed | tf_op | source)
XLA Modules:
  0.0 56.1 jit_solution(8562709456220786698)
XLA Ops:
  1.2 3.5 %shard_map.93 = (bf16[2,128,512]{2,1,0:T(8,128)(2,1)}, bf16[2,128,512]{2,1,0:T(8,128)(2,1)}, bf16[2,128,512]{2,1,0:T(8,128)(2,1)}, bf16[2,128,512]{2,1,0:T(8,128...) custom-call(s32[4]{0:T(128)} %pad_add_fusion.idx, bf16[1,128,2048]{2,1,0:T(8,128)(2,1)} %q.3, ...), custom_call_target="tpu_custom_call" | custom-call | flops 524288 | bytes 4194304 | tf_op jit(solution)/shard_map/pallas_call | solution.py:243
  4.8 4.0 %collective-permute-start.7 = (bf16[256,256]{1,0:T(8,128)(2,1)}, bf16[256,256]{1,0:T(8,128)(2,1)S(1)}, u32[]{:S(2)}, u32[]{:S(2)}) collective-permute-start(bf16[256,256]{1,0:T(8,128)(2,1)} %get-tuple-element.76), channel_id=1, source_target_pairs={{0,2},{1,3},{2,0},{3,1},{4,6},{5,7},{6,4},{7,5},{8,10},{9,11},{10,... | collective-permute-start | bytes 393224 | tf_op jit(solution)/shard_map/ppermute | solution.py:224
  8.8 1.6 %collective-permute-start.9 = (bf16[2,128,512]{2,1,0:T(8,128)(2,1)}, bf16[2,128,512]{2,1,0:T(8,128)(2,1)S(1)}, u32[]{:S(2)}, u32[]{:S(2)}) collective-permute-start(bf16[2,128,512]{2,1,0:T(8,128)(2,1)} %get-tuple-element.81), channel_id=1, source_target_pairs={{0,1},{1,0},{2,3},{3,2},{4,5},{5,4},{6,7},{7,6},{8,9},{9,8},{10,11... | collective-permute-start | bytes 786440 | tf_op jit(solution)/shard_map/ppermute | solution.py:224
  10.8 1.2 %copy-done = f32[512,512]{1,0:T(8,128)S(1)} copy-done((f32[512,512]{1,0:T(8,128)S(1)}, f32[512,512]{1,0:T(8,128)}, u32[]{:S(2)}) %copy-start) | copy-done | bytes 1048600
  13.5 2.0 %collective-permute-done.7.mine = bf16[256,256]{1,0:T(8,128)(2,1)S(1)} collective-permute-done((bf16[256,256]{1,0:T(8,128)(2,1)}, bf16[256,256]{1,0:T(8,128)(2,1)S(1)}, u32[]{:S(2)}, u32[]{:S(2)}) %collective-permute-start.7) | collective-permute-done | bytes 131104 | tf_op jit(solution)/shard_map/ppermute | solution.py:224
  16.3 2.7 %collective-permute-start.6 = (bf16[128,512]{1,0:T(8,128)(2,1)}, bf16[128,512]{1,0:T(8,128)(2,1)S(1)}, u32[]{:S(2)}, u32[]{:S(2)}) collective-permute-start(bf16[128,512]{1,0:T(8,128)(2,1)} %get-tuple-element.72), channel_id=1, source_target_pairs={{0,3},{1,2},{2,1},{3,0},{4,7},{5,6},{6,5},{7,4},{8,11},{9,10},{10,... | collective-permute-start | bytes 393224 | tf_op jit(solution)/shard_map/ppermute | solution.py:224
  19.0 3.5 %collective-permute-done.9.recv = bf16[2,128,512]{2,1,0:T(8,128)(2,1)S(1)} collective-permute-done((bf16[2,128,512]{2,1,0:T(8,128)(2,1)}, bf16[2,128,512]{2,1,0:T(8,128)(2,1)S(1)}, u32[]{:S(2)}, u32[]{:S(2)}) %collective-permute-start.9) | collective-permute-done | bytes 262176 | tf_op jit(solution)/shard_map/ppermute | solution.py:224
  22.5 2.8 %shard_map.95 = (bf16[2,128,512]{2,1,0:T(8,128)(2,1)S(1)}, bf16[2,128,512]{2,1,0:T(8,128)(2,1)S(1)}, bf16[256,256]{1,0:T(8,128)(2,1)S(1)}, bf16[256,256]{1,0:T(8,128)(2,1)}) custom-call(s32[4]{0:T(128)S(1)} %copy-done.6, bf16[512,512]{1,0:T(8,128)(2,1)S(1)} %copy-done.1, bf16[256,512]{1,0:T(8,128)(2,1)S(1)} %get-tuple-element.77.inv, ...), custom_call_target="tpu_custom_call" | custom-call | flops 536870912 | bytes 8388608 | tf_op jit(solution)/shard_map/pallas_call | solution.py:262
  25.3 2.2 %conditional.4 = (bf16[256,256]{1,0:T(8,128)(2,1)}) conditional(s32[]{:T(128)} %convert_element_type.44, () %tuple.38, (bf16[256,256]{1,0:T(8,128)(2,1)S(1)}, bf16[256,256]{1,0:T(8,128)(2,1)}) %tuple.39), branch_computations={%region_0.0_spmd, %region_1.0_spmd} | conditional | flops 262144 | bytes 917552 | solution.py:231
  25.3 1.6 %collective-permute-done = bf16[256,256]{1,0:T(8,128)(2,1)S(1)} collective-permute-done((bf16[256,256]{1,0:T(8,128)(2,1)}, bf16[256,256]{1,0:T(8,128)(2,1)S(1)}, u32[]{:S(2)}, u32[]{:S(2)}) %collective-permute-start) | collective-permute-done | bytes 131104 | tf_op jit(solution)/shard_map/cond/branch_1_fun/ppermute | solution.py:227
  28.0 1.9 %shard_map.97 = (bf16[128,512]{1,0:T(8,128)(2,1)}, bf16[128,512]{1,0:T(8,128)(2,1)}) custom-call(s32[4]{0:T(128)S(1)} %copy-done.6, bf16[512,512]{1,0:T(8,128)(2,1)S(1)} %copy-done.1, bf16[256,512]{1,0:T(8,128)(2,1)S(1)} %get-tuple-element.77.inv, bf16[512,512]{1,0:T(8,128)(2,1)S(1)} %get-tuple-element.85.cross, bf16[2,128,512]{2,1,0:T(8,128)(2,1)S(1)} %copy-done.5, ...), custom_call_target="tpu_custom_call" | custom-call | flops 268435456 | bytes 2097152 | tf_op jit(solution)/shard_map/pallas_call | solution.py:274
  29.9 2.5 %collective-permute-start.13 = (bf16[128,512]{1,0:T(8,128)(2,1)}, bf16[128,512]{1,0:T(8,128)(2,1)S(1)}, u32[]{:S(2)}, u32[]{:S(2)}) collective-permute-start(bf16[128,512]{1,0:T(8,128)(2,1)} %get-tuple-element.96), channel_id=1, source_target_pairs={{0,2},{1,3},{2,0},{3,1},{4,6},{5,7},{6,4},{7,5},{8,10},{9,11},{10,... | collective-permute-start | bytes 393224 | tf_op jit(solution)/shard_map/ppermute | solution.py:224
  32.4 1.5 %collective-permute-start.14 = (bf16[128,512]{1,0:T(8,128)(2,1)}, bf16[128,512]{1,0:T(8,128)(2,1)S(1)}, u32[]{:S(2)}, u32[]{:S(2)}) collective-permute-start(bf16[128,512]{1,0:T(8,128)(2,1)} %get-tuple-element.97), channel_id=1, source_target_pairs={{0,3},{1,2},{2,1},{3,0},{4,7},{5,6},{6,5},{7,4},{8,11},{9,10},{10,... | collective-permute-start | bytes 393224 | tf_op jit(solution)/shard_map/ppermute | solution.py:224
  33.9 4.2 %shard_map.96 = (bf16[2,128,512]{2,1,0:T(8,128)(2,1)S(1)}, bf16[2,128,512]{2,1,0:T(8,128)(2,1)}, bf16[256,512]{1,0:T(8,128)(2,1)}, bf16[256,512]{1,0:T(8,128)(2,1)}) custom-call(s32[4]{0:T(128)S(1)} %copy-done.6, bf16[128,512]{1,0:T(8,128)(2,1)S(1)} %collective-permute-done.5.r2, bf16[128,512]{1,0:T(8,128)(2,1)S(1)} %collective-permute-done.6.r3, ...), custom_call_target="tpu_custom_call" | custom-call | flops 3221225472 | bytes 8388608 | tf_op jit(solution)/shard_map/pallas_call | solution.py:278
  38.2 2.8 %conditional.5 = (bf16[256,512]{1,0:T(8,128)(2,1)S(1)}) conditional(s32[]{:T(128)} %convert_element_type.44, () %tuple.42, (bf16[256,512]{1,0:T(8,128)(2,1)}, bf16[256,512]{1,0:T(8,128)(2,1)}) %tuple.43), branch_computations={%region_2.0_spmd, %region_3.0_spmd} | conditional | flops 524288 | bytes 1835056 | solution.py:231
  38.3 1.7 %collective-permute-done.1 = bf16[256,512]{1,0:T(8,128)(2,1)S(1)} collective-permute-done((bf16[256,512]{1,0:T(8,128)(2,1)}, bf16[256,512]{1,0:T(8,128)(2,1)S(1)}, u32[]{:S(2)}, u32[]{:S(2)}) %collective-permute-start.1) | collective-permute-done | bytes 262176 | tf_op jit(solution)/shard_map/cond/branch_1_fun/ppermute | solution.py:227
  40.0 1.0 %add_convert_fusion.1 = bf16[256,512]{1,0:T(8,128)(2,1)S(1)} fusion(bf16[256,512]{1,0:T(8,128)(2,1)S(1)} %collective-permute-done.1, bf16[256,512]{1,0:T(8,128)(2,1)} %get-tuple-element.28), kind=kLoop, calls=%fused_computation.1 | loop fusion | flops 524288 | bytes 786432 | tf_op jit(solution)/shard_map/cond/branch_1_fun/convert_element_type | solution.py:234
  41.1 12.2 %conditional.6 = (bf16[2,128,512]{2,1,0:T(8,128)(2,1)}, bf16[256,512]{1,0:T(8,128)(2,1)}, bf16[256,512]{1,0:T(8,128)(2,1)}) conditional(s32[]{:T(128)} %convert_element_type.44, () %tuple.41, (bf16[2,128,512]{2,1,0:T(8,128)(2,1)}, s32[]{:T(128)}, bf16[256,512]{1,0:T(8,128)(2,1)S(1)}, bf16[256,256]{1,0:T(8,128)(2,1)}) %tuple.44), branch_computations={%region_4.0_spmd, %region_5.0_spmd} | conditional | flops 1376258 | bytes 5111998 | solution.py:231
  41.1 1.1 %reduce-precision_convert_fusion = bf16[256,256]{1,0:T(8,128)(2,1)S(1)} fusion(bf16[256,256]{1,0:T(8,128)(2,1)} %get-tuple-element.35, bf16[256,512]{1,0:T(8,128)(2,1)S(1)} %get-tuple-element.34), kind=kLoop, calls=%fused_computation.4 | loop fusion | flops 327680 | bytes 393216 | tf_op jit(solution)/shard_map/cond/branch_1_fun/convert_element_type | solution.py:291
  42.2 1.6 %collective-permute-start.4 = (bf16[256,512]{1,0:T(8,128)(2,1)S(1)}, bf16[256,512]{1,0:T(8,128)(2,1)S(1)}, u32[]{:S(2)}, u32[]{:S(2)}) collective-permute-start(bf16[256,512]{1,0:T(8,128)(2,1)S(1)} %pad_maximum_fusion), channel_id=1, source_target_pairs={{0,16},{8,24},{16,0},{24,8},{1,17},{9,25},{17,1},{25,9},{2,18},{10... | collective-permute-start | bytes 786440 | tf_op jit(solution)/shard_map/cond/branch_1_fun/ppermute | solution.py:227
  44.7 5.9 %collective-permute-done.4 = bf16[256,512]{1,0:T(8,128)(2,1)S(1)} collective-permute-done((bf16[256,512]{1,0:T(8,128)(2,1)S(1)}, bf16[256,512]{1,0:T(8,128)(2,1)S(1)}, u32[]{:S(2)}, u32[]{:S(2)}) %collective-permute-start.4) | collective-permute-done | bytes 262176 | tf_op jit(solution)/shard_map/cond/branch_1_fun/ppermute | solution.py:227
  50.6 2.6 %conditional = (bf16[256,512]{1,0:T(8,128)(2,1)}, bf16[256,512]{1,0:T(8,128)(2,1)}) conditional(s32[]{:T(128)} %convert_element_type.39, () %tuple.25, (bf16[256,512]{1,0:T(8,128)(2,1)S(1)}, bf16[256,512]{1,0:T(8,128)(2,1)S(1)}) %tuple.26), branch_computations={%region_6.0_spmd, %region_7.0_spmd} | conditional | flops 524288 | bytes 1835064 | solution.py:231
  51.3 1.9 %collective-permute-done.2 = bf16[256,512]{1,0:T(8,128)(2,1)} collective-permute-done((bf16[256,512]{1,0:T(8,128)(2,1)}, bf16[256,512]{1,0:T(8,128)(2,1)}, u32[]{:S(2)}, u32[]{:S(2)}) %collective-permute-start.2) | collective-permute-done | bytes 262176 | tf_op jit(solution)/shard_map/cond/branch_1_fun/cond/branch_1_fun/ppermute | solution.py:227
  53.3 2.8 %shard_map.98 = (bf16[1,128,2048]{2,1,0:T(8,128)(2,1)}, bf16[1,128,2048]{2,1,0:T(8,128)(2,1)}, bf16[1,128,2048]{2,1,0:T(8,128)(2,1)}, f32[512,512]{1,0:T(8,128)}) custom-call(s32[4]{0:T(128)S(1)} %copy-done.6, bf16[1,128,2048]{2,1,0:T(8,128)(2,1)S(1)} %copy-done.2, bf16[1,128,2048]{2,1,0:T(8,128)(2,1)S(1)} %copy-done.3, bf16[1,128,2048]{2,1,0:T(8,128)(2,1)S(1)} %copy-done.4, ...), custom_call_target="tpu_custom_call" | custom-call | flops 786432 | bytes 4718592 | tf_op jit(solution)/shard_map/pallas_call | solution.py:304
  (43 shorter events, 6.3 us)
Async XLA Ops:
  1.2 9.6 %copy-start.1 = (bf16[512,512]{1,0:T(8,128)(2,1)S(1)}, bf16[512,512]{1,0:T(8,128)(2,1)}, u32[]{:S(2)}) copy-start(bf16[512,512]{1,0:T(8,128)(2,1)} %constant.24.clone.table) | copy-start | bytes 1572868
  4.8 10.7 %collective-permute-start.7 = (bf16[256,256]{1,0:T(8,128)(2,1)}, bf16[256,256]{1,0:T(8,128)(2,1)S(1)}, u32[]{:S(2)}, u32[]{:S(2)}) collective-permute-start(bf16[256,256]{1,0:T(8,128)(2,1)} %get-tuple-element.76), channel_id=1, source_target_pairs={{0,2},{1,3},{2,0},{3,1},{4,6},{5,7},{6,4},{7,5},{8,10},{9,11},{10,... | collective-permute-start | bytes 393224 | tf_op jit(solution)/shard_map/ppermute | solution.py:224
  8.8 13.7 %collective-permute-start.9 = (bf16[2,128,512]{2,1,0:T(8,128)(2,1)}, bf16[2,128,512]{2,1,0:T(8,128)(2,1)S(1)}, u32[]{:S(2)}, u32[]{:S(2)}) collective-permute-start(bf16[2,128,512]{2,1,0:T(8,128)(2,1)} %get-tuple-element.81), channel_id=1, source_target_pairs={{0,1},{1,0},{2,3},{3,2},{4,5},{5,4},{6,7},{7,6},{8,9},{9,8},{10,11... | collective-permute-start | bytes 786440 | tf_op jit(solution)/shard_map/ppermute | solution.py:224
  10.4 17.6 %collective-permute-start.10 = (bf16[2,128,512]{2,1,0:T(8,128)(2,1)}, bf16[2,128,512]{2,1,0:T(8,128)(2,1)S(1)}, u32[]{:S(2)}, u32[]{:S(2)}) collective-permute-start(bf16[2,128,512]{2,1,0:T(8,128)(2,1)} %get-tuple-element.87), channel_id=1, source_target_pairs={{0,1},{1,0},{2,3},{3,2},{4,5},{5,4},{6,7},{7,6},{8,9},{9,8},{10,11... | collective-permute-start | bytes 786440 | tf_op jit(solution)/shard_map/ppermute | solution.py:224
  10.8 1.2 %copy-start = (f32[512,512]{1,0:T(8,128)S(1)}, f32[512,512]{1,0:T(8,128)}, u32[]{:S(2)}) copy-start(f32[512,512]{1,0:T(8,128)} %taps.3) | copy-start | bytes 3145732
  12.0 10.4 %copy-start.9 = (bf16[2,128,512]{2,1,0:T(8,128)(2,1)S(1)}, bf16[2,128,512]{2,1,0:T(8,128)(2,1)}, u32[]{:S(2)}) copy-start(bf16[2,128,512]{2,1,0:T(8,128)(2,1)} %get-tuple-element.80.keep) | copy-start | bytes 786436
  15.4 3.5 %collective-permute-start.8 = (bf16[256,256]{1,0:T(8,128)(2,1)S(1)}, bf16[256,256]{1,0:T(8,128)(2,1)S(1)}, u32[]{:S(2)}, u32[]{:S(2)}) collective-permute-start(bf16[256,256]{1,0:T(8,128)(2,1)S(1)} %collective-permute-done.7.mine), channel_id=1, source_target_pairs={{0,8},{8,0},{16,24},{24,16},{1,9},{9,1},{17,25},{25,17},{2,10},{10... | collective-permute-start | bytes 393224 | tf_op jit(solution)/shard_map/ppermute | solution.py:227
  15.4 17.0 %collective-permute-start.5 = (bf16[128,512]{1,0:T(8,128)(2,1)}, bf16[128,512]{1,0:T(8,128)(2,1)S(1)}, u32[]{:S(2)}, u32[]{:S(2)}) collective-permute-start(bf16[128,512]{1,0:T(8,128)(2,1)} %get-tuple-element.71), channel_id=1, source_target_pairs={{0,2},{1,3},{2,0},{3,1},{4,6},{5,7},{6,4},{7,5},{8,10},{9,11},{10,... | collective-permute-start | bytes 393224 | tf_op jit(solution)/shard_map/ppermute | solution.py:224
  16.3 17.6 %collective-permute-start.6 = (bf16[128,512]{1,0:T(8,128)(2,1)}, bf16[128,512]{1,0:T(8,128)(2,1)S(1)}, u32[]{:S(2)}, u32[]{:S(2)}) collective-permute-start(bf16[128,512]{1,0:T(8,128)(2,1)} %get-tuple-element.72), channel_id=1, source_target_pairs={{0,3},{1,2},{2,1},{3,0},{4,7},{5,6},{6,5},{7,4},{8,11},{9,10},{10,... | collective-permute-start | bytes 393224 | tf_op jit(solution)/shard_map/ppermute | solution.py:224
  19.0 3.5 %copy-start.6 = (s32[4]{0:T(128)S(1)}, s32[4]{0:T(128)}, u32[]{:S(2)}) copy-start(s32[4]{0:T(128)} %pad_add_fusion.idx) | copy-start | bytes 52
  25.3 2.7 %copy-start.5 = (bf16[2,128,512]{2,1,0:T(8,128)(2,1)S(1)}, bf16[2,128,512]{2,1,0:T(8,128)(2,1)}, u32[]{:S(2)}) copy-start(bf16[2,128,512]{2,1,0:T(8,128)(2,1)} %get-tuple-element.86.keep) | copy-start | bytes 786436
  25.3 1.6 %collective-permute-start = (bf16[256,256]{1,0:T(8,128)(2,1)}, bf16[256,256]{1,0:T(8,128)(2,1)S(1)}, u32[]{:S(2)}, u32[]{:S(2)}) collective-permute-start(bf16[256,256]{1,0:T(8,128)(2,1)} %get-tuple-element.21), channel_id=1, source_target_pairs={{0,8},{8,0},{16,24},{24,16},{1,9},{9,1},{17,25},{25,17},{2,10},{10... | collective-permute-start | bytes 393224 | tf_op jit(solution)/shard_map/cond/branch_1_fun/ppermute | solution.py:227
  27.6 13.5 %collective-permute-start.11 = (bf16[256,256]{1,0:T(8,128)(2,1)}, bf16[256,256]{1,0:T(8,128)(2,1)}, u32[]{:S(2)}, u32[]{:S(2)}) collective-permute-start(bf16[256,256]{1,0:T(8,128)(2,1)} %get-tuple-element.110), channel_id=1, source_target_pairs={{0,2},{1,3},{2,0},{3,1},{4,6},{5,7},{6,4},{7,5},{8,10},{9,11},{10,... | collective-permute-start | bytes 393224 | tf_op jit(solution)/shard_map/ppermute | solution.py:224
  27.6 25.7 %collective-permute-start.12 = (bf16[2,128,512]{2,1,0:T(8,128)(2,1)S(1)}, bf16[2,128,512]{2,1,0:T(8,128)(2,1)S(1)}, u32[]{:S(2)}, u32[]{:S(2)}) collective-permute-start(bf16[2,128,512]{2,1,0:T(8,128)(2,1)S(1)} %get-tuple-element.95), channel_id=1, source_target_pairs={{0,1},{1,0},{2,3},{3,2},{4,5},{5,4},{6,7},{7,6},{8,9},{9,8},{10,11... | collective-permute-start | bytes 786440 | tf_op jit(solution)/shard_map/ppermute | solution.py:224
  28.0 6.0 %copy-start.8 = (bf16[512,512]{1,0:T(8,128)(2,1)S(1)}, bf16[512,512]{1,0:T(8,128)(2,1)}, u32[]{:S(2)}) copy-start(bf16[512,512]{1,0:T(8,128)(2,1)} %copy-done.7) | copy-start | bytes 1572868
  29.9 23.3 %collective-permute-start.13 = (bf16[128,512]{1,0:T(8,128)(2,1)}, bf16[128,512]{1,0:T(8,128)(2,1)S(1)}, u32[]{:S(2)}, u32[]{:S(2)}) collective-permute-start(bf16[128,512]{1,0:T(8,128)(2,1)} %get-tuple-element.96), channel_id=1, source_target_pairs={{0,2},{1,3},{2,0},{3,1},{4,6},{5,7},{6,4},{7,5},{8,10},{9,11},{10,... | collective-permute-start | bytes 393224 | tf_op jit(solution)/shard_map/ppermute | solution.py:224
  32.4 20.8 %collective-permute-start.14 = (bf16[128,512]{1,0:T(8,128)(2,1)}, bf16[128,512]{1,0:T(8,128)(2,1)S(1)}, u32[]{:S(2)}, u32[]{:S(2)}) collective-permute-start(bf16[128,512]{1,0:T(8,128)(2,1)} %get-tuple-element.97), channel_id=1, source_target_pairs={{0,3},{1,2},{2,1},{3,0},{4,7},{5,6},{6,5},{7,4},{8,11},{9,10},{10,... | collective-permute-start | bytes 393224 | tf_op jit(solution)/shard_map/ppermute | solution.py:224
  38.2 1.8 %collective-permute-start.1 = (bf16[256,512]{1,0:T(8,128)(2,1)}, bf16[256,512]{1,0:T(8,128)(2,1)S(1)}, u32[]{:S(2)}, u32[]{:S(2)}) collective-permute-start(bf16[256,512]{1,0:T(8,128)(2,1)} %get-tuple-element.29), channel_id=1, source_target_pairs={{0,8},{8,0},{16,24},{24,16},{1,9},{9,1},{17,25},{25,17},{2,10},{10... | collective-permute-start | bytes 786440 | tf_op jit(solution)/shard_map/cond/branch_1_fun/ppermute | solution.py:227
  41.0 12.2 %copy-start.2 = (bf16[1,128,2048]{2,1,0:T(8,128)(2,1)S(1)}, bf16[1,128,2048]{2,1,0:T(8,128)(2,1)}, u32[]{:S(2)}) copy-start(bf16[1,128,2048]{2,1,0:T(8,128)(2,1)} %q.3) | copy-start | bytes 1572868
  41.0 12.2 %copy-start.3 = (bf16[1,128,2048]{2,1,0:T(8,128)(2,1)S(1)}, bf16[1,128,2048]{2,1,0:T(8,128)(2,1)}, u32[]{:S(2)}) copy-start(bf16[1,128,2048]{2,1,0:T(8,128)(2,1)} %k.3) | copy-start | bytes 1572868
  41.0 12.2 %copy-start.4 = (bf16[1,128,2048]{2,1,0:T(8,128)(2,1)S(1)}, bf16[1,128,2048]{2,1,0:T(8,128)(2,1)}, u32[]{:S(2)}) copy-start(bf16[1,128,2048]{2,1,0:T(8,128)(2,1)} %g.3) | copy-start | bytes 1572868
  42.2 8.4 %collective-permute-start.4 = (bf16[256,512]{1,0:T(8,128)(2,1)S(1)}, bf16[256,512]{1,0:T(8,128)(2,1)S(1)}, u32[]{:S(2)}, u32[]{:S(2)}) collective-permute-start(bf16[256,512]{1,0:T(8,128)(2,1)S(1)} %pad_maximum_fusion), channel_id=1, source_target_pairs={{0,16},{8,24},{16,0},{24,8},{1,17},{9,25},{17,1},{25,9},{2,18},{10... | collective-permute-start | bytes 786440 | tf_op jit(solution)/shard_map/cond/branch_1_fun/ppermute | solution.py:227
  43.8 9.4 %collective-permute-start.3 = (bf16[2,128,512]{2,1,0:T(8,128)(2,1)}, bf16[2,128,512]{2,1,0:T(8,128)(2,1)}, u32[]{:S(2)}, u32[]{:S(2)}) collective-permute-start(bf16[2,128,512]{2,1,0:T(8,128)(2,1)} %get-tuple-element.32), channel_id=1, source_target_pairs={{0,1},{1,0},{2,3},{3,2},{4,5},{5,4},{6,7},{7,6},{8,9},{9,8},{10,11... | collective-permute-start | bytes 786440 | tf_op jit(solution)/shard_map/cond/branch_1_fun/ppermute | solution.py:224
  51.3 1.9 %collective-permute-start.2 = (bf16[256,512]{1,0:T(8,128)(2,1)}, bf16[256,512]{1,0:T(8,128)(2,1)}, u32[]{:S(2)}, u32[]{:S(2)}) collective-permute-start(bf16[256,512]{1,0:T(8,128)(2,1)} %add_convert_fusion.2), channel_id=1, source_target_pairs={{0,8},{8,0},{16,24},{24,16},{1,9},{9,1},{17,25},{25,17},{2,10},{10... | collective-permute-start | bytes 786440 | tf_op jit(solution)/shard_map/cond/branch_1_fun/cond/branch_1_fun/ppermute | solution.py:227
  (1 other events, 0.8 us)

commit v2 on v1

--- a/solution.py
+++ b/solution.py
@@ -141,43 +141,68 @@
     halves(low, mm(inv[...], join(pair).astype(bf16)).astype(bf16), held.at[1], o2, o3)
 
 
-def conv_own_kernel(idx, r2, r3, table, inv, near, cross, keep, recv, okeep, o1, gkeep, gsend, q_near, q_cross, held, sems):
-    low, upper, core = idx[1], idx[2], idx[3] & 1
-    half = table.shape[1] // 2
+def load_blocks(low, r2, r3, held, sems):
     block = r2.shape[0]
     loads = []
     for j, (src, place) in enumerate(((r2, low), (r3, 1 - low))):
         at = pl.ds(pl.multiple_of(place * block, block), block)
-        loads.append(pltpu.make_async_copy(src, held.at[2, at], sems.at[j]))
+        loads.append(pltpu.make_async_copy(src, held.at[at], sems.at[j]))
         loads[j].start()
-
-    def inverse(pair):
-        return mm(inv[...], join(pair).astype(bf16)).astype(bf16)
-
-    def run(is_upper):
-        fwd = table[:, half:]
-        x = mm(fwd, in_order(low, keep[0], recv[0], held.at[0]))
-        g = mm(fwd, in_order(low, keep[1], recv[1], held.at[1]))
-        for load in loads:
-            load.wait()
-        rec = mm(fwd, held[2])
-        hx = cross[...].astype(f32)
-        add = cmul(hx, rec) if is_upper else cmulc(hx, rec)
-        h = near[...].astype(f32)
-        conv = cmul(x, h)
-        back = cmulc(h, g)
-        if is_upper:
-            conv = (conv[0] + add[0], conv[1] + add[1])
-        else:
-            back = (back[0] + add[0], back[1] + add[1])
-        halves(low, inverse(conv), held.at[3], okeep.at[0], o1.at[0])
-        halves(low, inverse(back), held.at[4], okeep.at[1], o1.at[1])
-        q_near[...] = join(cmulc(x, g)).astype(bf16)
-        q_cross[...] = join(cmulc(rec, g) if is_upper else cmulc(x, rec)).astype(bf16)
-
-    pl.when(upper == 0)(functools.partial(run, False))
-    pl.when(upper != 0)(functools.partial(run, True))
+    return loads
+
+
+def own_filter_grad_kernel(idx, r2, r3, table, keep, recv, gkeep, gsend, q_near, q_cross, held, sems):
+    low, upper, core = idx[1], idx[2], idx[3] & 1
+    half = table.shape[1] // 2
+    loads = load_blocks(low, r2, r3, held.at[2], sems)
+    fwd = table[:, half:]
+    x = mm(fwd, in_order(low, keep[0], recv[0], held.at[0]))
+    g = mm(fwd, in_order(low, keep[1], recv[1], held.at[1]))
+    q_near[...] = join(cmulc(x, g)).astype(bf16)
+    for load in loads:
+        load.wait()
+    rec = mm(fwd, held[2])
+
+    def lower():
+        q_cross[...] = join(cmulc(x, rec)).astype(bf16)
+
+    def higher():
+        q_cross[...] = join(cmulc(rec, g)).astype(bf16)
+
+    pl.when(upper == 0)(lower)
+    pl.when(upper != 0)(higher)
     filt_part(core, table, [(0, [(q_cross, 0), (q_near, half)]), (half, [(q_cross, half)])], gkeep, gsend)
+
+
+def conv_own_kernel(idx, r2, r3, table, inv, near, cross, keep, recv, okeep, o1, held, sems):
+    low, upper = idx[1], idx[2]
+    half = table.shape[1] // 2
+    loads = load_blocks(low, r2, r3, held.at[2], sems)
+    fwd = table[:, half:]
+    x = mm(fwd, in_order(low, keep[0], recv[0], held.at[0]))
+    g = mm(fwd, in_order(low, keep[1], recv[1], held.at[1]))
+    h = near[...].astype(f32)
+    hx = cross[...].astype(f32)
+    for load in loads:
+        load.wait()
+    rec = mm(fwd, held[2])
+
+    def put(kind, pair):
+        vals = mm(inv[...], join(pair).astype(bf16)).astype(bf16)
+        halves(low, vals, held.at[3 + kind], okeep.at[kind], o1.at[kind])
+
+    def lower():
+        put(0, cmul(x, h))
+        back, add = cmulc(h, g), cmulc(hx, rec)
+        put(1, (back[0] + add[0], back[1] + add[1]))
+
+    def higher():
+        conv, add = cmul(x, h), cmul(hx, rec)
+        put(0, (conv[0] + add[0], conv[1] + add[1]))
+        put(1, cmulc(h, g))
+
+    pl.when(upper == 0)(lower)
+    pl.when(upper != 0)(higher)
 
 
 def final_kernel(quarter, idx, q, k, g, own, far, own1, far1, r2, r3, mine, other, dq, dk, dv, grad_filt, held, filt_held, sems):
@@ -275,31 +300,42 @@
         cross_kernel, [one] * 2, 5, cost=(4 * macs, 8 * length * quarter), scratch=[pltpu.VMEM((2, half, quarter), bf16)]
     )(idx, table, inv, cross, keep_own, own1)
     o2, o3 = xz(o2, 2), xz(o3, 3)
-    okeep, o1, *own_parts = call(
-        conv_own_kernel,
-        [two] * 2 + [((rows, length), bf16)] * 2,
-        8,
+    own_parts = call(
+        own_filter_grad_kernel,
+        [((rows, length), bf16)] * 2,
+        5,
         in_hbm=2,
         cost=(48 * macs, 32 * length * quarter),
         limit=CONV_VMEM,
         scratch=[pltpu.VMEM((length, quarter), bf16)] * 2
-        + [pltpu.VMEM((5, half, quarter), bf16), pltpu.SemaphoreType.DMA((2,))],
-    )(idx, to2, to3, table, inv, near, cross, keep_own, own1)
-    chip = apart(over_cores, *own_parts)
-
-    def across_chips(chip, far, o1):
-        low = lax.reduce_precision(chip[:, :half].astype(f32) + far.astype(f32), 8, 7).astype(bf16)
-        chip = jnp.concatenate([low, chip[:, half:]], 1)
+        + [pltpu.VMEM((3, half, quarter), bf16), pltpu.SemaphoreType.DMA((2,))],
+    )(idx, to2, to3, table, keep_own, own1)
+
+    def own_quarter(own_parts, far, idx, *conv_ins):
+        chip = own_parts[0].astype(f32) + xd(own_parts[1], 1).astype(f32)
+        chip = jnp.concatenate([chip[:, :half] + far.astype(f32), chip[:, half:]], 1)
+        chip = lax.reduce_precision(chip, 8, 7).astype(bf16)
         theirs = xd(chip, 2)
+        okeep, o1 = call(
+            conv_own_kernel,
+            [two] * 2,
+            8,
+            in_hbm=2,
+            cost=(4 * macs, 4 * length * quarter),
+            limit=CONV_VMEM,
+            scratch=[pltpu.VMEM((5, half, quarter), bf16), pltpu.SemaphoreType.DMA((2,))],
+        )(idx, *conv_ins)
         o1 = xz(o1, 1)
 
         def both_cores(chip, theirs):
             mine = (chip.astype(f32) + theirs.astype(f32)).astype(bf16)
             return mine, xd(mine, 1)
 
-        return o1, *apart(both_cores, chip, theirs)
-
-    o1, mine, other = apart(across_chips, chip, far, o1)
+        return okeep, o1, *apart(both_cores, chip, theirs)
+
+    okeep, o1, mine, other = apart(
+        own_quarter, own_parts, far, idx, to2, to3, table, inv, near, cross, keep_own, own1
+    )
     act = (query_proj.shape, bf16)
     return call(
         functools.partial(final_kernel, quarter),

time: 56.4 us -> 54.8 us (0.972)
  waiting for transfers between devices: 16.5 us -> 14.4 us
  Pallas kernels: 15.9 us -> 17.9 us
  local copies, waits for them, and re-layouts: 2.06 us -> 1.3 us
  other arithmetic: 4.12 us -> 3.52 us
    ppermute x5, waiting for transfers between devices: 11 us -> 7.66 us  [xd(): return lax.ppermute(vals, 'dp', [(i, i ^ k) for i in range(4)])]
    pallas_call x1 -> x2, Pallas kernels: 4.23 us -> 6.25 us  [the longest x1 3.51 us: own_quarter(): call(conv_own_kernel, [two] * 2, 8, in_hbm=2, cost=(4 * macs, 4 * length...]
    ppermute x10, waiting for transfers between devices: 5.5 us -> 6.75 us  [xz(): return lax.ppermute(vals, 'ctx', [(i, i ^ k) for i in range(4)])]
    convert_element_type x1, other arithmetic: 1.05 us -> 0.03 us  [own_quarter(): chip = lax.reduce_precision(chip, 8, 7).astype(bf16)]
    convert_element_type x1, other arithmetic: 0.77 us -> 1.72 us  [both_cores(): mine = (chip.astype(f32) + theirs.astype(f32)).astype(bf16)]
    pallas_call x1, Pallas kernels: 0.61 us -> 1.4 us  [half_plan(): call(own_filter_kernel, [spec] * 2 + [((half, length), bf16)], 2, smem_fi...]
    unnamed x20 -> x28, local copies, waits for them, and re-layouts: 2.05 us -> 1.28 us
    pallas_call x1, Pallas kernels: 1.93 us -> 1.23 us  [half_plan(): call(cross_kernel, [one] * 2, 5, cost=(4 * macs, 8 * length * quarter), s...]
  transfers between devices with their start and end apart: 15 -> 15, of which waited for: 6 -> 7; matrix products, arithmetic and copies ran while one was open for 6% -> 6% of each run, Pallas kernels for 17% -> 21%
where the time goes in v2:
time: 54.8 us; the launch traced here: 54.5 us
  Pallas kernels  17.9 us (33%)
  starting transfers between devices  16.5 us (30%)
  waiting for transfers between devices  14.4 us (26%)
  other arithmetic  3.52 us (6%)
  local copies, waits for them, and re-layouts  1.3 us (2%)
  between operations  0.79 us (1%)
    ppermute x10, starting transfers between devices, xz(): return lax.ppermute(vals, 'ctx', [(i, i ^ k) for i in range(4)])  14.9 us
    ppermute x5, waiting for transfers between devices, xd(): return lax.ppermute(vals, 'dp', [(i, i ^ k) for i in range(4)])  7.66 us
    ppermute x10, waiting for transfers between devices, xz(): return lax.ppermute(vals, 'ctx', [(i, i ^ k) for i in range(4)])  6.75 us
    pallas_call x1, Pallas kernels, own_quarter(): call(conv_own_kernel, [two] * 2, 8, in_hbm=2, cost=(4 * macs, 4 * length...  3.51 us
    pallas_call x1, Pallas kernels, half_plan(): pl.pallas_call(functools.partial(gate_kernel, quarter), out_shape=[jax.Sh...  3.25 us
    pallas_call x1, Pallas kernels, half_plan(): call(functools.partial(final_kernel, quarter), [act] * 3 + [(filter_taps....  2.89 us
    pallas_call x1, Pallas kernels, half_plan(): call(conv_far_kernel, [two] * 2 + [((rows, half), bf16)] * 2, 6, cost=(8...  2.83 us
    pallas_call x1, Pallas kernels, half_plan(): call(own_filter_grad_kernel, [((rows, length), bf16)] * 2, 5, in_hbm=2, c...  2.74 us
  transfers between devices with their start and end apart: 15, of which 7 were waited for; matrix products, arithmetic and copies ran while one was open for 6% of the time, Pallas kernels for 21%

profile of v2, /device:TPU:0, one launch (start us, length us, event | category | flops | bytes accessed | tf_op | source)
XLA Modules:
  0.0 54.5 jit_solution(11926131705479339621)
XLA Ops:
  0.7 3.2 %shard_map.93 = (bf16[2,128,512]{2,1,0:T(8,128)(2,1)S(1)}, bf16[2,128,512]{2,1,0:T(8,128)(2,1)}, bf16[2,128,512]{2,1,0:T(8,128)(2,1)}, bf16[2,128,512]{2,1,0:T(8...) custom-call(s32[4]{0:T(128)S(1)} %pad_add_fusion.idx, ...), custom_call_target="tpu_custom_call" | custom-call | flops 524288 | bytes 4194304 | tf_op jit(solution)/shard_map/pallas_call | solution.py:268
  4.0 4.0 %collective-permute-start.7 = (bf16[256,256]{1,0:T(8,128)(2,1)}, bf16[256,256]{1,0:T(8,128)(2,1)S(1)}, u32[]{:S(2)}, u32[]{:S(2)}) collective-permute-start(bf16[256,256]{1,0:T(8,128)(2,1)} %get-tuple-element.95), channel_id=1, source_target_pairs={{0,2},{1,3},{2,0},{3,1},{4,6},{5,7},{6,4},{7,5},{8,10},{9,11},{10,... | collective-permute-start | bytes 393224 | tf_op jit(solution)/shard_map/ppermute | solution.py:249
  8.0 1.6 %collective-permute-start.9 = (bf16[2,128,512]{2,1,0:T(8,128)(2,1)}, bf16[2,128,512]{2,1,0:T(8,128)(2,1)S(1)}, u32[]{:S(2)}, u32[]{:S(2)}) collective-permute-start(bf16[2,128,512]{2,1,0:T(8,128)(2,1)} %get-tuple-element.100), channel_id=1, source_target_pairs={{0,1},{1,0},{2,3},{3,2},{4,5},{5,4},{6,7},{7,6},{8,9},{9,8},{10,11... | collective-permute-start | bytes 786440 | tf_op jit(solution)/shard_map/ppermute | solution.py:249
  11.3 1.4 %shard_map.94 = (bf16[512,512]{1,0:T(8,128)(2,1)}, bf16[512,512]{1,0:T(8,128)(2,1)S(1)}, bf16[256,512]{1,0:T(8,128)(2,1)S(1)}) custom-call(bf16[512,512]{1,0:T(8,128)(2,1)S(1)} %copy-done.5, f32[512,512]{1,0:T(8,128)S(1)} %copy-done), custom_call_target="tpu_custom_call" | custom-call | flops 402653184 | bytes 4194304 | tf_op jit(solution)/shard_map/pallas_call | solution.py:281
  12.7 2.0 %collective-permute-done.7.mine = bf16[256,256]{1,0:T(8,128)(2,1)S(1)} collective-permute-done((bf16[256,256]{1,0:T(8,128)(2,1)}, bf16[256,256]{1,0:T(8,128)(2,1)S(1)}, u32[]{:S(2)}, u32[]{:S(2)}) %collective-permute-start.7) | collective-permute-done | bytes 131104 | tf_op jit(solution)/shard_map/ppermute | solution.py:249
  15.5 2.7 %collective-permute-start.6 = (bf16[128,512]{1,0:T(8,128)(2,1)}, bf16[128,512]{1,0:T(8,128)(2,1)}, u32[]{:S(2)}, u32[]{:S(2)}) collective-permute-start(bf16[128,512]{1,0:T(8,128)(2,1)} %get-tuple-element.91), channel_id=1, source_target_pairs={{0,3},{1,2},{2,1},{3,0},{4,7},{5,6},{6,5},{7,4},{8,11},{9,10},{10,... | collective-permute-start | bytes 393224 | tf_op jit(solution)/shard_map/ppermute | solution.py:249
  18.2 3.5 %collective-permute-done.9.recv = bf16[2,128,512]{2,1,0:T(8,128)(2,1)S(1)} collective-permute-done((bf16[2,128,512]{2,1,0:T(8,128)(2,1)}, bf16[2,128,512]{2,1,0:T(8,128)(2,1)S(1)}, u32[]{:S(2)}, u32[]{:S(2)}) %collective-permute-start.9) | collective-permute-done | bytes 262176 | tf_op jit(solution)/shard_map/ppermute | solution.py:249
  21.7 2.8 %shard_map.95 = (bf16[2,128,512]{2,1,0:T(8,128)(2,1)S(1)}, bf16[2,128,512]{2,1,0:T(8,128)(2,1)S(1)}, bf16[256,256]{1,0:T(8,128)(2,1)}, bf16[256,256]{1,0:T(8,128)(2,1)}) custom-call(s32[4]{0:T(128)S(1)} %pad_add_fusion.idx, bf16[512,512]{1,0:T(8,128)(2,1)S(1)} %copy-done.5, bf16[256,512]{1,0:T(8,128)(2,1)S(1)} %get-tuple-element.96.inv, ...), custom_call_target="tpu_custom_call" | custom-call | flops 536870912 | bytes 8388608 | tf_op jit(solution)/shard_map/pallas_call | solution.py:287
  24.5 3.1 %conditional.3 = (bf16[256,256]{1,0:T(8,128)(2,1)}) conditional(s32[]{:T(128)} %convert_element_type.37, () %tuple.33, (bf16[256,256]{1,0:T(8,128)(2,1)}, bf16[256,256]{1,0:T(8,128)(2,1)}) %tuple.34), branch_computations={%region_0.0_spmd, %region_1.0_spmd} | conditional | flops 262144 | bytes 917552 | solution.py:256
  24.5 1.6 %collective-permute-done = bf16[256,256]{1,0:T(8,128)(2,1)S(1)} collective-permute-done((bf16[256,256]{1,0:T(8,128)(2,1)}, bf16[256,256]{1,0:T(8,128)(2,1)S(1)}, u32[]{:S(2)}, u32[]{:S(2)}) %collective-permute-start) | collective-permute-done | bytes 131104 | tf_op jit(solution)/shard_map/cond/branch_1_fun/ppermute | solution.py:252
  26.1 1.6 %add_convert_fusion = bf16[256,256]{1,0:T(8,128)(2,1)} fusion(bf16[256,256]{1,0:T(8,128)(2,1)S(1)} %collective-permute-done, bf16[256,256]{1,0:T(8,128)(2,1)} %get-tuple-element.18), kind=kLoop, calls=%fused_computation | loop fusion | flops 262144 | bytes 393216 | tf_op jit(solution)/shard_map/cond/branch_1_fun/convert_element_type | solution.py:259
  29.4 2.6 %collective-permute-start.13 = (bf16[128,512]{1,0:T(8,128)(2,1)S(1)}, bf16[128,512]{1,0:T(8,128)(2,1)S(1)}, u32[]{:S(2)}, u32[]{:S(2)}) collective-permute-start(bf16[128,512]{1,0:T(8,128)(2,1)S(1)} %get-tuple-element.114), channel_id=1, source_target_pairs={{0,2},{1,3},{2,0},{3,1},{4,6},{5,7},{6,4},{7,5},{8,10},{9,11},{10,... | collective-permute-start | bytes 393224 | tf_op jit(solution)/shard_map/ppermute | solution.py:249
  32.0 1.6 %collective-permute-start.14 = (bf16[128,512]{1,0:T(8,128)(2,1)S(1)}, bf16[128,512]{1,0:T(8,128)(2,1)S(1)}, u32[]{:S(2)}, u32[]{:S(2)}) collective-permute-start(bf16[128,512]{1,0:T(8,128)(2,1)S(1)} %get-tuple-element.115), channel_id=1, source_target_pairs={{0,3},{1,2},{2,1},{3,0},{4,7},{5,6},{6,5},{7,4},{8,11},{9,10},{10,... | collective-permute-start | bytes 393224 | tf_op jit(solution)/shard_map/ppermute | solution.py:249
  33.5 2.7 %shard_map.96 = (bf16[256,512]{1,0:T(8,128)(2,1)S(1)}, bf16[256,512]{1,0:T(8,128)(2,1)S(1)}) custom-call(s32[4]{0:T(128)S(1)} %pad_add_fusion.idx, bf16[128,512]{1,0:T(8,128)(2,1)S(1)} %collective-permute-done.5.r2, bf16[128,512]{1,0:T(8,128)(2,1)} %collective-permute-done.6.r3, bf16[512,512]{1,0:T(8,128)(2,1)S(1)} %copy-done.6, ...), custom_call_target="tpu_custom_call" | custom-call | flops 3221225472 | bytes 8388608 | tf_op jit(solution)/shard_map/pallas_call | solution.py:303
  36.4 15.2 %conditional.4 = (bf16[2,128,512]{2,1,0:T(8,128)(2,1)}, bf16[2,128,512]{2,1,0:T(8,128)(2,1)}, bf16[256,512]{1,0:T(8,128)(2,1)}, bf16[256,512]{1,0:T(8,128)(2,1)}) conditional(s32[]{:T(128)} %convert_element_type.37, () %tuple.31, (s32[4]{0:T(128)S(1)}, bf16[128,512]{1,0:T(8,128)(2,1)S(1)}, bf16[128,512]{1,0:T(8,128)(2,1)}, ...), branch_computations={%region_2.0_spmd, %region_3.0_spmd} | conditional | flops 269877248 | bytes 12190018 | solution.py:256
  36.5 1.5 %collective-permute-done.3 = bf16[256,512]{1,0:T(8,128)(2,1)S(1)} collective-permute-done((bf16[256,512]{1,0:T(8,128)(2,1)S(1)}, bf16[256,512]{1,0:T(8,128)(2,1)S(1)}, u32[]{:S(2)}, u32[]{:S(2)}) %collective-permute-start.3) | collective-permute-done | bytes 262176 | tf_op jit(solution)/shard_map/cond/branch_1_fun/ppermute | solution.py:252
  38.2 1.6 %collective-permute-start.4 = (bf16[256,512]{1,0:T(8,128)(2,1)S(1)}, bf16[256,512]{1,0:T(8,128)(2,1)}, u32[]{:S(2)}, u32[]{:S(2)}) collective-permute-start(bf16[256,512]{1,0:T(8,128)(2,1)S(1)} %fusion), channel_id=1, source_target_pairs={{0,16},{8,24},{16,0},{24,8},{1,17},{9,25},{17,1},{25,9},{2,18},{10... | collective-permute-start | bytes 786440 | tf_op jit(solution)/shard_map/cond/branch_1_fun/ppermute | solution.py:252
  39.8 3.5 %branch_1_fun.1 = (bf16[2,128,512]{2,1,0:T(8,128)(2,1)}, bf16[2,128,512]{2,1,0:T(8,128)(2,1)S(1)}) custom-call(s32[4]{0:T(128)S(1)} %get-tuple-element.41.idx, bf16[128,512]{1,0:T(8,128)(2,1)S(1)} %get-tuple-element.42.r2, bf16[128,512]{1,0:T(8,128)(2,1)} %get-tuple-element.43.r3, bf16[512,512]{1,0:T(8,128)(2,1)S(1)} %get-tuple-element.44.table, ...), custom_call_target="tpu_custom_call" | custom-call | flops 268435456 | bytes 1048576 | tf_op jit(solution)/shard_map/cond/branch_1_fun/pallas_call | solution.py:319
  44.0 2.7 %collective-permute-done.4 = bf16[256,512]{1,0:T(8,128)(2,1)} collective-permute-done((bf16[256,512]{1,0:T(8,128)(2,1)S(1)}, bf16[256,512]{1,0:T(8,128)(2,1)}, u32[]{:S(2)}, u32[]{:S(2)}) %collective-permute-start.4) | collective-permute-done | bytes 262176 | tf_op jit(solution)/shard_map/cond/branch_1_fun/ppermute | solution.py:252
  46.7 3.6 %conditional = (bf16[256,512]{1,0:T(8,128)(2,1)}, bf16[256,512]{1,0:T(8,128)(2,1)}) conditional(s32[]{:T(128)} %convert_element_type.31, () %tuple.21, (bf16[256,512]{1,0:T(8,128)(2,1)S(1)}, bf16[256,512]{1,0:T(8,128)(2,1)}) %tuple.22), branch_computations={%region_4.0_spmd, %region_5.0_spmd} | conditional | flops 524288 | bytes 1835064 | solution.py:256
  46.7 1.7 %add_convert_fusion.1 = bf16[256,512]{1,0:T(8,128)(2,1)} fusion(bf16[256,512]{1,0:T(8,128)(2,1)} %get-tuple-element.40, bf16[256,512]{1,0:T(8,128)(2,1)S(1)} %get-tuple-element.39), kind=kLoop, calls=%fused_computation.1 | loop fusion | flops 524288 | bytes 786432 | tf_op jit(solution)/shard_map/cond/branch_1_fun/cond/branch_1_fun/convert_element_type | solution.py:331
  48.4 1.9 %collective-permute-done.1 = bf16[256,512]{1,0:T(8,128)(2,1)} collective-permute-done((bf16[256,512]{1,0:T(8,128)(2,1)}, bf16[256,512]{1,0:T(8,128)(2,1)}, u32[]{:S(2)}, u32[]{:S(2)}) %collective-permute-start.1) | collective-permute-done | bytes 262176 | tf_op jit(solution)/shard_map/cond/branch_1_fun/cond/branch_1_fun/ppermute | solution.py:252
  50.3 1.2 %collective-permute-done.2 = bf16[2,128,512]{2,1,0:T(8,128)(2,1)} collective-permute-done((bf16[2,128,512]{2,1,0:T(8,128)(2,1)S(1)}, bf16[2,128,512]{2,1,0:T(8,128)(2,1)}, u32[]{:S(2)}, u32[]{:S(2)}) %collective-permute-start.2) | collective-permute-done | bytes 262176 | tf_op jit(solution)/shard_map/cond/branch_1_fun/ppermute | solution.py:249
  51.6 2.9 %shard_map.98 = (bf16[1,128,2048]{2,1,0:T(8,128)(2,1)}, bf16[1,128,2048]{2,1,0:T(8,128)(2,1)}, bf16[1,128,2048]{2,1,0:T(8,128)(2,1)}, f32[512,512]{1,0:T(8,128)}) custom-call(s32[4]{0:T(128)S(1)} %pad_add_fusion.idx, bf16[1,128,2048]{2,1,0:T(8,128)(2,1)S(1)} %copy-done.1, bf16[1,128,2048]{2,1,0:T(8,128)(2,1)S(1)} %copy-done.2, ...), custom_call_target="tpu_custom_call" | custom-call | flops 786432 | bytes 4718592 | tf_op jit(solution)/shard_map/pallas_call | solution.py:340
  (56 shorter events, 5.3 us)
Async XLA Ops:
  0.7 9.3 %copy-start.5 = (bf16[512,512]{1,0:T(8,128)(2,1)S(1)}, bf16[512,512]{1,0:T(8,128)(2,1)}, u32[]{:S(2)}) copy-start(bf16[512,512]{1,0:T(8,128)(2,1)} %constant.22.clone.table) | copy-start | bytes 1572868
  4.0 10.7 %collective-permute-start.7 = (bf16[256,256]{1,0:T(8,128)(2,1)}, bf16[256,256]{1,0:T(8,128)(2,1)S(1)}, u32[]{:S(2)}, u32[]{:S(2)}) collective-permute-start(bf16[256,256]{1,0:T(8,128)(2,1)} %get-tuple-element.95), channel_id=1, source_target_pairs={{0,2},{1,3},{2,0},{3,1},{4,6},{5,7},{6,4},{7,5},{8,10},{9,11},{10,... | collective-permute-start | bytes 393224 | tf_op jit(solution)/shard_map/ppermute | solution.py:249
  8.0 13.7 %collective-permute-start.9 = (bf16[2,128,512]{2,1,0:T(8,128)(2,1)}, bf16[2,128,512]{2,1,0:T(8,128)(2,1)S(1)}, u32[]{:S(2)}, u32[]{:S(2)}) collective-permute-start(bf16[2,128,512]{2,1,0:T(8,128)(2,1)} %get-tuple-element.100), channel_id=1, source_target_pairs={{0,1},{1,0},{2,3},{3,2},{4,5},{5,4},{6,7},{7,6},{8,9},{9,8},{10,11... | collective-permute-start | bytes 786440 | tf_op jit(solution)/shard_map/ppermute | solution.py:249
  9.6 18.5 %collective-permute-start.10 = (bf16[2,128,512]{2,1,0:T(8,128)(2,1)}, bf16[2,128,512]{2,1,0:T(8,128)(2,1)S(1)}, u32[]{:S(2)}, u32[]{:S(2)}) collective-permute-start(bf16[2,128,512]{2,1,0:T(8,128)(2,1)} %get-tuple-element.106), channel_id=1, source_target_pairs={{0,1},{1,0},{2,3},{3,2},{4,5},{5,4},{6,7},{7,6},{8,9},{9,8},{10,11... | collective-permute-start | bytes 786440 | tf_op jit(solution)/shard_map/ppermute | solution.py:249
  11.3 10.4 %copy-start.4 = (bf16[2,128,512]{2,1,0:T(8,128)(2,1)S(1)}, bf16[2,128,512]{2,1,0:T(8,128)(2,1)}, u32[]{:S(2)}) copy-start(bf16[2,128,512]{2,1,0:T(8,128)(2,1)} %get-tuple-element.99.keep) | copy-start | bytes 786436
  12.7 15.4 %copy-start.8 = (bf16[512,512]{1,0:T(8,128)(2,1)}, bf16[512,512]{1,0:T(8,128)(2,1)S(1)}, u32[]{:S(2)}) copy-start(bf16[512,512]{1,0:T(8,128)(2,1)S(1)} %get-tuple-element.104.cross) | copy-start | bytes 1572868
  12.7 15.4 %copy-start.14 = (bf16[256,512]{1,0:T(8,128)(2,1)}, bf16[256,512]{1,0:T(8,128)(2,1)S(1)}, u32[]{:S(2)}) copy-start(bf16[256,512]{1,0:T(8,128)(2,1)S(1)} %get-tuple-element.96.inv) | copy-start | bytes 786436
  14.6 3.5 %collective-permute-start.8 = (bf16[256,256]{1,0:T(8,128)(2,1)S(1)}, bf16[256,256]{1,0:T(8,128)(2,1)S(1)}, u32[]{:S(2)}, u32[]{:S(2)}) collective-permute-start(bf16[256,256]{1,0:T(8,128)(2,1)S(1)} %collective-permute-done.7.mine), channel_id=1, source_target_pairs={{0,8},{8,0},{16,24},{24,16},{1,9},{9,1},{17,25},{25,17},{2,10},{10... | collective-permute-start | bytes 393224 | tf_op jit(solution)/shard_map/ppermute | solution.py:252
  14.6 17.3 %collective-permute-start.5 = (bf16[128,512]{1,0:T(8,128)(2,1)}, bf16[128,512]{1,0:T(8,128)(2,1)S(1)}, u32[]{:S(2)}, u32[]{:S(2)}) collective-permute-start(bf16[128,512]{1,0:T(8,128)(2,1)} %get-tuple-element.90), channel_id=1, source_target_pairs={{0,2},{1,3},{2,0},{3,1},{4,6},{5,7},{6,4},{7,5},{8,10},{9,11},{10,... | collective-permute-start | bytes 393224 | tf_op jit(solution)/shard_map/ppermute | solution.py:249
  15.5 18.0 %collective-permute-start.6 = (bf16[128,512]{1,0:T(8,128)(2,1)}, bf16[128,512]{1,0:T(8,128)(2,1)}, u32[]{:S(2)}, u32[]{:S(2)}) collective-permute-start(bf16[128,512]{1,0:T(8,128)(2,1)} %get-tuple-element.91), channel_id=1, source_target_pairs={{0,3},{1,2},{2,1},{3,0},{4,7},{5,6},{6,5},{7,4},{8,11},{9,10},{10,... | collective-permute-start | bytes 393224 | tf_op jit(solution)/shard_map/ppermute | solution.py:249
  24.5 1.6 %collective-permute-start = (bf16[256,256]{1,0:T(8,128)(2,1)}, bf16[256,256]{1,0:T(8,128)(2,1)S(1)}, u32[]{:S(2)}, u32[]{:S(2)}) collective-permute-start(bf16[256,256]{1,0:T(8,128)(2,1)} %get-tuple-element.38), channel_id=1, source_target_pairs={{0,8},{8,0},{16,24},{24,16},{1,9},{9,1},{17,25},{25,17},{2,10},{10... | collective-permute-start | bytes 393224 | tf_op jit(solution)/shard_map/cond/branch_1_fun/ppermute | solution.py:252
  27.7 8.6 %collective-permute-start.11 = (bf16[256,256]{1,0:T(8,128)(2,1)}, bf16[256,256]{1,0:T(8,128)(2,1)S(1)}, u32[]{:S(2)}, u32[]{:S(2)}) collective-permute-start(bf16[256,256]{1,0:T(8,128)(2,1)} %get-tuple-element.132), channel_id=1, source_target_pairs={{0,2},{1,3},{2,0},{3,1},{4,6},{5,7},{6,4},{7,5},{8,10},{9,11},{10,... | collective-permute-start | bytes 393224 | tf_op jit(solution)/shard_map/ppermute | solution.py:249
  27.7 23.9 %collective-permute-start.12 = (bf16[2,128,512]{2,1,0:T(8,128)(2,1)S(1)}, bf16[2,128,512]{2,1,0:T(8,128)(2,1)S(1)}, u32[]{:S(2)}, u32[]{:S(2)}) collective-permute-start(bf16[2,128,512]{2,1,0:T(8,128)(2,1)S(1)} %get-tuple-element.113), channel_id=1, source_target_pairs={{0,1},{1,0},{2,3},{3,2},{4,5},{5,4},{6,7},{7,6},{8,9},{9,8},{10,11... | collective-permute-start | bytes 786440 | tf_op jit(solution)/shard_map/ppermute | solution.py:249
  28.1 5.4 %copy-start.12 = (bf16[2,128,512]{2,1,0:T(8,128)(2,1)}, bf16[2,128,512]{2,1,0:T(8,128)(2,1)S(1)}, u32[]{:S(2)}) copy-start(bf16[2,128,512]{2,1,0:T(8,128)(2,1)S(1)} %collective-permute-done.10.recv) | copy-start | bytes 786436
  29.4 22.2 %collective-permute-start.13 = (bf16[128,512]{1,0:T(8,128)(2,1)S(1)}, bf16[128,512]{1,0:T(8,128)(2,1)S(1)}, u32[]{:S(2)}, u32[]{:S(2)}) collective-permute-start(bf16[128,512]{1,0:T(8,128)(2,1)S(1)} %get-tuple-element.114), channel_id=1, source_target_pairs={{0,2},{1,3},{2,0},{3,1},{4,6},{5,7},{6,4},{7,5},{8,10},{9,11},{10,... | collective-permute-start | bytes 393224 | tf_op jit(solution)/shard_map/ppermute | solution.py:249
  32.0 4.4 %copy-start.16 = (bf16[512,512]{1,0:T(8,128)(2,1)S(1)}, bf16[512,512]{1,0:T(8,128)(2,1)}, u32[]{:S(2)}) copy-start(bf16[512,512]{1,0:T(8,128)(2,1)} %get-tuple-element.97) | copy-start | bytes 1572868
  32.0 19.6 %collective-permute-start.14 = (bf16[128,512]{1,0:T(8,128)(2,1)S(1)}, bf16[128,512]{1,0:T(8,128)(2,1)S(1)}, u32[]{:S(2)}, u32[]{:S(2)}) collective-permute-start(bf16[128,512]{1,0:T(8,128)(2,1)S(1)} %get-tuple-element.115), channel_id=1, source_target_pairs={{0,3},{1,2},{2,1},{3,0},{4,7},{5,6},{6,5},{7,4},{8,11},{9,10},{10,... | collective-permute-start | bytes 393224 | tf_op jit(solution)/shard_map/ppermute | solution.py:249
  36.3 15.2 %copy-start.1 = (bf16[1,128,2048]{2,1,0:T(8,128)(2,1)S(1)}, bf16[1,128,2048]{2,1,0:T(8,128)(2,1)}, u32[]{:S(2)}) copy-start(bf16[1,128,2048]{2,1,0:T(8,128)(2,1)} %q.3) | copy-start | bytes 1572868
  36.4 15.2 %copy-start.2 = (bf16[1,128,2048]{2,1,0:T(8,128)(2,1)S(1)}, bf16[1,128,2048]{2,1,0:T(8,128)(2,1)}, u32[]{:S(2)}) copy-start(bf16[1,128,2048]{2,1,0:T(8,128)(2,1)} %k.3) | copy-start | bytes 1572868
  36.4 15.2 %copy-start.3 = (bf16[1,128,2048]{2,1,0:T(8,128)(2,1)S(1)}, bf16[1,128,2048]{2,1,0:T(8,128)(2,1)}, u32[]{:S(2)}) copy-start(bf16[1,128,2048]{2,1,0:T(8,128)(2,1)} %g.3) | copy-start | bytes 1572868
  36.4 1.6 %collective-permute-start.3 = (bf16[256,512]{1,0:T(8,128)(2,1)S(1)}, bf16[256,512]{1,0:T(8,128)(2,1)S(1)}, u32[]{:S(2)}, u32[]{:S(2)}) collective-permute-start(bf16[256,512]{1,0:T(8,128)(2,1)S(1)} %get-tuple-element.54), channel_id=1, source_target_pairs={{0,8},{8,0},{16,24},{24,16},{1,9},{9,1},{17,25},{25,17},{2,10},{10... | collective-permute-start | bytes 786440 | tf_op jit(solution)/shard_map/cond/branch_1_fun/ppermute | solution.py:252
  38.2 8.5 %collective-permute-start.4 = (bf16[256,512]{1,0:T(8,128)(2,1)S(1)}, bf16[256,512]{1,0:T(8,128)(2,1)}, u32[]{:S(2)}, u32[]{:S(2)}) collective-permute-start(bf16[256,512]{1,0:T(8,128)(2,1)S(1)} %fusion), channel_id=1, source_target_pairs={{0,16},{8,24},{16,0},{24,8},{1,17},{9,25},{17,1},{25,9},{2,18},{10... | collective-permute-start | bytes 786440 | tf_op jit(solution)/shard_map/cond/branch_1_fun/ppermute | solution.py:252
  43.3 8.2 %collective-permute-start.2 = (bf16[2,128,512]{2,1,0:T(8,128)(2,1)S(1)}, bf16[2,128,512]{2,1,0:T(8,128)(2,1)}, u32[]{:S(2)}, u32[]{:S(2)}) collective-permute-start(bf16[2,128,512]{2,1,0:T(8,128)(2,1)S(1)} %get-tuple-element.51), channel_id=1, source_target_pairs={{0,1},{1,0},{2,3},{3,2},{4,5},{5,4},{6,7},{7,6},{8,9},{9,8},{10,11... | collective-permute-start | bytes 786440 | tf_op jit(solution)/shard_map/cond/branch_1_fun/ppermute | solution.py:249
  48.4 1.9 %collective-permute-start.1 = (bf16[256,512]{1,0:T(8,128)(2,1)}, bf16[256,512]{1,0:T(8,128)(2,1)}, u32[]{:S(2)}, u32[]{:S(2)}) collective-permute-start(bf16[256,512]{1,0:T(8,128)(2,1)} %add_convert_fusion.1), channel_id=1, source_target_pairs={{0,8},{8,0},{16,24},{24,16},{1,9},{9,1},{17,25},{25,17},{2,10},{10... | collective-permute-start | bytes 786440 | tf_op jit(solution)/shard_map/cond/branch_1_fun/cond/branch_1_fun/ppermute | solution.py:252
  (8 other events, 22.9 us)

commit v3 on v2

--- a/solution.py
+++ b/solution.py
@@ -284,16 +284,20 @@
     near, cross, inv, piece = lax.optimization_barrier((near, cross, inv, piece))
     other_piece = xd(piece, 1)
     far1, to2, to3, own1 = xz(far1, 1), xz(to2, 2), xz(to3, 3), xz(own1, 1)
-    okeep_far, ofar1, *far_parts = call(
-        conv_far_kernel,
-        [two] * 2 + [((rows, half), bf16)] * 2,
-        6,
-        cost=(8 * macs, 32 * length * quarter),
-        limit=CONV_VMEM,
-        scratch=[pltpu.VMEM((length, quarter), f32), pltpu.VMEM((length, quarter), bf16), pltpu.VMEM((4, half, quarter), bf16)],
-    )(idx, table, inv, piece, other_piece, keep_far, far1)
+
+    def far_quarter(idx, inv, piece, other_piece, keep_far, far1):
+        okeep, o1, *parts = call(
+            conv_far_kernel,
+            [two] * 2 + [((rows, half), bf16)] * 2,
+            6,
+            cost=(8 * macs, 32 * length * quarter),
+            limit=CONV_VMEM,
+            scratch=[pltpu.VMEM((length, quarter), f32), pltpu.VMEM((length, quarter), bf16), pltpu.VMEM((4, half, quarter), bf16)],
+        )(idx, table, inv, piece, other_piece, keep_far, far1)
+        return okeep, o1, over_cores(*parts)
+
+    okeep_far, ofar1, far = apart(far_quarter, idx, inv, piece, other_piece, keep_far, far1)
     ofar1 = xz(ofar1, 1)
-    far = apart(over_cores, *far_parts)
     far, cross = lax.optimization_barrier((far, cross))
     far = xz(far, 2)
     o2, o3 = call(

time: 54.8 us -> 54.1 us (0.987)
  other arithmetic: 3.52 us -> 1.98 us
  waiting for transfers between devices: 14.4 us -> 15.1 us
    convert_element_type x1, other arithmetic: 1.58 us -> 0.03 us  [over_cores(): return (keep.astype(f32) + xd(send, 1).astype(f32)).astype(bf16)]
    ppermute x10, waiting for transfers between devices: 6.75 us -> 7.81 us  [xz(): return lax.ppermute(vals, 'ctx', [(i, i ^ k) for i in range(4)])]
    unnamed x28 -> x34, local copies, waits for them, and re-layouts: 1.28 us -> 1.29 us
  transfers between devices with their start and end apart: 15 -> 15, of which waited for: 7 -> 8; matrix products, arithmetic and copies ran while one was open for 6% -> 4% of each run, Pallas kernels for 21% -> 21%
where the time goes in v3:
time: 54.1 us; the launch traced here: 53.9 us
  Pallas kernels  17.6 us (33%)
  starting transfers between devices  17 us (31%)
  waiting for transfers between devices  15.1 us (28%)
  other arithmetic  1.98 us (4%)
  local copies, waits for them, and re-layouts  1.3 us (2%)
  between operations  0.78 us (1%)
    ppermute x10, starting transfers between devices, xz(): return lax.ppermute(vals, 'ctx', [(i, i ^ k) for i in range(4)])  15.3 us
    ppermute x10, waiting for transfers between devices, xz(): return lax.ppermute(vals, 'ctx', [(i, i ^ k) for i in range(4)])  7.81 us
    ppermute x5, waiting for transfers between devices, xd(): return lax.ppermute(vals, 'dp', [(i, i ^ k) for i in range(4)])  7.3 us
    pallas_call x1, Pallas kernels, own_quarter(): call(conv_own_kernel, [two] * 2, 8, in_hbm=2, cost=(4 * macs, 4 * length...  3.36 us
    pallas_call x1, Pallas kernels, half_plan(): pl.pallas_call(functools.partial(gate_kernel, quarter), out_shape=[jax.Sh...  3.28 us
    pallas_call x1, Pallas kernels, half_plan(): call(functools.partial(final_kernel, quarter), [act] * 3 + [(filter_taps....  2.97 us
    pallas_call x1, Pallas kernels, far_quarter(): call(conv_far_kernel, [two] * 2 + [((rows, half), bf16)] * 2, 6, cost=(8...  2.84 us
    pallas_call x1, Pallas kernels, half_plan(): call(own_filter_grad_kernel, [((rows, length), bf16)] * 2, 5, in_hbm=2, c...  2.53 us
  transfers between devices with their start and end apart: 15, of which 8 were waited for; matrix products, arithmetic and copies ran while one was open for 4% of the time, Pallas kernels for 21%

profile of v3, /device:TPU:0, one launch (start us, length us, event | category | flops | bytes accessed | tf_op | source)
XLA Modules:
  0.0 53.9 jit_solution(14794286824975683185)
XLA Ops:
  0.7 3.3 %shard_map.93 = (bf16[2,128,512]{2,1,0:T(8,128)(2,1)}, bf16[2,128,512]{2,1,0:T(8,128)(2,1)}, bf16[2,128,512]{2,1,0:T(8,128)(2,1)}, bf16[2,128,512]{2,1,0:T(8,128...) custom-call(s32[4]{0:T(128)S(1)} %pad_add_fusion.idx, ...), custom_call_target="tpu_custom_call" | custom-call | flops 524288 | bytes 4194304 | tf_op jit(solution)/shard_map/pallas_call | solution.py:268
  4.0 4.0 %collective-permute-start.7 = (bf16[256,256]{1,0:T(8,128)(2,1)}, bf16[256,256]{1,0:T(8,128)(2,1)S(1)}, u32[]{:S(2)}, u32[]{:S(2)}) collective-permute-start(bf16[256,256]{1,0:T(8,128)(2,1)} %get-tuple-element.110), channel_id=1, source_target_pairs={{0,2},{1,3},{2,0},{3,1},{4,6},{5,7},{6,4},{7,5},{8,10},{9,11},{10,... | collective-permute-start | bytes 393224 | tf_op jit(solution)/shard_map/ppermute | solution.py:249
  8.0 1.6 %collective-permute-start.9 = (bf16[2,128,512]{2,1,0:T(8,128)(2,1)}, bf16[2,128,512]{2,1,0:T(8,128)(2,1)S(1)}, u32[]{:S(2)}, u32[]{:S(2)}) collective-permute-start(bf16[2,128,512]{2,1,0:T(8,128)(2,1)} %get-tuple-element.115), channel_id=1, source_target_pairs={{0,1},{1,0},{2,3},{3,2},{4,5},{5,4},{6,7},{7,6},{8,9},{9,8},{10,11... | collective-permute-start | bytes 786440 | tf_op jit(solution)/shard_map/ppermute | solution.py:249
  10.1 1.2 %copy-done = f32[512,512]{1,0:T(8,128)S(1)} copy-done((f32[512,512]{1,0:T(8,128)S(1)}, f32[512,512]{1,0:T(8,128)}, u32[]{:S(2)}) %copy-start) | copy-done | bytes 1048600
  11.3 1.4 %shard_map.94 = (bf16[512,512]{1,0:T(8,128)(2,1)}, bf16[512,512]{1,0:T(8,128)(2,1)S(1)}, bf16[256,512]{1,0:T(8,128)(2,1)S(1)}) custom-call(bf16[512,512]{1,0:T(8,128)(2,1)S(1)} %copy-done.4, f32[512,512]{1,0:T(8,128)S(1)} %copy-done), custom_call_target="tpu_custom_call" | custom-call | flops 402653184 | bytes 4194304 | tf_op jit(solution)/shard_map/pallas_call | solution.py:281
  12.7 2.0 %collective-permute-done.7 = bf16[256,256]{1,0:T(8,128)(2,1)S(1)} collective-permute-done((bf16[256,256]{1,0:T(8,128)(2,1)}, bf16[256,256]{1,0:T(8,128)(2,1)S(1)}, u32[]{:S(2)}, u32[]{:S(2)}) %collective-permute-start.7) | collective-permute-done | bytes 131104 | tf_op jit(solution)/shard_map/ppermute | solution.py:249
  15.5 2.7 %collective-permute-start.6 = (bf16[128,512]{1,0:T(8,128)(2,1)S(1)}, bf16[128,512]{1,0:T(8,128)(2,1)S(1)}, u32[]{:S(2)}, u32[]{:S(2)}) collective-permute-start(bf16[128,512]{1,0:T(8,128)(2,1)S(1)} %copy-done.17), channel_id=1, source_target_pairs={{0,3},{1,2},{2,1},{3,0},{4,7},{5,6},{6,5},{7,4},{8,11},{9,10},{10,... | collective-permute-start | bytes 393224 | tf_op jit(solution)/shard_map/ppermute | solution.py:249
  18.3 3.6 %collective-permute-done.9 = bf16[2,128,512]{2,1,0:T(8,128)(2,1)S(1)} collective-permute-done((bf16[2,128,512]{2,1,0:T(8,128)(2,1)}, bf16[2,128,512]{2,1,0:T(8,128)(2,1)S(1)}, u32[]{:S(2)}, u32[]{:S(2)}) %collective-permute-start.9) | collective-permute-done | bytes 262176 | tf_op jit(solution)/shard_map/ppermute | solution.py:249
  21.9 4.2 %conditional.3 = (bf16[2,128,512]{2,1,0:T(8,128)(2,1)}, bf16[2,128,512]{2,1,0:T(8,128)(2,1)}, bf16[256,256]{1,0:T(8,128)(2,1)S(1)}) conditional(s32[]{:T(128)} %convert_element_type.37, () %tuple.35, (s32[4]{0:T(128)S(1)}, bf16[512,512]{1,0:T(8,128)(2,1)S(1)}, bf16[256,512]{1,0:T(8,128)(2,1)S(1)}, bf16[256,256]{1,0:T(8,128)(2,1)S(1)}, ...), branch_computations={%region_0.0_spmd, %region_1.0_spmd} | conditional | flops 537133056 | bytes 9306176 | solution.py:256
  21.9 2.8 %branch_1_fun.2 = (bf16[2,128,512]{2,1,0:T(8,128)(2,1)}, bf16[2,128,512]{2,1,0:T(8,128)(2,1)}, bf16[256,256]{1,0:T(8,128)(2,1)S(1)}, bf16[256,256]{1,0:T(8,128)(2,1)S(1)}) custom-call(s32[4]{0:T(128)S(1)} %get-tuple-element.44.idx, bf16[512,512]{1,0:T(8,128)(2,1)S(1)} %get-tuple-element.45.table, bf16[256,512]{1,0:T(8,128)(2,1)S(1)} %get-tuple-element.46.inv, ...), custom_call_target="tpu_custom_call" | custom-call | flops 536870912 | bytes 8388608 | tf_op jit(solution)/shard_map/cond/branch_1_fun/pallas_call | solution.py:289
  24.8 1.3 %collective-permute-done = bf16[256,256]{1,0:T(8,128)(2,1)S(1)} collective-permute-done((bf16[256,256]{1,0:T(8,128)(2,1)S(1)}, bf16[256,256]{1,0:T(8,128)(2,1)S(1)}, u32[]{:S(2)}, u32[]{:S(2)}) %collective-permute-start) | collective-permute-done | bytes 131104 | tf_op jit(solution)/shard_map/cond/branch_1_fun/ppermute | solution.py:252
  26.5 1.2 %shard_map.96 = (bf16[128,512]{1,0:T(8,128)(2,1)S(1)}, bf16[128,512]{1,0:T(8,128)(2,1)S(1)}) custom-call(s32[4]{0:T(128)S(1)} %pad_add_fusion.idx, bf16[512,512]{1,0:T(8,128)(2,1)S(1)} %copy-done.4, bf16[256,512]{1,0:T(8,128)(2,1)S(1)} %get-tuple-element.111.inv, bf16[512,512]{1,0:T(8,128)(2,1)S(1)} %get-tuple-element.118.cross, ...), custom_call_target="tpu_custom_call" | custom-call | flops 268435456 | bytes 2097152 | tf_op jit(solution)/shard_map/pallas_call | solution.py:303
  27.7 2.8 %collective-permute-start.13 = (bf16[128,512]{1,0:T(8,128)(2,1)S(1)}, bf16[128,512]{1,0:T(8,128)(2,1)S(1)}, u32[]{:S(2)}, u32[]{:S(2)}) collective-permute-start(bf16[128,512]{1,0:T(8,128)(2,1)S(1)} %get-tuple-element.128), channel_id=1, source_target_pairs={{0,2},{1,3},{2,0},{3,1},{4,6},{5,7},{6,4},{7,5},{8,10},{9,11},{10,... | collective-permute-start | bytes 393224 | tf_op jit(solution)/shard_map/ppermute | solution.py:249
  30.5 1.6 %collective-permute-start.14 = (bf16[128,512]{1,0:T(8,128)(2,1)S(1)}, bf16[128,512]{1,0:T(8,128)(2,1)S(1)}, u32[]{:S(2)}, u32[]{:S(2)}) collective-permute-start(bf16[128,512]{1,0:T(8,128)(2,1)S(1)} %get-tuple-element.129), channel_id=1, source_target_pairs={{0,3},{1,2},{2,1},{3,0},{4,7},{5,6},{6,5},{7,4},{8,11},{9,10},{10,... | collective-permute-start | bytes 393224 | tf_op jit(solution)/shard_map/ppermute | solution.py:249
  32.1 2.5 %shard_map.95 = (bf16[256,512]{1,0:T(8,128)(2,1)S(1)}, bf16[256,512]{1,0:T(8,128)(2,1)S(1)}) custom-call(s32[4]{0:T(128)S(1)} %pad_add_fusion.idx, bf16[128,512]{1,0:T(8,128)(2,1)S(1)} %collective-permute-done.5.r2, bf16[128,512]{1,0:T(8,128)(2,1)S(1)} %collective-permute-done.6.r3, bf16[512,512]{1,0:T(8,128)(2,1)S(1)} %copy-done.4, ...), custom_call_target="tpu_custom_call" | custom-call | flops 3221225472 | bytes 8388608 | tf_op jit(solution)/shard_map/pallas_call | solution.py:307
  35.8 15.1 %conditional.4 = (bf16[2,128,512]{2,1,0:T(8,128)(2,1)}, bf16[2,128,512]{2,1,0:T(8,128)(2,1)}, bf16[256,512]{1,0:T(8,128)(2,1)}, bf16[256,512]{1,0:T(8,128)(2,1)}) conditional(s32[]{:T(128)} %convert_element_type.37, () %tuple.33, (s32[4]{0:T(128)S(1)}, bf16[128,512]{1,0:T(8,128)(2,1)S(1)}, bf16[128,512]{1,0:T(8,128)(2,1)}, ...), branch_computations={%region_2.0_spmd, %region_3.0_spmd} | conditional | flops 269877248 | bytes 10617126 | solution.py:256
  35.9 1.5 %collective-permute-done.3 = bf16[256,512]{1,0:T(8,128)(2,1)S(1)} collective-permute-done((bf16[256,512]{1,0:T(8,128)(2,1)S(1)}, bf16[256,512]{1,0:T(8,128)(2,1)S(1)}, u32[]{:S(2)}, u32[]{:S(2)}) %collective-permute-start.3) | collective-permute-done | bytes 262176 | tf_op jit(solution)/shard_map/cond/branch_1_fun/ppermute | solution.py:252
  37.6 1.7 %collective-permute-start.4 = (bf16[256,512]{1,0:T(8,128)(2,1)S(1)}, bf16[256,512]{1,0:T(8,128)(2,1)}, u32[]{:S(2)}, u32[]{:S(2)}) collective-permute-start(bf16[256,512]{1,0:T(8,128)(2,1)S(1)} %fusion), channel_id=1, source_target_pairs={{0,16},{8,24},{16,0},{24,8},{1,17},{9,25},{17,1},{25,9},{2,18},{10... | collective-permute-start | bytes 786440 | tf_op jit(solution)/shard_map/cond/branch_1_fun/ppermute | solution.py:252
  39.3 3.4 %branch_1_fun.3 = (bf16[2,128,512]{2,1,0:T(8,128)(2,1)}, bf16[2,128,512]{2,1,0:T(8,128)(2,1)S(1)}) custom-call(s32[4]{0:T(128)S(1)} %get-tuple-element.57.idx, bf16[128,512]{1,0:T(8,128)(2,1)S(1)} %get-tuple-element.58.r2, bf16[128,512]{1,0:T(8,128)(2,1)S(1)} %copy-done.15, bf16[512,512]{1,0:T(8,128)(2,1)S(1)} %get-tuple-element.60.table, ...), custom_call_target="tpu_custom_call" | custom-call | flops 268435456 | bytes 1048576 | tf_op jit(solution)/shard_map/cond/branch_1_fun/pallas_call | solution.py:323
  43.5 2.6 %collective-permute-done.4 = bf16[256,512]{1,0:T(8,128)(2,1)} collective-permute-done((bf16[256,512]{1,0:T(8,128)(2,1)S(1)}, bf16[256,512]{1,0:T(8,128)(2,1)}, u32[]{:S(2)}, u32[]{:S(2)}) %collective-permute-start.4) | collective-permute-done | bytes 262176 | tf_op jit(solution)/shard_map/cond/branch_1_fun/ppermute | solution.py:252
  46.1 3.6 %conditional = (bf16[256,512]{1,0:T(8,128)(2,1)}, bf16[256,512]{1,0:T(8,128)(2,1)}) conditional(s32[]{:T(128)} %convert_element_type.31, () %tuple.23, (bf16[256,512]{1,0:T(8,128)(2,1)S(1)}, bf16[256,512]{1,0:T(8,128)(2,1)}) %tuple.24), branch_computations={%region_4.0_spmd, %region_5.0_spmd} | conditional | flops 524288 | bytes 1835064 | solution.py:256
  46.1 1.7 %add_convert_fusion.1 = bf16[256,512]{1,0:T(8,128)(2,1)} fusion(bf16[256,512]{1,0:T(8,128)(2,1)} %get-tuple-element.56, bf16[256,512]{1,0:T(8,128)(2,1)S(1)} %get-tuple-element.55), kind=kLoop, calls=%fused_computation.1 | loop fusion | flops 524288 | bytes 786432 | tf_op jit(solution)/shard_map/cond/branch_1_fun/cond/branch_1_fun/convert_element_type | solution.py:335
  47.8 1.9 %collective-permute-done.1 = bf16[256,512]{1,0:T(8,128)(2,1)} collective-permute-done((bf16[256,512]{1,0:T(8,128)(2,1)}, bf16[256,512]{1,0:T(8,128)(2,1)}, u32[]{:S(2)}, u32[]{:S(2)}) %collective-permute-start.1) | collective-permute-done | bytes 262176 | tf_op jit(solution)/shard_map/cond/branch_1_fun/cond/branch_1_fun/ppermute | solution.py:252
  50.9 3.0 %shard_map.97 = (bf16[1,128,2048]{2,1,0:T(8,128)(2,1)}, bf16[1,128,2048]{2,1,0:T(8,128)(2,1)}, bf16[1,128,2048]{2,1,0:T(8,128)(2,1)}, f32[512,512]{1,0:T(8,128)}) custom-call(s32[4]{0:T(128)S(1)} %pad_add_fusion.idx, bf16[1,128,2048]{2,1,0:T(8,128)(2,1)S(1)} %copy-done.1, bf16[1,128,2048]{2,1,0:T(8,128)(2,1)S(1)} %copy-done.2, ...), custom_call_target="tpu_custom_call" | custom-call | flops 786432 | bytes 4718592 | tf_op jit(solution)/shard_map/pallas_call | solution.py:344
  (60 shorter events, 5.2 us)
Async XLA Ops:
  0.7 9.3 %copy-start.4 = (bf16[512,512]{1,0:T(8,128)(2,1)S(1)}, bf16[512,512]{1,0:T(8,128)(2,1)}, u32[]{:S(2)}) copy-start(bf16[512,512]{1,0:T(8,128)(2,1)} %constant.15.clone.table) | copy-start | bytes 1572868
  4.0 10.7 %collective-permute-start.7 = (bf16[256,256]{1,0:T(8,128)(2,1)}, bf16[256,256]{1,0:T(8,128)(2,1)S(1)}, u32[]{:S(2)}, u32[]{:S(2)}) collective-permute-start(bf16[256,256]{1,0:T(8,128)(2,1)} %get-tuple-element.110), channel_id=1, source_target_pairs={{0,2},{1,3},{2,0},{3,1},{4,6},{5,7},{6,4},{7,5},{8,10},{9,11},{10,... | collective-permute-start | bytes 393224 | tf_op jit(solution)/shard_map/ppermute | solution.py:249
  8.0 13.9 %collective-permute-start.9 = (bf16[2,128,512]{2,1,0:T(8,128)(2,1)}, bf16[2,128,512]{2,1,0:T(8,128)(2,1)S(1)}, u32[]{:S(2)}, u32[]{:S(2)}) collective-permute-start(bf16[2,128,512]{2,1,0:T(8,128)(2,1)} %get-tuple-element.115), channel_id=1, source_target_pairs={{0,1},{1,0},{2,3},{3,2},{4,5},{5,4},{6,7},{7,6},{8,9},{9,8},{10,11... | collective-permute-start | bytes 786440 | tf_op jit(solution)/shard_map/ppermute | solution.py:249
  9.6 16.8 %collective-permute-start.10 = (bf16[2,128,512]{2,1,0:T(8,128)(2,1)}, bf16[2,128,512]{2,1,0:T(8,128)(2,1)S(1)}, u32[]{:S(2)}, u32[]{:S(2)}) collective-permute-start(bf16[2,128,512]{2,1,0:T(8,128)(2,1)} %get-tuple-element.120), channel_id=1, source_target_pairs={{0,1},{1,0},{2,3},{3,2},{4,5},{5,4},{6,7},{7,6},{8,9},{9,8},{10,11... | collective-permute-start | bytes 786440 | tf_op jit(solution)/shard_map/ppermute | solution.py:249
  11.3 10.6 %copy-start.16 = (bf16[2,128,512]{2,1,0:T(8,128)(2,1)S(1)}, bf16[2,128,512]{2,1,0:T(8,128)(2,1)}, u32[]{:S(2)}) copy-start(bf16[2,128,512]{2,1,0:T(8,128)(2,1)} %get-tuple-element.114) | copy-start | bytes 786436
  12.7 13.8 %copy-start.5 = (bf16[512,512]{1,0:T(8,128)(2,1)}, bf16[512,512]{1,0:T(8,128)(2,1)S(1)}, u32[]{:S(2)}) copy-start(bf16[512,512]{1,0:T(8,128)(2,1)S(1)} %get-tuple-element.118.cross) | copy-start | bytes 1572868
  12.7 13.8 %copy-start.11 = (bf16[256,512]{1,0:T(8,128)(2,1)}, bf16[256,512]{1,0:T(8,128)(2,1)S(1)}, u32[]{:S(2)}) copy-start(bf16[256,512]{1,0:T(8,128)(2,1)S(1)} %get-tuple-element.111.inv) | copy-start | bytes 786436
  14.7 3.6 %collective-permute-start.8 = (bf16[256,256]{1,0:T(8,128)(2,1)S(1)}, bf16[256,256]{1,0:T(8,128)(2,1)S(1)}, u32[]{:S(2)}, u32[]{:S(2)}) collective-permute-start(bf16[256,256]{1,0:T(8,128)(2,1)S(1)} %collective-permute-done.7), channel_id=1, source_target_pairs={{0,8},{8,0},{16,24},{24,16},{1,9},{9,1},{17,25},{25,17},{2,10},{10... | collective-permute-start | bytes 393224 | tf_op jit(solution)/shard_map/ppermute | solution.py:252
  14.7 15.8 %collective-permute-start.5 = (bf16[128,512]{1,0:T(8,128)(2,1)S(1)}, bf16[128,512]{1,0:T(8,128)(2,1)S(1)}, u32[]{:S(2)}, u32[]{:S(2)}) collective-permute-start(bf16[128,512]{1,0:T(8,128)(2,1)S(1)} %copy-done.18), channel_id=1, source_target_pairs={{0,2},{1,3},{2,0},{3,1},{4,6},{5,7},{6,4},{7,5},{8,10},{9,11},{10,... | collective-permute-start | bytes 393224 | tf_op jit(solution)/shard_map/ppermute | solution.py:249
  15.5 16.6 %collective-permute-start.6 = (bf16[128,512]{1,0:T(8,128)(2,1)S(1)}, bf16[128,512]{1,0:T(8,128)(2,1)S(1)}, u32[]{:S(2)}, u32[]{:S(2)}) collective-permute-start(bf16[128,512]{1,0:T(8,128)(2,1)S(1)} %copy-done.17), channel_id=1, source_target_pairs={{0,3},{1,2},{2,1},{3,0},{4,7},{5,6},{6,5},{7,4},{8,11},{9,10},{10,... | collective-permute-start | bytes 393224 | tf_op jit(solution)/shard_map/ppermute | solution.py:249
  24.8 1.3 %collective-permute-start = (bf16[256,256]{1,0:T(8,128)(2,1)S(1)}, bf16[256,256]{1,0:T(8,128)(2,1)S(1)}, u32[]{:S(2)}, u32[]{:S(2)}) collective-permute-start(bf16[256,256]{1,0:T(8,128)(2,1)S(1)} %get-tuple-element.54), channel_id=1, source_target_pairs={{0,8},{8,0},{16,24},{24,16},{1,9},{9,1},{17,25},{25,17},{2,10},{10... | collective-permute-start | bytes 393224 | tf_op jit(solution)/shard_map/cond/branch_1_fun/ppermute | solution.py:252
  26.2 9.6 %collective-permute-start.11 = (bf16[256,256]{1,0:T(8,128)(2,1)S(1)}, bf16[256,256]{1,0:T(8,128)(2,1)S(1)}, u32[]{:S(2)}, u32[]{:S(2)}) collective-permute-start(bf16[256,256]{1,0:T(8,128)(2,1)S(1)} %get-tuple-element.123), channel_id=1, source_target_pairs={{0,2},{1,3},{2,0},{3,1},{4,6},{5,7},{6,4},{7,5},{8,10},{9,11},{10,... | collective-permute-start | bytes 393224 | tf_op jit(solution)/shard_map/ppermute | solution.py:249
  26.2 24.6 %collective-permute-start.12 = (bf16[2,128,512]{2,1,0:T(8,128)(2,1)}, bf16[2,128,512]{2,1,0:T(8,128)(2,1)S(1)}, u32[]{:S(2)}, u32[]{:S(2)}) collective-permute-start(bf16[2,128,512]{2,1,0:T(8,128)(2,1)} %get-tuple-element.127), channel_id=1, source_target_pairs={{0,1},{1,0},{2,3},{3,2},{4,5},{5,4},{6,7},{7,6},{8,9},{9,8},{10,11... | collective-permute-start | bytes 786440 | tf_op jit(solution)/shard_map/ppermute | solution.py:249
  26.4 5.7 %copy-start.9 = (bf16[2,128,512]{2,1,0:T(8,128)(2,1)}, bf16[2,128,512]{2,1,0:T(8,128)(2,1)S(1)}, u32[]{:S(2)}) copy-start(bf16[2,128,512]{2,1,0:T(8,128)(2,1)S(1)} %collective-permute-done.10.recv) | copy-start | bytes 786436
  27.7 23.1 %collective-permute-start.13 = (bf16[128,512]{1,0:T(8,128)(2,1)S(1)}, bf16[128,512]{1,0:T(8,128)(2,1)S(1)}, u32[]{:S(2)}, u32[]{:S(2)}) collective-permute-start(bf16[128,512]{1,0:T(8,128)(2,1)S(1)} %get-tuple-element.128), channel_id=1, source_target_pairs={{0,2},{1,3},{2,0},{3,1},{4,6},{5,7},{6,4},{7,5},{8,10},{9,11},{10,... | collective-permute-start | bytes 393224 | tf_op jit(solution)/shard_map/ppermute | solution.py:249
  30.5 5.2 %copy-start.13 = (bf16[512,512]{1,0:T(8,128)(2,1)S(1)}, bf16[512,512]{1,0:T(8,128)(2,1)}, u32[]{:S(2)}) copy-start(bf16[512,512]{1,0:T(8,128)(2,1)} %get-tuple-element.112) | copy-start | bytes 1572868
  30.5 20.3 %collective-permute-start.14 = (bf16[128,512]{1,0:T(8,128)(2,1)S(1)}, bf16[128,512]{1,0:T(8,128)(2,1)S(1)}, u32[]{:S(2)}, u32[]{:S(2)}) collective-permute-start(bf16[128,512]{1,0:T(8,128)(2,1)S(1)} %get-tuple-element.129), channel_id=1, source_target_pairs={{0,3},{1,2},{2,1},{3,0},{4,7},{5,6},{6,5},{7,4},{8,11},{9,10},{10,... | collective-permute-start | bytes 393224 | tf_op jit(solution)/shard_map/ppermute | solution.py:249
  35.8 15.1 %copy-start.1 = (bf16[1,128,2048]{2,1,0:T(8,128)(2,1)S(1)}, bf16[1,128,2048]{2,1,0:T(8,128)(2,1)}, u32[]{:S(2)}) copy-start(bf16[1,128,2048]{2,1,0:T(8,128)(2,1)} %q.3) | copy-start | bytes 1572868
  35.8 15.1 %copy-start.2 = (bf16[1,128,2048]{2,1,0:T(8,128)(2,1)S(1)}, bf16[1,128,2048]{2,1,0:T(8,128)(2,1)}, u32[]{:S(2)}) copy-start(bf16[1,128,2048]{2,1,0:T(8,128)(2,1)} %k.3) | copy-start | bytes 1572868
  35.8 15.1 %copy-start.3 = (bf16[1,128,2048]{2,1,0:T(8,128)(2,1)S(1)}, bf16[1,128,2048]{2,1,0:T(8,128)(2,1)}, u32[]{:S(2)}) copy-start(bf16[1,128,2048]{2,1,0:T(8,128)(2,1)} %g.3) | copy-start | bytes 1572868
  35.8 1.6 %collective-permute-start.3 = (bf16[256,512]{1,0:T(8,128)(2,1)S(1)}, bf16[256,512]{1,0:T(8,128)(2,1)S(1)}, u32[]{:S(2)}, u32[]{:S(2)}) collective-permute-start(bf16[256,512]{1,0:T(8,128)(2,1)S(1)} %get-tuple-element.70), channel_id=1, source_target_pairs={{0,8},{8,0},{16,24},{24,16},{1,9},{9,1},{17,25},{25,17},{2,10},{10... | collective-permute-start | bytes 786440 | tf_op jit(solution)/shard_map/cond/branch_1_fun/ppermute | solution.py:252
  37.6 8.5 %collective-permute-start.4 = (bf16[256,512]{1,0:T(8,128)(2,1)S(1)}, bf16[256,512]{1,0:T(8,128)(2,1)}, u32[]{:S(2)}, u32[]{:S(2)}) collective-permute-start(bf16[256,512]{1,0:T(8,128)(2,1)S(1)} %fusion), channel_id=1, source_target_pairs={{0,16},{8,24},{16,0},{24,8},{1,17},{9,25},{17,1},{25,9},{2,18},{10... | collective-permute-start | bytes 786440 | tf_op jit(solution)/shard_map/cond/branch_1_fun/ppermute | solution.py:252
  42.6 8.2 %collective-permute-start.2 = (bf16[2,128,512]{2,1,0:T(8,128)(2,1)S(1)}, bf16[2,128,512]{2,1,0:T(8,128)(2,1)}, u32[]{:S(2)}, u32[]{:S(2)}) collective-permute-start(bf16[2,128,512]{2,1,0:T(8,128)(2,1)S(1)} %get-tuple-element.67), channel_id=1, source_target_pairs={{0,1},{1,0},{2,3},{3,2},{4,5},{5,4},{6,7},{7,6},{8,9},{9,8},{10,11... | collective-permute-start | bytes 786440 | tf_op jit(solution)/shard_map/cond/branch_1_fun/ppermute | solution.py:249
  47.8 1.9 %collective-permute-start.1 = (bf16[256,512]{1,0:T(8,128)(2,1)}, bf16[256,512]{1,0:T(8,128)(2,1)}, u32[]{:S(2)}, u32[]{:S(2)}) collective-permute-start(bf16[256,512]{1,0:T(8,128)(2,1)} %add_convert_fusion.1), channel_id=1, source_target_pairs={{0,8},{8,0},{16,24},{24,16},{1,9},{9,1},{17,25},{25,17},{2,10},{10... | collective-permute-start | bytes 786440 | tf_op jit(solution)/shard_map/cond/branch_1_fun/cond/branch_1_fun/ppermute | solution.py:252
  (10 other events, 35.1 us)

commit v4 on v3

--- a/solution.py
+++ b/solution.py
@@ -14,8 +14,9 @@
 f32 = jnp.float32
 VMEM_LIMIT = 20 * 1024 * 1024
 CONV_VMEM = 20 * 1024 * 1024
-GATE_VMEM = 63 * 1024 * 1024
-ROW_CHUNKS = 4
+GATE_VMEM = 58 * 1024 * 1024
+ROW_CHUNKS = 2
+FILT_CHUNKS = 4
 
 
 def dft_table(size):
@@ -209,10 +210,14 @@
     z, upper, core = idx[0], idx[2], idx[3] & 1
     is_up = jnp.where(upper == 0, 0.0, 1.0)
     size = mine.shape[0]
+    part_size = size // FILT_CHUNKS
+    copies = []
     for which, piece in ((core, mine), (1 - core, other)):
-        filt_held[pl.ds(pl.multiple_of(which * size, 8), size), :] = piece[...].astype(f32)
-    copies = [pltpu.make_async_copy(filt_held, grad_filt, sems.at[3 * ROW_CHUNKS])]
-    copies[0].start()
+        for j in range(FILT_CHUNKS):
+            at = pl.ds(pl.multiple_of(which * size + j * part_size, 8), part_size)
+            filt_held[at, :] = piece[j * part_size : (j + 1) * part_size, :].astype(f32)
+            copies.append(pltpu.make_async_copy(filt_held.at[at], grad_filt.at[at], sems.at[3 * ROW_CHUNKS + len(copies)]))
+            copies[-1].start()
     rows = q.shape[1] // ROW_CHUNKS
     for c in range(ROW_CHUNKS):
         part = pl.ds(c * rows, rows)
@@ -350,7 +355,7 @@
         scratch=[
             pltpu.VMEM((3, block, group), bf16),
             pltpu.VMEM(filter_taps.shape, f32),
-            pltpu.SemaphoreType.DMA((3 * ROW_CHUNKS + 1,)),
+            pltpu.SemaphoreType.DMA((3 * ROW_CHUNKS + 2 * FILT_CHUNKS,)),
         ],
     )(idx, query_proj, key_proj, out_grad, okeep, okeep_far, o1, ofar1, o2, o3, mine, other)
 

time: 54.1 us -> 53.8 us (level)
  local copies, waits for them, and re-layouts: 1.3 us -> 0.08 us
  waiting for transfers between devices: 15.1 us -> 16.3 us
    unnamed x34 -> x30, local copies, waits for them, and re-layouts: 1.29 us -> 0.06 us
    ppermute x10, waiting for transfers between devices: 7.81 us -> 9.04 us  [xz(): return lax.ppermute(vals, 'ctx', [(i, i ^ k) for i in range(4)])]
where the time goes in v4:
time: 53.8 us; the launch traced here: 53.6 us
  Pallas kernels  17.3 us (32%)
  starting transfers between devices  17 us (32%)
  waiting for transfers between devices  16.3 us (30%)
  other arithmetic  1.98 us (4%)
  between operations  0.77 us (1%)
    ppermute x10, starting transfers between devices, xz(): return lax.ppermute(vals, 'ctx', [(i, i ^ k) for i in range(4)])  15.3 us
    ppermute x10, waiting for transfers between devices, xz(): return lax.ppermute(vals, 'ctx', [(i, i ^ k) for i in range(4)])  9.04 us
    ppermute x5, waiting for transfers between devices, xd(): return lax.ppermute(vals, 'dp', [(i, i ^ k) for i in range(4)])  7.31 us
    pallas_call x1, Pallas kernels, own_quarter(): call(conv_own_kernel, [two] * 2, 8, in_hbm=2, cost=(4 * macs, 4 * length...  3.34 us
    pallas_call x1, Pallas kernels, half_plan(): pl.pallas_call(functools.partial(gate_kernel, quarter), out_shape=[jax.Sh...  3.08 us
    pallas_call x1, Pallas kernels, half_plan(): call(functools.partial(final_kernel, quarter), [act] * 3 + [(filter_taps....  2.89 us
    pallas_call x1, Pallas kernels, far_quarter(): call(conv_far_kernel, [two] * 2 + [((rows, half), bf16)] * 2, 6, cost=(8...  2.83 us
    pallas_call x1, Pallas kernels, half_plan(): call(own_filter_grad_kernel, [((rows, length), bf16)] * 2, 5, in_hbm=2, c...  2.54 us
  transfers between devices with their start and end apart: 15, of which 8 were waited for; matrix products, arithmetic and copies ran while one was open for 4% of the time, Pallas kernels for 21%

profile of v4, /device:TPU:0, one launch (start us, length us, event | category | flops | bytes accessed | tf_op | source)
XLA Modules:
  0.0 53.6 jit_solution(8737729887151622147)
XLA Ops:
  0.7 3.1 %shard_map.93 = (bf16[2,128,512]{2,1,0:T(8,128)(2,1)S(1)}, bf16[2,128,512]{2,1,0:T(8,128)(2,1)S(1)}, bf16[2,128,512]{2,1,0:T(8,128)(2,1)}, bf16[2,128,512]{2,1,0...) custom-call(s32[4]{0:T(128)S(1)} %pad_add_fusion.idx, ...), custom_call_target="tpu_custom_call" | custom-call | flops 524288 | bytes 4194304 | tf_op jit(solution)/shard_map/pallas_call | solution.py:273
  3.8 4.0 %collective-permute-start.7 = (bf16[256,256]{1,0:T(8,128)(2,1)}, bf16[256,256]{1,0:T(8,128)(2,1)S(1)}, u32[]{:S(2)}, u32[]{:S(2)}) collective-permute-start(bf16[256,256]{1,0:T(8,128)(2,1)} %get-tuple-element.110), channel_id=1, source_target_pairs={{0,2},{1,3},{2,0},{3,1},{4,6},{5,7},{6,4},{7,5},{8,10},{9,11},{10,... | collective-permute-start | bytes 393224 | tf_op jit(solution)/shard_map/ppermute | solution.py:254
  7.8 1.6 %collective-permute-start.9 = (bf16[2,128,512]{2,1,0:T(8,128)(2,1)}, bf16[2,128,512]{2,1,0:T(8,128)(2,1)S(1)}, u32[]{:S(2)}, u32[]{:S(2)}) collective-permute-start(bf16[2,128,512]{2,1,0:T(8,128)(2,1)} %get-tuple-element.115), channel_id=1, source_target_pairs={{0,1},{1,0},{2,3},{3,2},{4,5},{5,4},{6,7},{7,6},{8,9},{9,8},{10,11... | collective-permute-start | bytes 786440 | tf_op jit(solution)/shard_map/ppermute | solution.py:254
  9.9 1.4 %shard_map.94 = (bf16[512,512]{1,0:T(8,128)(2,1)}, bf16[512,512]{1,0:T(8,128)(2,1)S(1)}, bf16[256,512]{1,0:T(8,128)(2,1)S(1)}) custom-call(bf16[512,512]{1,0:T(8,128)(2,1)S(1)} %copy-done.4, f32[512,512]{1,0:T(8,128)S(1)} %copy-done), custom_call_target="tpu_custom_call" | custom-call | flops 402653184 | bytes 4194304 | tf_op jit(solution)/shard_map/pallas_call | solution.py:286
  11.3 3.2 %collective-permute-done.7 = bf16[256,256]{1,0:T(8,128)(2,1)S(1)} collective-permute-done((bf16[256,256]{1,0:T(8,128)(2,1)}, bf16[256,256]{1,0:T(8,128)(2,1)S(1)}, u32[]{:S(2)}, u32[]{:S(2)}) %collective-permute-start.7) | collective-permute-done | bytes 131104 | tf_op jit(solution)/shard_map/ppermute | solution.py:254
  15.3 2.7 %collective-permute-start.6 = (bf16[128,512]{1,0:T(8,128)(2,1)S(1)}, bf16[128,512]{1,0:T(8,128)(2,1)S(1)}, u32[]{:S(2)}, u32[]{:S(2)}) collective-permute-start(bf16[128,512]{1,0:T(8,128)(2,1)S(1)} %copy-done.16), channel_id=1, source_target_pairs={{0,3},{1,2},{2,1},{3,0},{4,7},{5,6},{6,5},{7,4},{8,11},{9,10},{10,... | collective-permute-start | bytes 393224 | tf_op jit(solution)/shard_map/ppermute | solution.py:254
  18.1 3.6 %collective-permute-done.9 = bf16[2,128,512]{2,1,0:T(8,128)(2,1)S(1)} collective-permute-done((bf16[2,128,512]{2,1,0:T(8,128)(2,1)}, bf16[2,128,512]{2,1,0:T(8,128)(2,1)S(1)}, u32[]{:S(2)}, u32[]{:S(2)}) %collective-permute-start.9) | collective-permute-done | bytes 262176 | tf_op jit(solution)/shard_map/ppermute | solution.py:254
  21.7 4.2 %conditional.3 = (bf16[2,128,512]{2,1,0:T(8,128)(2,1)}, bf16[2,128,512]{2,1,0:T(8,128)(2,1)}, bf16[256,256]{1,0:T(8,128)(2,1)S(1)}) conditional(s32[]{:T(128)} %convert_element_type.37, () %tuple.35, (s32[4]{0:T(128)S(1)}, bf16[512,512]{1,0:T(8,128)(2,1)S(1)}, bf16[256,512]{1,0:T(8,128)(2,1)S(1)}, bf16[256,256]{1,0:T(8,128)(2,1)S(1)}, ...), branch_computations={%region_0.0_spmd, %region_1.0_spmd} | conditional | flops 537133056 | bytes 9306176 | solution.py:261
  21.7 2.8 %branch_1_fun.2 = (bf16[2,128,512]{2,1,0:T(8,128)(2,1)}, bf16[2,128,512]{2,1,0:T(8,128)(2,1)}, bf16[256,256]{1,0:T(8,128)(2,1)S(1)}, bf16[256,256]{1,0:T(8,128)(2,1)S(1)}) custom-call(s32[4]{0:T(128)S(1)} %get-tuple-element.44.idx, bf16[512,512]{1,0:T(8,128)(2,1)S(1)} %get-tuple-element.45.table, bf16[256,512]{1,0:T(8,128)(2,1)S(1)} %get-tuple-element.46.inv, ...), custom_call_target="tpu_custom_call" | custom-call | flops 536870912 | bytes 8388608 | tf_op jit(solution)/shard_map/cond/branch_1_fun/pallas_call | solution.py:294
  24.6 1.3 %collective-permute-done = bf16[256,256]{1,0:T(8,128)(2,1)S(1)} collective-permute-done((bf16[256,256]{1,0:T(8,128)(2,1)S(1)}, bf16[256,256]{1,0:T(8,128)(2,1)S(1)}, u32[]{:S(2)}, u32[]{:S(2)}) %collective-permute-start) | collective-permute-done | bytes 131104 | tf_op jit(solution)/shard_map/cond/branch_1_fun/ppermute | solution.py:257
  26.2 1.2 %shard_map.96 = (bf16[128,512]{1,0:T(8,128)(2,1)S(1)}, bf16[128,512]{1,0:T(8,128)(2,1)S(1)}) custom-call(s32[4]{0:T(128)S(1)} %pad_add_fusion.idx, bf16[512,512]{1,0:T(8,128)(2,1)S(1)} %copy-done.4, bf16[256,512]{1,0:T(8,128)(2,1)S(1)} %get-tuple-element.111.inv, bf16[512,512]{1,0:T(8,128)(2,1)S(1)} %get-tuple-element.118.cross, ...), custom_call_target="tpu_custom_call" | custom-call | flops 268435456 | bytes 2097152 | tf_op jit(solution)/shard_map/pallas_call | solution.py:308
  27.5 2.8 %collective-permute-start.13 = (bf16[128,512]{1,0:T(8,128)(2,1)S(1)}, bf16[128,512]{1,0:T(8,128)(2,1)S(1)}, u32[]{:S(2)}, u32[]{:S(2)}) collective-permute-start(bf16[128,512]{1,0:T(8,128)(2,1)S(1)} %get-tuple-element.128), channel_id=1, source_target_pairs={{0,2},{1,3},{2,0},{3,1},{4,6},{5,7},{6,4},{7,5},{8,10},{9,11},{10,... | collective-permute-start | bytes 393224 | tf_op jit(solution)/shard_map/ppermute | solution.py:254
  30.3 1.6 %collective-permute-start.14 = (bf16[128,512]{1,0:T(8,128)(2,1)S(1)}, bf16[128,512]{1,0:T(8,128)(2,1)S(1)}, u32[]{:S(2)}, u32[]{:S(2)}) collective-permute-start(bf16[128,512]{1,0:T(8,128)(2,1)S(1)} %get-tuple-element.129), channel_id=1, source_target_pairs={{0,3},{1,2},{2,1},{3,0},{4,7},{5,6},{6,5},{7,4},{8,11},{9,10},{10,... | collective-permute-start | bytes 393224 | tf_op jit(solution)/shard_map/ppermute | solution.py:254
  31.9 2.5 %shard_map.95 = (bf16[256,512]{1,0:T(8,128)(2,1)S(1)}, bf16[256,512]{1,0:T(8,128)(2,1)S(1)}) custom-call(s32[4]{0:T(128)S(1)} %pad_add_fusion.idx, bf16[128,512]{1,0:T(8,128)(2,1)S(1)} %collective-permute-done.5.r2, bf16[128,512]{1,0:T(8,128)(2,1)S(1)} %collective-permute-done.6.r3, bf16[512,512]{1,0:T(8,128)(2,1)S(1)} %copy-done.4, ...), custom_call_target="tpu_custom_call" | custom-call | flops 3221225472 | bytes 8388608 | tf_op jit(solution)/shard_map/pallas_call | solution.py:312
  35.6 15.1 %conditional.4 = (bf16[2,128,512]{2,1,0:T(8,128)(2,1)}, bf16[2,128,512]{2,1,0:T(8,128)(2,1)}, bf16[256,512]{1,0:T(8,128)(2,1)}, bf16[256,512]{1,0:T(8,128)(2,1)}) conditional(s32[]{:T(128)} %convert_element_type.37, () %tuple.33, (s32[4]{0:T(128)S(1)}, bf16[128,512]{1,0:T(8,128)(2,1)S(1)}, bf16[128,512]{1,0:T(8,128)(2,1)}, ...), branch_computations={%region_2.0_spmd, %region_3.0_spmd} | conditional | flops 269877248 | bytes 11665730 | solution.py:261
  35.7 1.5 %collective-permute-done.3 = bf16[256,512]{1,0:T(8,128)(2,1)S(1)} collective-permute-done((bf16[256,512]{1,0:T(8,128)(2,1)S(1)}, bf16[256,512]{1,0:T(8,128)(2,1)S(1)}, u32[]{:S(2)}, u32[]{:S(2)}) %collective-permute-start.3) | collective-permute-done | bytes 262176 | tf_op jit(solution)/shard_map/cond/branch_1_fun/ppermute | solution.py:257
  37.4 1.7 %collective-permute-start.4 = (bf16[256,512]{1,0:T(8,128)(2,1)S(1)}, bf16[256,512]{1,0:T(8,128)(2,1)}, u32[]{:S(2)}, u32[]{:S(2)}) collective-permute-start(bf16[256,512]{1,0:T(8,128)(2,1)S(1)} %fusion), channel_id=1, source_target_pairs={{0,16},{8,24},{16,0},{24,8},{1,17},{9,25},{17,1},{25,9},{2,18},{10... | collective-permute-start | bytes 786440 | tf_op jit(solution)/shard_map/cond/branch_1_fun/ppermute | solution.py:257
  39.1 3.3 %branch_1_fun.3 = (bf16[2,128,512]{2,1,0:T(8,128)(2,1)}, bf16[2,128,512]{2,1,0:T(8,128)(2,1)S(1)}) custom-call(s32[4]{0:T(128)S(1)} %get-tuple-element.57.idx, bf16[128,512]{1,0:T(8,128)(2,1)S(1)} %get-tuple-element.58.r2, bf16[128,512]{1,0:T(8,128)(2,1)S(1)} %copy-done.15, bf16[512,512]{1,0:T(8,128)(2,1)S(1)} %get-tuple-element.60.table, ...), custom_call_target="tpu_custom_call" | custom-call | flops 268435456 | bytes 1048576 | tf_op jit(solution)/shard_map/cond/branch_1_fun/pallas_call | solution.py:328
  43.4 2.6 %collective-permute-done.4 = bf16[256,512]{1,0:T(8,128)(2,1)} collective-permute-done((bf16[256,512]{1,0:T(8,128)(2,1)S(1)}, bf16[256,512]{1,0:T(8,128)(2,1)}, u32[]{:S(2)}, u32[]{:S(2)}) %collective-permute-start.4) | collective-permute-done | bytes 262176 | tf_op jit(solution)/shard_map/cond/branch_1_fun/ppermute | solution.py:257
  45.9 3.6 %conditional = (bf16[256,512]{1,0:T(8,128)(2,1)}, bf16[256,512]{1,0:T(8,128)(2,1)}) conditional(s32[]{:T(128)} %convert_element_type.31, () %tuple.23, (bf16[256,512]{1,0:T(8,128)(2,1)S(1)}, bf16[256,512]{1,0:T(8,128)(2,1)}) %tuple.24), branch_computations={%region_4.0_spmd, %region_5.0_spmd} | conditional | flops 524288 | bytes 1835064 | solution.py:261
  45.9 1.7 %add_convert_fusion.1 = bf16[256,512]{1,0:T(8,128)(2,1)} fusion(bf16[256,512]{1,0:T(8,128)(2,1)} %get-tuple-element.56, bf16[256,512]{1,0:T(8,128)(2,1)S(1)} %get-tuple-element.55), kind=kLoop, calls=%fused_computation.1 | loop fusion | flops 524288 | bytes 786432 | tf_op jit(solution)/shard_map/cond/branch_1_fun/cond/branch_1_fun/convert_element_type | solution.py:340
  47.6 1.9 %collective-permute-done.1 = bf16[256,512]{1,0:T(8,128)(2,1)} collective-permute-done((bf16[256,512]{1,0:T(8,128)(2,1)}, bf16[256,512]{1,0:T(8,128)(2,1)}, u32[]{:S(2)}, u32[]{:S(2)}) %collective-permute-start.1) | collective-permute-done | bytes 262176 | tf_op jit(solution)/shard_map/cond/branch_1_fun/cond/branch_1_fun/ppermute | solution.py:257
  49.5 1.1 %collective-permute-done.2 = bf16[2,128,512]{2,1,0:T(8,128)(2,1)} collective-permute-done((bf16[2,128,512]{2,1,0:T(8,128)(2,1)S(1)}, bf16[2,128,512]{2,1,0:T(8,128)(2,1)}, u32[]{:S(2)}, u32[]{:S(2)}) %collective-permute-start.2) | collective-permute-done | bytes 262176 | tf_op jit(solution)/shard_map/cond/branch_1_fun/ppermute | solution.py:254
  50.7 2.9 %shard_map.97 = (bf16[1,128,2048]{2,1,0:T(8,128)(2,1)}, bf16[1,128,2048]{2,1,0:T(8,128)(2,1)}, bf16[1,128,2048]{2,1,0:T(8,128)(2,1)}, f32[512,512]{1,0:T(8,128)}) custom-call(s32[4]{0:T(128)S(1)} %pad_add_fusion.idx, bf16[1,128,2048]{2,1,0:T(8,128)(2,1)S(1)} %copy-done.1, bf16[1,128,2048]{2,1,0:T(8,128)(2,1)S(1)} %copy-done.2, ...), custom_call_target="tpu_custom_call" | custom-call | flops 786432 | bytes 4718592 | tf_op jit(solution)/shard_map/pallas_call | solution.py:349
  (58 shorter events, 4.1 us)
Async XLA Ops:
  0.7 9.2 %copy-start = (f32[512,512]{1,0:T(8,128)S(1)}, f32[512,512]{1,0:T(8,128)}, u32[]{:S(2)}) copy-start(f32[512,512]{1,0:T(8,128)} %taps.3) | copy-start | bytes 3145732
  0.7 9.2 %copy-start.4 = (bf16[512,512]{1,0:T(8,128)(2,1)S(1)}, bf16[512,512]{1,0:T(8,128)(2,1)}, u32[]{:S(2)}) copy-start(bf16[512,512]{1,0:T(8,128)(2,1)} %constant.15.clone.table) | copy-start | bytes 1572868
  3.8 28.1 %copy-start.7 = (bf16[2,128,512]{2,1,0:T(8,128)(2,1)}, bf16[2,128,512]{2,1,0:T(8,128)(2,1)S(1)}, u32[]{:S(2)}) copy-start(bf16[2,128,512]{2,1,0:T(8,128)(2,1)S(1)} %get-tuple-element.119.keep) | copy-start | bytes 786436
  3.8 10.7 %collective-permute-start.7 = (bf16[256,256]{1,0:T(8,128)(2,1)}, bf16[256,256]{1,0:T(8,128)(2,1)S(1)}, u32[]{:S(2)}, u32[]{:S(2)}) collective-permute-start(bf16[256,256]{1,0:T(8,128)(2,1)} %get-tuple-element.110), channel_id=1, source_target_pairs={{0,2},{1,3},{2,0},{3,1},{4,6},{5,7},{6,4},{7,5},{8,10},{9,11},{10,... | collective-permute-start | bytes 393224 | tf_op jit(solution)/shard_map/ppermute | solution.py:254
  7.8 13.9 %collective-permute-start.9 = (bf16[2,128,512]{2,1,0:T(8,128)(2,1)}, bf16[2,128,512]{2,1,0:T(8,128)(2,1)S(1)}, u32[]{:S(2)}, u32[]{:S(2)}) collective-permute-start(bf16[2,128,512]{2,1,0:T(8,128)(2,1)} %get-tuple-element.115), channel_id=1, source_target_pairs={{0,1},{1,0},{2,3},{3,2},{4,5},{5,4},{6,7},{7,6},{8,9},{9,8},{10,11... | collective-permute-start | bytes 786440 | tf_op jit(solution)/shard_map/ppermute | solution.py:254
  9.4 5.9 %copy-start.16 = (bf16[128,512]{1,0:T(8,128)(2,1)S(1)}, bf16[128,512]{1,0:T(8,128)(2,1)}, u32[]{:S(2)}) copy-start(bf16[128,512]{1,0:T(8,128)(2,1)} %get-tuple-element.106) | copy-start | bytes 393220
  9.4 16.8 %collective-permute-start.10 = (bf16[2,128,512]{2,1,0:T(8,128)(2,1)}, bf16[2,128,512]{2,1,0:T(8,128)(2,1)S(1)}, u32[]{:S(2)}, u32[]{:S(2)}) collective-permute-start(bf16[2,128,512]{2,1,0:T(8,128)(2,1)} %get-tuple-element.120), channel_id=1, source_target_pairs={{0,1},{1,0},{2,3},{3,2},{4,5},{5,4},{6,7},{7,6},{8,9},{9,8},{10,11... | collective-permute-start | bytes 786440 | tf_op jit(solution)/shard_map/ppermute | solution.py:254
  11.3 15.0 %copy-start.5 = (bf16[512,512]{1,0:T(8,128)(2,1)}, bf16[512,512]{1,0:T(8,128)(2,1)S(1)}, u32[]{:S(2)}) copy-start(bf16[512,512]{1,0:T(8,128)(2,1)S(1)} %get-tuple-element.118.cross) | copy-start | bytes 1572868
  11.3 15.0 %copy-start.11 = (bf16[256,512]{1,0:T(8,128)(2,1)}, bf16[256,512]{1,0:T(8,128)(2,1)S(1)}, u32[]{:S(2)}) copy-start(bf16[256,512]{1,0:T(8,128)(2,1)S(1)} %get-tuple-element.111.inv) | copy-start | bytes 786436
  14.5 3.6 %collective-permute-start.8 = (bf16[256,256]{1,0:T(8,128)(2,1)S(1)}, bf16[256,256]{1,0:T(8,128)(2,1)S(1)}, u32[]{:S(2)}, u32[]{:S(2)}) collective-permute-start(bf16[256,256]{1,0:T(8,128)(2,1)S(1)} %collective-permute-done.7), channel_id=1, source_target_pairs={{0,8},{8,0},{16,24},{24,16},{1,9},{9,1},{17,25},{25,17},{2,10},{10... | collective-permute-start | bytes 393224 | tf_op jit(solution)/shard_map/ppermute | solution.py:257
  14.5 15.8 %collective-permute-start.5 = (bf16[128,512]{1,0:T(8,128)(2,1)S(1)}, bf16[128,512]{1,0:T(8,128)(2,1)S(1)}, u32[]{:S(2)}, u32[]{:S(2)}) collective-permute-start(bf16[128,512]{1,0:T(8,128)(2,1)S(1)} %copy-done.17), channel_id=1, source_target_pairs={{0,2},{1,3},{2,0},{3,1},{4,6},{5,7},{6,4},{7,5},{8,10},{9,11},{10,... | collective-permute-start | bytes 393224 | tf_op jit(solution)/shard_map/ppermute | solution.py:254
  15.3 16.5 %collective-permute-start.6 = (bf16[128,512]{1,0:T(8,128)(2,1)S(1)}, bf16[128,512]{1,0:T(8,128)(2,1)S(1)}, u32[]{:S(2)}, u32[]{:S(2)}) collective-permute-start(bf16[128,512]{1,0:T(8,128)(2,1)S(1)} %copy-done.16), channel_id=1, source_target_pairs={{0,3},{1,2},{2,1},{3,0},{4,7},{5,6},{6,5},{7,4},{8,11},{9,10},{10,... | collective-permute-start | bytes 393224 | tf_op jit(solution)/shard_map/ppermute | solution.py:254
  24.6 1.3 %collective-permute-start = (bf16[256,256]{1,0:T(8,128)(2,1)S(1)}, bf16[256,256]{1,0:T(8,128)(2,1)S(1)}, u32[]{:S(2)}, u32[]{:S(2)}) collective-permute-start(bf16[256,256]{1,0:T(8,128)(2,1)S(1)} %get-tuple-element.54), channel_id=1, source_target_pairs={{0,8},{8,0},{16,24},{24,16},{1,9},{9,1},{17,25},{25,17},{2,10},{10... | collective-permute-start | bytes 393224 | tf_op jit(solution)/shard_map/cond/branch_1_fun/ppermute | solution.py:257
  25.9 9.6 %collective-permute-start.11 = (bf16[256,256]{1,0:T(8,128)(2,1)S(1)}, bf16[256,256]{1,0:T(8,128)(2,1)S(1)}, u32[]{:S(2)}, u32[]{:S(2)}) collective-permute-start(bf16[256,256]{1,0:T(8,128)(2,1)S(1)} %get-tuple-element.123), channel_id=1, source_target_pairs={{0,2},{1,3},{2,0},{3,1},{4,6},{5,7},{6,4},{7,5},{8,10},{9,11},{10,... | collective-permute-start | bytes 393224 | tf_op jit(solution)/shard_map/ppermute | solution.py:254
  26.0 24.6 %collective-permute-start.12 = (bf16[2,128,512]{2,1,0:T(8,128)(2,1)}, bf16[2,128,512]{2,1,0:T(8,128)(2,1)S(1)}, u32[]{:S(2)}, u32[]{:S(2)}) collective-permute-start(bf16[2,128,512]{2,1,0:T(8,128)(2,1)} %get-tuple-element.127), channel_id=1, source_target_pairs={{0,1},{1,0},{2,3},{3,2},{4,5},{5,4},{6,7},{7,6},{8,9},{9,8},{10,11... | collective-permute-start | bytes 786440 | tf_op jit(solution)/shard_map/ppermute | solution.py:254
  27.5 23.2 %collective-permute-start.13 = (bf16[128,512]{1,0:T(8,128)(2,1)S(1)}, bf16[128,512]{1,0:T(8,128)(2,1)S(1)}, u32[]{:S(2)}, u32[]{:S(2)}) collective-permute-start(bf16[128,512]{1,0:T(8,128)(2,1)S(1)} %get-tuple-element.128), channel_id=1, source_target_pairs={{0,2},{1,3},{2,0},{3,1},{4,6},{5,7},{6,4},{7,5},{8,10},{9,11},{10,... | collective-permute-start | bytes 393224 | tf_op jit(solution)/shard_map/ppermute | solution.py:254
  30.3 20.4 %collective-permute-start.14 = (bf16[128,512]{1,0:T(8,128)(2,1)S(1)}, bf16[128,512]{1,0:T(8,128)(2,1)S(1)}, u32[]{:S(2)}, u32[]{:S(2)}) collective-permute-start(bf16[128,512]{1,0:T(8,128)(2,1)S(1)} %get-tuple-element.129), channel_id=1, source_target_pairs={{0,3},{1,2},{2,1},{3,0},{4,7},{5,6},{6,5},{7,4},{8,11},{9,10},{10,... | collective-permute-start | bytes 393224 | tf_op jit(solution)/shard_map/ppermute | solution.py:254
  35.5 15.1 %copy-start.1 = (bf16[1,128,2048]{2,1,0:T(8,128)(2,1)S(1)}, bf16[1,128,2048]{2,1,0:T(8,128)(2,1)}, u32[]{:S(2)}) copy-start(bf16[1,128,2048]{2,1,0:T(8,128)(2,1)} %q.3) | copy-start | bytes 1572868
  35.6 15.1 %copy-start.2 = (bf16[1,128,2048]{2,1,0:T(8,128)(2,1)S(1)}, bf16[1,128,2048]{2,1,0:T(8,128)(2,1)}, u32[]{:S(2)}) copy-start(bf16[1,128,2048]{2,1,0:T(8,128)(2,1)} %k.3) | copy-start | bytes 1572868
  35.6 15.1 %copy-start.3 = (bf16[1,128,2048]{2,1,0:T(8,128)(2,1)S(1)}, bf16[1,128,2048]{2,1,0:T(8,128)(2,1)}, u32[]{:S(2)}) copy-start(bf16[1,128,2048]{2,1,0:T(8,128)(2,1)} %g.3) | copy-start | bytes 1572868
  35.6 1.6 %collective-permute-start.3 = (bf16[256,512]{1,0:T(8,128)(2,1)S(1)}, bf16[256,512]{1,0:T(8,128)(2,1)S(1)}, u32[]{:S(2)}, u32[]{:S(2)}) collective-permute-start(bf16[256,512]{1,0:T(8,128)(2,1)S(1)} %get-tuple-element.70), channel_id=1, source_target_pairs={{0,8},{8,0},{16,24},{24,16},{1,9},{9,1},{17,25},{25,17},{2,10},{10... | collective-permute-start | bytes 786440 | tf_op jit(solution)/shard_map/cond/branch_1_fun/ppermute | solution.py:257
  37.4 8.5 %collective-permute-start.4 = (bf16[256,512]{1,0:T(8,128)(2,1)S(1)}, bf16[256,512]{1,0:T(8,128)(2,1)}, u32[]{:S(2)}, u32[]{:S(2)}) collective-permute-start(bf16[256,512]{1,0:T(8,128)(2,1)S(1)} %fusion), channel_id=1, source_target_pairs={{0,16},{8,24},{16,0},{24,8},{1,17},{9,25},{17,1},{25,9},{2,18},{10... | collective-permute-start | bytes 786440 | tf_op jit(solution)/shard_map/cond/branch_1_fun/ppermute | solution.py:257
  42.4 8.2 %collective-permute-start.2 = (bf16[2,128,512]{2,1,0:T(8,128)(2,1)S(1)}, bf16[2,128,512]{2,1,0:T(8,128)(2,1)}, u32[]{:S(2)}, u32[]{:S(2)}) collective-permute-start(bf16[2,128,512]{2,1,0:T(8,128)(2,1)S(1)} %get-tuple-element.67), channel_id=1, source_target_pairs={{0,1},{1,0},{2,3},{3,2},{4,5},{5,4},{6,7},{7,6},{8,9},{9,8},{10,11... | collective-permute-start | bytes 786440 | tf_op jit(solution)/shard_map/cond/branch_1_fun/ppermute | solution.py:254
  47.6 1.9 %collective-permute-start.1 = (bf16[256,512]{1,0:T(8,128)(2,1)}, bf16[256,512]{1,0:T(8,128)(2,1)}, u32[]{:S(2)}, u32[]{:S(2)}) collective-permute-start(bf16[256,512]{1,0:T(8,128)(2,1)} %add_convert_fusion.1), channel_id=1, source_target_pairs={{0,8},{8,0},{16,24},{24,16},{1,9},{9,1},{17,25},{25,17},{2,10},{10... | collective-permute-start | bytes 786440 | tf_op jit(solution)/shard_map/cond/branch_1_fun/cond/branch_1_fun/ppermute | solution.py:257
  (9 other events, 34.2 us)

commit v5 on v4

--- a/solution.py
+++ b/solution.py
@@ -99,6 +99,12 @@
     return held[...]
 
 
+def forward_two(fwd, first, second):
+    both = mm(fwd, jnp.concatenate([first, second], 1))
+    width = first.shape[1]
+    return both[:, :width], both[:, width:]
+
+
 def halves(low, vals, held, mine, partner):
     held[...] = vals
     block = vals.shape[0] // 2
@@ -121,8 +127,7 @@
     half = table.shape[1] // 2
     share = mine.shape[0]
     fwd = table[:, half:]
-    x = mm(fwd, in_order(low, keep[0], recv[0], held.at[0]))
-    g = mm(fwd, in_order(low, keep[1], recv[1], held.at[1]))
+    x, g = forward_two(fwd, in_order(low, keep[0], recv[0], held.at[0]), in_order(low, keep[1], recv[1], held.at[1]))
     for which, piece in ((core, mine), (1 - core, other)):
         filt[:, lanes(which * share, share)] = mm(fwd, piece[...], ((1,), (1,)))
     h = filt[...]
@@ -157,8 +162,7 @@
     half = table.shape[1] // 2
     loads = load_blocks(low, r2, r3, held.at[2], sems)
     fwd = table[:, half:]
-    x = mm(fwd, in_order(low, keep[0], recv[0], held.at[0]))
-    g = mm(fwd, in_order(low, keep[1], recv[1], held.at[1]))
+    x, g = forward_two(fwd, in_order(low, keep[0], recv[0], held.at[0]), in_order(low, keep[1], recv[1], held.at[1]))
     q_near[...] = join(cmulc(x, g)).astype(bf16)
     for load in loads:
         load.wait()
@@ -180,27 +184,27 @@
     half = table.shape[1] // 2
     loads = load_blocks(low, r2, r3, held.at[2], sems)
     fwd = table[:, half:]
-    x = mm(fwd, in_order(low, keep[0], recv[0], held.at[0]))
-    g = mm(fwd, in_order(low, keep[1], recv[1], held.at[1]))
+    x, g = forward_two(fwd, in_order(low, keep[0], recv[0], held.at[0]), in_order(low, keep[1], recv[1], held.at[1]))
     h = near[...].astype(f32)
     hx = cross[...].astype(f32)
     for load in loads:
         load.wait()
     rec = mm(fwd, held[2])
 
-    def put(kind, pair):
-        vals = mm(inv[...], join(pair).astype(bf16)).astype(bf16)
-        halves(low, vals, held.at[3 + kind], okeep.at[kind], o1.at[kind])
+    def put(conv, back):
+        width = x.shape[1]
+        both = jnp.concatenate([join(conv).astype(bf16), join(back).astype(bf16)], 1)
+        vals = mm(inv[...], both).astype(bf16)
+        halves(low, vals[:, :width], held.at[3], okeep.at[0], o1.at[0])
+        halves(low, vals[:, width:], held.at[4], okeep.at[1], o1.at[1])
 
     def lower():
-        put(0, cmul(x, h))
         back, add = cmulc(h, g), cmulc(hx, rec)
-        put(1, (back[0] + add[0], back[1] + add[1]))
+        put(cmul(x, h), (back[0] + add[0], back[1] + add[1]))
 
     def higher():
         conv, add = cmul(x, h), cmul(hx, rec)
-        put(0, (conv[0] + add[0], conv[1] + add[1]))
-        put(1, cmulc(h, g))
+        put((conv[0] + add[0], conv[1] + add[1]), cmulc(h, g))
 
     pl.when(upper == 0)(lower)
     pl.when(upper != 0)(higher)

time: 53.8 us -> 53.8 us (level)
  no operation moved by 1% of the time
where the time goes in v5:
time: 53.8 us; the launch traced here: 53.6 us
  Pallas kernels  17.3 us (32%)
  starting transfers between devices  17 us (32%)
  waiting for transfers between devices  16.3 us (30%)
  other arithmetic  1.98 us (4%)
  between operations  0.77 us (1%)
    ppermute x10, starting transfers between devices, xz(): return lax.ppermute(vals, 'ctx', [(i, i ^ k) for i in range(4)])  15.3 us
    ppermute x10, waiting for transfers between devices, xz(): return lax.ppermute(vals, 'ctx', [(i, i ^ k) for i in range(4)])  9.04 us
    ppermute x5, waiting for transfers between devices, xd(): return lax.ppermute(vals, 'dp', [(i, i ^ k) for i in range(4)])  7.3 us
    pallas_call x1, Pallas kernels, own_quarter(): call(conv_own_kernel, [two] * 2, 8, in_hbm=2, cost=(4 * macs, 4 * length...  3.34 us
    pallas_call x1, Pallas kernels, half_plan(): pl.pallas_call(functools.partial(gate_kernel, quarter), out_shape=[jax.Sh...  3.08 us
    pallas_call x1, Pallas kernels, half_plan(): call(functools.partial(final_kernel, quarter), [act] * 3 + [(filter_taps....  2.89 us
    pallas_call x1, Pallas kernels, far_quarter(): call(conv_far_kernel, [two] * 2 + [((rows, half), bf16)] * 2, 6, cost=(8...  2.83 us
    pallas_call x1, Pallas kernels, half_plan(): call(own_filter_grad_kernel, [((rows, length), bf16)] * 2, 5, in_hbm=2, c...  2.54 us
  transfers between devices with their start and end apart: 15, of which 8 were waited for; matrix products, arithmetic and copies ran while one was open for 4% of the time, Pallas kernels for 21%

profile of v5, /device:TPU:0, one launch (start us, length us, event | category | flops | bytes accessed | tf_op | source)
XLA Modules:
  0.0 53.6 jit_solution(17868852871790240352)
XLA Ops:
  0.7 3.1 %shard_map.93 = (bf16[2,128,512]{2,1,0:T(8,128)(2,1)S(1)}, bf16[2,128,512]{2,1,0:T(8,128)(2,1)S(1)}, bf16[2,128,512]{2,1,0:T(8,128)(2,1)}, bf16[2,128,512]{2,1,0...) custom-call(s32[4]{0:T(128)S(1)} %pad_add_fusion.idx, ...), custom_call_target="tpu_custom_call" | custom-call | flops 524288 | bytes 4194304 | tf_op jit(solution)/shard_map/pallas_call | solution.py:277
  3.8 4.0 %collective-permute-start.7 = (bf16[256,256]{1,0:T(8,128)(2,1)}, bf16[256,256]{1,0:T(8,128)(2,1)S(1)}, u32[]{:S(2)}, u32[]{:S(2)}) collective-permute-start(bf16[256,256]{1,0:T(8,128)(2,1)} %get-tuple-element.110), channel_id=1, source_target_pairs={{0,2},{1,3},{2,0},{3,1},{4,6},{5,7},{6,4},{7,5},{8,10},{9,11},{10,... | collective-permute-start | bytes 393224 | tf_op jit(solution)/shard_map/ppermute | solution.py:258
  7.8 1.6 %collective-permute-start.9 = (bf16[2,128,512]{2,1,0:T(8,128)(2,1)}, bf16[2,128,512]{2,1,0:T(8,128)(2,1)S(1)}, u32[]{:S(2)}, u32[]{:S(2)}) collective-permute-start(bf16[2,128,512]{2,1,0:T(8,128)(2,1)} %get-tuple-element.115), channel_id=1, source_target_pairs={{0,1},{1,0},{2,3},{3,2},{4,5},{5,4},{6,7},{7,6},{8,9},{9,8},{10,11... | collective-permute-start | bytes 786440 | tf_op jit(solution)/shard_map/ppermute | solution.py:258
  9.9 1.4 %shard_map.94 = (bf16[512,512]{1,0:T(8,128)(2,1)}, bf16[512,512]{1,0:T(8,128)(2,1)S(1)}, bf16[256,512]{1,0:T(8,128)(2,1)S(1)}) custom-call(bf16[512,512]{1,0:T(8,128)(2,1)S(1)} %copy-done.4, f32[512,512]{1,0:T(8,128)S(1)} %copy-done), custom_call_target="tpu_custom_call" | custom-call | flops 402653184 | bytes 4194304 | tf_op jit(solution)/shard_map/pallas_call | solution.py:290
  11.3 3.2 %collective-permute-done.7 = bf16[256,256]{1,0:T(8,128)(2,1)S(1)} collective-permute-done((bf16[256,256]{1,0:T(8,128)(2,1)}, bf16[256,256]{1,0:T(8,128)(2,1)S(1)}, u32[]{:S(2)}, u32[]{:S(2)}) %collective-permute-start.7) | collective-permute-done | bytes 131104 | tf_op jit(solution)/shard_map/ppermute | solution.py:258
  15.3 2.7 %collective-permute-start.6 = (bf16[128,512]{1,0:T(8,128)(2,1)S(1)}, bf16[128,512]{1,0:T(8,128)(2,1)S(1)}, u32[]{:S(2)}, u32[]{:S(2)}) collective-permute-start(bf16[128,512]{1,0:T(8,128)(2,1)S(1)} %copy-done.16), channel_id=1, source_target_pairs={{0,3},{1,2},{2,1},{3,0},{4,7},{5,6},{6,5},{7,4},{8,11},{9,10},{10,... | collective-permute-start | bytes 393224 | tf_op jit(solution)/shard_map/ppermute | solution.py:258
  18.1 3.6 %collective-permute-done.9 = bf16[2,128,512]{2,1,0:T(8,128)(2,1)S(1)} collective-permute-done((bf16[2,128,512]{2,1,0:T(8,128)(2,1)}, bf16[2,128,512]{2,1,0:T(8,128)(2,1)S(1)}, u32[]{:S(2)}, u32[]{:S(2)}) %collective-permute-start.9) | collective-permute-done | bytes 262176 | tf_op jit(solution)/shard_map/ppermute | solution.py:258
  21.7 4.2 %conditional.3 = (bf16[2,128,512]{2,1,0:T(8,128)(2,1)}, bf16[2,128,512]{2,1,0:T(8,128)(2,1)}, bf16[256,256]{1,0:T(8,128)(2,1)S(1)}) conditional(s32[]{:T(128)} %convert_element_type.37, () %tuple.35, (s32[4]{0:T(128)S(1)}, bf16[512,512]{1,0:T(8,128)(2,1)S(1)}, bf16[256,512]{1,0:T(8,128)(2,1)S(1)}, bf16[256,256]{1,0:T(8,128)(2,1)S(1)}, ...), branch_computations={%region_0.0_spmd, %region_1.0_spmd} | conditional | flops 537133056 | bytes 9306176 | solution.py:265
  21.7 2.8 %branch_1_fun.2 = (bf16[2,128,512]{2,1,0:T(8,128)(2,1)}, bf16[2,128,512]{2,1,0:T(8,128)(2,1)}, bf16[256,256]{1,0:T(8,128)(2,1)S(1)}, bf16[256,256]{1,0:T(8,128)(2,1)S(1)}) custom-call(s32[4]{0:T(128)S(1)} %get-tuple-element.44.idx, bf16[512,512]{1,0:T(8,128)(2,1)S(1)} %get-tuple-element.45.table, bf16[256,512]{1,0:T(8,128)(2,1)S(1)} %get-tuple-element.46.inv, ...), custom_call_target="tpu_custom_call" | custom-call | flops 536870912 | bytes 8388608 | tf_op jit(solution)/shard_map/cond/branch_1_fun/pallas_call | solution.py:298
  24.6 1.3 %collective-permute-done = bf16[256,256]{1,0:T(8,128)(2,1)S(1)} collective-permute-done((bf16[256,256]{1,0:T(8,128)(2,1)S(1)}, bf16[256,256]{1,0:T(8,128)(2,1)S(1)}, u32[]{:S(2)}, u32[]{:S(2)}) %collective-permute-start) | collective-permute-done | bytes 131104 | tf_op jit(solution)/shard_map/cond/branch_1_fun/ppermute | solution.py:261
  26.2 1.2 %shard_map.96 = (bf16[128,512]{1,0:T(8,128)(2,1)S(1)}, bf16[128,512]{1,0:T(8,128)(2,1)S(1)}) custom-call(s32[4]{0:T(128)S(1)} %pad_add_fusion.idx, bf16[512,512]{1,0:T(8,128)(2,1)S(1)} %copy-done.4, bf16[256,512]{1,0:T(8,128)(2,1)S(1)} %get-tuple-element.111.inv, bf16[512,512]{1,0:T(8,128)(2,1)S(1)} %get-tuple-element.118.cross, ...), custom_call_target="tpu_custom_call" | custom-call | flops 268435456 | bytes 2097152 | tf_op jit(solution)/shard_map/pallas_call | solution.py:312
  27.5 2.8 %collective-permute-start.13 = (bf16[128,512]{1,0:T(8,128)(2,1)S(1)}, bf16[128,512]{1,0:T(8,128)(2,1)S(1)}, u32[]{:S(2)}, u32[]{:S(2)}) collective-permute-start(bf16[128,512]{1,0:T(8,128)(2,1)S(1)} %get-tuple-element.128), channel_id=1, source_target_pairs={{0,2},{1,3},{2,0},{3,1},{4,6},{5,7},{6,4},{7,5},{8,10},{9,11},{10,... | collective-permute-start | bytes 393224 | tf_op jit(solution)/shard_map/ppermute | solution.py:258
  30.3 1.6 %collective-permute-start.14 = (bf16[128,512]{1,0:T(8,128)(2,1)S(1)}, bf16[128,512]{1,0:T(8,128)(2,1)S(1)}, u32[]{:S(2)}, u32[]{:S(2)}) collective-permute-start(bf16[128,512]{1,0:T(8,128)(2,1)S(1)} %get-tuple-element.129), channel_id=1, source_target_pairs={{0,3},{1,2},{2,1},{3,0},{4,7},{5,6},{6,5},{7,4},{8,11},{9,10},{10,... | collective-permute-start | bytes 393224 | tf_op jit(solution)/shard_map/ppermute | solution.py:258
  31.9 2.5 %shard_map.95 = (bf16[256,512]{1,0:T(8,128)(2,1)S(1)}, bf16[256,512]{1,0:T(8,128)(2,1)S(1)}) custom-call(s32[4]{0:T(128)S(1)} %pad_add_fusion.idx, bf16[128,512]{1,0:T(8,128)(2,1)S(1)} %collective-permute-done.5.r2, bf16[128,512]{1,0:T(8,128)(2,1)S(1)} %collective-permute-done.6.r3, bf16[512,512]{1,0:T(8,128)(2,1)S(1)} %copy-done.4, ...), custom_call_target="tpu_custom_call" | custom-call | flops 3221225472 | bytes 8388608 | tf_op jit(solution)/shard_map/pallas_call | solution.py:316
  35.6 15.1 %conditional.4 = (bf16[2,128,512]{2,1,0:T(8,128)(2,1)}, bf16[2,128,512]{2,1,0:T(8,128)(2,1)}, bf16[256,512]{1,0:T(8,128)(2,1)}, bf16[256,512]{1,0:T(8,128)(2,1)}) conditional(s32[]{:T(128)} %convert_element_type.37, () %tuple.33, (s32[4]{0:T(128)S(1)}, bf16[128,512]{1,0:T(8,128)(2,1)S(1)}, bf16[128,512]{1,0:T(8,128)(2,1)}, ...), branch_computations={%region_2.0_spmd, %region_3.0_spmd} | conditional | flops 269877248 | bytes 11665730 | solution.py:265
  35.7 1.5 %collective-permute-done.3 = bf16[256,512]{1,0:T(8,128)(2,1)S(1)} collective-permute-done((bf16[256,512]{1,0:T(8,128)(2,1)S(1)}, bf16[256,512]{1,0:T(8,128)(2,1)S(1)}, u32[]{:S(2)}, u32[]{:S(2)}) %collective-permute-start.3) | collective-permute-done | bytes 262176 | tf_op jit(solution)/shard_map/cond/branch_1_fun/ppermute | solution.py:261
  37.4 1.7 %collective-permute-start.4 = (bf16[256,512]{1,0:T(8,128)(2,1)S(1)}, bf16[256,512]{1,0:T(8,128)(2,1)}, u32[]{:S(2)}, u32[]{:S(2)}) collective-permute-start(bf16[256,512]{1,0:T(8,128)(2,1)S(1)} %fusion), channel_id=1, source_target_pairs={{0,16},{8,24},{16,0},{24,8},{1,17},{9,25},{17,1},{25,9},{2,18},{10... | collective-permute-start | bytes 786440 | tf_op jit(solution)/shard_map/cond/branch_1_fun/ppermute | solution.py:261
  39.1 3.3 %branch_1_fun.3 = (bf16[2,128,512]{2,1,0:T(8,128)(2,1)}, bf16[2,128,512]{2,1,0:T(8,128)(2,1)S(1)}) custom-call(s32[4]{0:T(128)S(1)} %get-tuple-element.57.idx, bf16[128,512]{1,0:T(8,128)(2,1)S(1)} %get-tuple-element.58.r2, bf16[128,512]{1,0:T(8,128)(2,1)S(1)} %copy-done.15, bf16[512,512]{1,0:T(8,128)(2,1)S(1)} %get-tuple-element.60.table, ...), custom_call_target="tpu_custom_call" | custom-call | flops 268435456 | bytes 1048576 | tf_op jit(solution)/shard_map/cond/branch_1_fun/pallas_call | solution.py:332
  43.4 2.6 %collective-permute-done.4 = bf16[256,512]{1,0:T(8,128)(2,1)} collective-permute-done((bf16[256,512]{1,0:T(8,128)(2,1)S(1)}, bf16[256,512]{1,0:T(8,128)(2,1)}, u32[]{:S(2)}, u32[]{:S(2)}) %collective-permute-start.4) | collective-permute-done | bytes 262176 | tf_op jit(solution)/shard_map/cond/branch_1_fun/ppermute | solution.py:261
  45.9 3.6 %conditional = (bf16[256,512]{1,0:T(8,128)(2,1)}, bf16[256,512]{1,0:T(8,128)(2,1)}) conditional(s32[]{:T(128)} %convert_element_type.31, () %tuple.23, (bf16[256,512]{1,0:T(8,128)(2,1)S(1)}, bf16[256,512]{1,0:T(8,128)(2,1)}) %tuple.24), branch_computations={%region_4.0_spmd, %region_5.0_spmd} | conditional | flops 524288 | bytes 1835064 | solution.py:265
  45.9 1.7 %add_convert_fusion.1 = bf16[256,512]{1,0:T(8,128)(2,1)} fusion(bf16[256,512]{1,0:T(8,128)(2,1)} %get-tuple-element.56, bf16[256,512]{1,0:T(8,128)(2,1)S(1)} %get-tuple-element.55), kind=kLoop, calls=%fused_computation.1 | loop fusion | flops 524288 | bytes 786432 | tf_op jit(solution)/shard_map/cond/branch_1_fun/cond/branch_1_fun/convert_element_type | solution.py:344
  47.6 1.9 %collective-permute-done.1 = bf16[256,512]{1,0:T(8,128)(2,1)} collective-permute-done((bf16[256,512]{1,0:T(8,128)(2,1)}, bf16[256,512]{1,0:T(8,128)(2,1)}, u32[]{:S(2)}, u32[]{:S(2)}) %collective-permute-start.1) | collective-permute-done | bytes 262176 | tf_op jit(solution)/shard_map/cond/branch_1_fun/cond/branch_1_fun/ppermute | solution.py:261
  49.5 1.1 %collective-permute-done.2 = bf16[2,128,512]{2,1,0:T(8,128)(2,1)} collective-permute-done((bf16[2,128,512]{2,1,0:T(8,128)(2,1)S(1)}, bf16[2,128,512]{2,1,0:T(8,128)(2,1)}, u32[]{:S(2)}, u32[]{:S(2)}) %collective-permute-start.2) | collective-permute-done | bytes 262176 | tf_op jit(solution)/shard_map/cond/branch_1_fun/ppermute | solution.py:258
  50.7 2.9 %shard_map.97 = (bf16[1,128,2048]{2,1,0:T(8,128)(2,1)}, bf16[1,128,2048]{2,1,0:T(8,128)(2,1)}, bf16[1,128,2048]{2,1,0:T(8,128)(2,1)}, f32[512,512]{1,0:T(8,128)}) custom-call(s32[4]{0:T(128)S(1)} %pad_add_fusion.idx, bf16[1,128,2048]{2,1,0:T(8,128)(2,1)S(1)} %copy-done.1, bf16[1,128,2048]{2,1,0:T(8,128)(2,1)S(1)} %copy-done.2, ...), custom_call_target="tpu_custom_call" | custom-call | flops 786432 | bytes 4718592 | tf_op jit(solution)/shard_map/pallas_call | solution.py:353
  (58 shorter events, 4.1 us)
Async XLA Ops:
  0.7 9.2 %copy-start = (f32[512,512]{1,0:T(8,128)S(1)}, f32[512,512]{1,0:T(8,128)}, u32[]{:S(2)}) copy-start(f32[512,512]{1,0:T(8,128)} %taps.3) | copy-start | bytes 3145732
  0.7 9.2 %copy-start.4 = (bf16[512,512]{1,0:T(8,128)(2,1)S(1)}, bf16[512,512]{1,0:T(8,128)(2,1)}, u32[]{:S(2)}) copy-start(bf16[512,512]{1,0:T(8,128)(2,1)} %constant.15.clone.table) | copy-start | bytes 1572868
  3.8 28.1 %copy-start.7 = (bf16[2,128,512]{2,1,0:T(8,128)(2,1)}, bf16[2,128,512]{2,1,0:T(8,128)(2,1)S(1)}, u32[]{:S(2)}) copy-start(bf16[2,128,512]{2,1,0:T(8,128)(2,1)S(1)} %get-tuple-element.119.keep) | copy-start | bytes 786436
  3.8 10.7 %collective-permute-start.7 = (bf16[256,256]{1,0:T(8,128)(2,1)}, bf16[256,256]{1,0:T(8,128)(2,1)S(1)}, u32[]{:S(2)}, u32[]{:S(2)}) collective-permute-start(bf16[256,256]{1,0:T(8,128)(2,1)} %get-tuple-element.110), channel_id=1, source_target_pairs={{0,2},{1,3},{2,0},{3,1},{4,6},{5,7},{6,4},{7,5},{8,10},{9,11},{10,... | collective-permute-start | bytes 393224 | tf_op jit(solution)/shard_map/ppermute | solution.py:258
  7.8 13.9 %collective-permute-start.9 = (bf16[2,128,512]{2,1,0:T(8,128)(2,1)}, bf16[2,128,512]{2,1,0:T(8,128)(2,1)S(1)}, u32[]{:S(2)}, u32[]{:S(2)}) collective-permute-start(bf16[2,128,512]{2,1,0:T(8,128)(2,1)} %get-tuple-element.115), channel_id=1, source_target_pairs={{0,1},{1,0},{2,3},{3,2},{4,5},{5,4},{6,7},{7,6},{8,9},{9,8},{10,11... | collective-permute-start | bytes 786440 | tf_op jit(solution)/shard_map/ppermute | solution.py:258
  9.4 5.9 %copy-start.16 = (bf16[128,512]{1,0:T(8,128)(2,1)S(1)}, bf16[128,512]{1,0:T(8,128)(2,1)}, u32[]{:S(2)}) copy-start(bf16[128,512]{1,0:T(8,128)(2,1)} %get-tuple-element.106) | copy-start | bytes 393220
  9.4 16.8 %collective-permute-start.10 = (bf16[2,128,512]{2,1,0:T(8,128)(2,1)}, bf16[2,128,512]{2,1,0:T(8,128)(2,1)S(1)}, u32[]{:S(2)}, u32[]{:S(2)}) collective-permute-start(bf16[2,128,512]{2,1,0:T(8,128)(2,1)} %get-tuple-element.120), channel_id=1, source_target_pairs={{0,1},{1,0},{2,3},{3,2},{4,5},{5,4},{6,7},{7,6},{8,9},{9,8},{10,11... | collective-permute-start | bytes 786440 | tf_op jit(solution)/shard_map/ppermute | solution.py:258
  11.3 15.0 %copy-start.5 = (bf16[512,512]{1,0:T(8,128)(2,1)}, bf16[512,512]{1,0:T(8,128)(2,1)S(1)}, u32[]{:S(2)}) copy-start(bf16[512,512]{1,0:T(8,128)(2,1)S(1)} %get-tuple-element.118.cross) | copy-start | bytes 1572868
  11.3 15.0 %copy-start.11 = (bf16[256,512]{1,0:T(8,128)(2,1)}, bf16[256,512]{1,0:T(8,128)(2,1)S(1)}, u32[]{:S(2)}) copy-start(bf16[256,512]{1,0:T(8,128)(2,1)S(1)} %get-tuple-element.111.inv) | copy-start | bytes 786436
  14.5 3.6 %collective-permute-start.8 = (bf16[256,256]{1,0:T(8,128)(2,1)S(1)}, bf16[256,256]{1,0:T(8,128)(2,1)S(1)}, u32[]{:S(2)}, u32[]{:S(2)}) collective-permute-start(bf16[256,256]{1,0:T(8,128)(2,1)S(1)} %collective-permute-done.7), channel_id=1, source_target_pairs={{0,8},{8,0},{16,24},{24,16},{1,9},{9,1},{17,25},{25,17},{2,10},{10... | collective-permute-start | bytes 393224 | tf_op jit(solution)/shard_map/ppermute | solution.py:261
  14.5 15.8 %collective-permute-start.5 = (bf16[128,512]{1,0:T(8,128)(2,1)S(1)}, bf16[128,512]{1,0:T(8,128)(2,1)S(1)}, u32[]{:S(2)}, u32[]{:S(2)}) collective-permute-start(bf16[128,512]{1,0:T(8,128)(2,1)S(1)} %copy-done.17), channel_id=1, source_target_pairs={{0,2},{1,3},{2,0},{3,1},{4,6},{5,7},{6,4},{7,5},{8,10},{9,11},{10,... | collective-permute-start | bytes 393224 | tf_op jit(solution)/shard_map/ppermute | solution.py:258
  15.3 16.5 %collective-permute-start.6 = (bf16[128,512]{1,0:T(8,128)(2,1)S(1)}, bf16[128,512]{1,0:T(8,128)(2,1)S(1)}, u32[]{:S(2)}, u32[]{:S(2)}) collective-permute-start(bf16[128,512]{1,0:T(8,128)(2,1)S(1)} %copy-done.16), channel_id=1, source_target_pairs={{0,3},{1,2},{2,1},{3,0},{4,7},{5,6},{6,5},{7,4},{8,11},{9,10},{10,... | collective-permute-start | bytes 393224 | tf_op jit(solution)/shard_map/ppermute | solution.py:258
  24.6 1.3 %collective-permute-start = (bf16[256,256]{1,0:T(8,128)(2,1)S(1)}, bf16[256,256]{1,0:T(8,128)(2,1)S(1)}, u32[]{:S(2)}, u32[]{:S(2)}) collective-permute-start(bf16[256,256]{1,0:T(8,128)(2,1)S(1)} %get-tuple-element.54), channel_id=1, source_target_pairs={{0,8},{8,0},{16,24},{24,16},{1,9},{9,1},{17,25},{25,17},{2,10},{10... | collective-permute-start | bytes 393224 | tf_op jit(solution)/shard_map/cond/branch_1_fun/ppermute | solution.py:261
  25.9 9.6 %collective-permute-start.11 = (bf16[256,256]{1,0:T(8,128)(2,1)S(1)}, bf16[256,256]{1,0:T(8,128)(2,1)S(1)}, u32[]{:S(2)}, u32[]{:S(2)}) collective-permute-start(bf16[256,256]{1,0:T(8,128)(2,1)S(1)} %get-tuple-element.123), channel_id=1, source_target_pairs={{0,2},{1,3},{2,0},{3,1},{4,6},{5,7},{6,4},{7,5},{8,10},{9,11},{10,... | collective-permute-start | bytes 393224 | tf_op jit(solution)/shard_map/ppermute | solution.py:258
  26.0 24.6 %collective-permute-start.12 = (bf16[2,128,512]{2,1,0:T(8,128)(2,1)}, bf16[2,128,512]{2,1,0:T(8,128)(2,1)S(1)}, u32[]{:S(2)}, u32[]{:S(2)}) collective-permute-start(bf16[2,128,512]{2,1,0:T(8,128)(2,1)} %get-tuple-element.127), channel_id=1, source_target_pairs={{0,1},{1,0},{2,3},{3,2},{4,5},{5,4},{6,7},{7,6},{8,9},{9,8},{10,11... | collective-permute-start | bytes 786440 | tf_op jit(solution)/shard_map/ppermute | solution.py:258
  27.5 23.2 %collective-permute-start.13 = (bf16[128,512]{1,0:T(8,128)(2,1)S(1)}, bf16[128,512]{1,0:T(8,128)(2,1)S(1)}, u32[]{:S(2)}, u32[]{:S(2)}) collective-permute-start(bf16[128,512]{1,0:T(8,128)(2,1)S(1)} %get-tuple-element.128), channel_id=1, source_target_pairs={{0,2},{1,3},{2,0},{3,1},{4,6},{5,7},{6,4},{7,5},{8,10},{9,11},{10,... | collective-permute-start | bytes 393224 | tf_op jit(solution)/shard_map/ppermute | solution.py:258
  30.3 20.4 %collective-permute-start.14 = (bf16[128,512]{1,0:T(8,128)(2,1)S(1)}, bf16[128,512]{1,0:T(8,128)(2,1)S(1)}, u32[]{:S(2)}, u32[]{:S(2)}) collective-permute-start(bf16[128,512]{1,0:T(8,128)(2,1)S(1)} %get-tuple-element.129), channel_id=1, source_target_pairs={{0,3},{1,2},{2,1},{3,0},{4,7},{5,6},{6,5},{7,4},{8,11},{9,10},{10,... | collective-permute-start | bytes 393224 | tf_op jit(solution)/shard_map/ppermute | solution.py:258
  35.5 15.1 %copy-start.1 = (bf16[1,128,2048]{2,1,0:T(8,128)(2,1)S(1)}, bf16[1,128,2048]{2,1,0:T(8,128)(2,1)}, u32[]{:S(2)}) copy-start(bf16[1,128,2048]{2,1,0:T(8,128)(2,1)} %q.3) | copy-start | bytes 1572868
  35.6 15.1 %copy-start.2 = (bf16[1,128,2048]{2,1,0:T(8,128)(2,1)S(1)}, bf16[1,128,2048]{2,1,0:T(8,128)(2,1)}, u32[]{:S(2)}) copy-start(bf16[1,128,2048]{2,1,0:T(8,128)(2,1)} %k.3) | copy-start | bytes 1572868
  35.6 15.1 %copy-start.3 = (bf16[1,128,2048]{2,1,0:T(8,128)(2,1)S(1)}, bf16[1,128,2048]{2,1,0:T(8,128)(2,1)}, u32[]{:S(2)}) copy-start(bf16[1,128,2048]{2,1,0:T(8,128)(2,1)} %g.3) | copy-start | bytes 1572868
  35.6 1.6 %collective-permute-start.3 = (bf16[256,512]{1,0:T(8,128)(2,1)S(1)}, bf16[256,512]{1,0:T(8,128)(2,1)S(1)}, u32[]{:S(2)}, u32[]{:S(2)}) collective-permute-start(bf16[256,512]{1,0:T(8,128)(2,1)S(1)} %get-tuple-element.70), channel_id=1, source_target_pairs={{0,8},{8,0},{16,24},{24,16},{1,9},{9,1},{17,25},{25,17},{2,10},{10... | collective-permute-start | bytes 786440 | tf_op jit(solution)/shard_map/cond/branch_1_fun/ppermute | solution.py:261
  37.4 8.5 %collective-permute-start.4 = (bf16[256,512]{1,0:T(8,128)(2,1)S(1)}, bf16[256,512]{1,0:T(8,128)(2,1)}, u32[]{:S(2)}, u32[]{:S(2)}) collective-permute-start(bf16[256,512]{1,0:T(8,128)(2,1)S(1)} %fusion), channel_id=1, source_target_pairs={{0,16},{8,24},{16,0},{24,8},{1,17},{9,25},{17,1},{25,9},{2,18},{10... | collective-permute-start | bytes 786440 | tf_op jit(solution)/shard_map/cond/branch_1_fun/ppermute | solution.py:261
  42.4 8.2 %collective-permute-start.2 = (bf16[2,128,512]{2,1,0:T(8,128)(2,1)S(1)}, bf16[2,128,512]{2,1,0:T(8,128)(2,1)}, u32[]{:S(2)}, u32[]{:S(2)}) collective-permute-start(bf16[2,128,512]{2,1,0:T(8,128)(2,1)S(1)} %get-tuple-element.67), channel_id=1, source_target_pairs={{0,1},{1,0},{2,3},{3,2},{4,5},{5,4},{6,7},{7,6},{8,9},{9,8},{10,11... | collective-permute-start | bytes 786440 | tf_op jit(solution)/shard_map/cond/branch_1_fun/ppermute | solution.py:258
  47.6 1.9 %collective-permute-start.1 = (bf16[256,512]{1,0:T(8,128)(2,1)}, bf16[256,512]{1,0:T(8,128)(2,1)}, u32[]{:S(2)}, u32[]{:S(2)}) collective-permute-start(bf16[256,512]{1,0:T(8,128)(2,1)} %add_convert_fusion.1), channel_id=1, source_target_pairs={{0,8},{8,0},{16,24},{24,16},{1,9},{9,1},{17,25},{25,17},{2,10},{10... | collective-permute-start | bytes 786440 | tf_op jit(solution)/shard_map/cond/branch_1_fun/cond/branch_1_fun/ppermute | solution.py:261
  (9 other events, 34.2 us)
